TPU v7x, 32 devices: a whole 2x2x4 slice. The times are simulated.
32 devices in a mesh: groups: 2 (over x), inst: 8 (over z, y), tp: 2 (over core).
Axes of the slice: x: 2, y: 2, z: 4, core: 2. Of those that a mesh axis runs over, the one named last changes fastest.
Arguments:
- queries: bfloat16 [4, 512, 3072], P(None, ('groups', 'inst'), 'tp'), parts along dimension 1, may hold values from -130 to 130
- new_kv: bfloat16 [4, 512, 256], P(None, ('groups', 'inst')), parts along dimension 1, may hold values from -4.5 to 4.5
- cache_pool: bfloat16 [98304, 256], P(('groups', 'inst')), parts along dimension 0, may hold values from -6 to 6
- lengths: int32 [16, 32], P('groups'), parts along dimension 0, may hold values from 1 to 2, as said below
- anchor: int32 [16, 32], P('groups'), parts along dimension 0, may hold values from 0 to 7, as said below
- out_weight: bfloat16 [3072, 3072], P('tp'), may hold values from -0.875 to 0.875
Outputs:
- attended: bfloat16 [4, 512, 3072], P(None, ('groups', 'inst'), 'tp'), parts along dimension 1
There are 2 independent parts, one for each index of `groups`. A program takes and returns all parts, laid end to end along the dimension named above; an argument that names none is the same for every part. Nothing has to cross between parts.
Inputs may be any that keep to these rules, and one draw needn't show every extreme that they name: `lengths`: in every instance exactly 16 requests hold 2 blocks and the others one; the requests' blocks lie in the instance's pool in slot order, each right after the one before, filling its 48 blocks. anchor[d, j] is the instance whose request in slot j moves to slot j of instance d, or d where the slot stays. Exactly 7 slots move; for each of them the source is the destination rotated by one amount, nonzero and different for each moving slot, and one of these amounts is half the number of instances, rounded down; so every instance sends and receives exactly 7 requests, at most one to or from any other instance.
All inputs are finite; a program needn't handle non-finite values.
Results may differ from a plain program's by a relative error of at most 0.009.
Values may be sent and summed in bfloat16 or wider, within the bound.
No kernel may reach another device: no remote copies, remote signals or barrier semaphores. Data moves between devices by JAX's collectives and lax.ppermute only.
A program may use at most 128 MiB of HBM per device.

v0:
```python
import math

import jax
import jax.numpy as jnp
from jax import lax
from jax.sharding import PartitionSpec as P

HDIM = 128
BLK = 128
MAXB = 2


def body(queries, new_kv, cache_pool, lengths, anchor, out_weight):
    step_count, slot_count, query_width = queries.shape
    heads_local = query_width // HDIM
    window_rows = MAXB * BLK
    pool_rows = cache_pool.shape[0]
    inst_count = lax.axis_size("inst")
    own_index = lax.axis_index("inst")
    slot_ids = jnp.arange(slot_count, dtype=jnp.int32)
    inst_ids = jnp.arange(inst_count, dtype=jnp.int32)
    within = jnp.arange(window_rows, dtype=jnp.int32)
    offsets = jnp.cumsum(lengths, axis=1) - lengths
    own_offsets = offsets[own_index]
    own_lengths = lengths[own_index]
    sending = (anchor == own_index) & (inst_ids[:, None] != own_index)
    slot_for = jnp.sum(jnp.where(sending, slot_ids[None, :], 0), axis=1)
    send_count = jnp.sum(jnp.where(sending, own_lengths[None, :], 0), axis=1) * BLK
    send_start = own_offsets[slot_for] * BLK
    send_index = jnp.minimum(send_start[:, None] + within[None, :], pool_rows - 1)
    send_valid = within[None, :] < send_count[:, None]
    outgoing = jnp.where(
        send_valid[:, :, None], cache_pool[send_index], jnp.zeros((), cache_pool.dtype)
    )
    received = lax.all_to_all(outgoing, "inst", split_axis=0, concat_axis=0, tiled=True)
    source = anchor[own_index]
    row_count = lengths[source, slot_ids] * BLK
    own_index_rows = jnp.minimum((own_offsets * BLK)[:, None] + within[None, :], pool_rows - 1)
    staying = cache_pool[own_index_rows]
    moved_rows = received[source]
    cached = jnp.where((source != own_index)[:, None, None], moved_rows, staying)
    valid_rows = within[None, :] < row_count[:, None]
    score_scale = 1.0 / math.sqrt(HDIM)
    step_ids = jnp.arange(step_count, dtype=jnp.int32)
    causal = step_ids[:, None] >= step_ids[None, :]
    query_heads = queries.reshape(step_count, slot_count, heads_local, HDIM)
    cache_keys = cached[:, :, :HDIM]
    cache_values = cached[:, :, HDIM:]
    fresh_keys = new_kv[:, :, :HDIM]
    fresh_values = new_kv[:, :, HDIM:]
    cache_scores = (
        jnp.einsum("srhe,rte->srht", query_heads, cache_keys, preferred_element_type=jnp.float32)
        * score_scale
    )
    cache_scores = jnp.where(valid_rows[None, :, None, :], cache_scores, -jnp.inf)
    fresh_scores = (
        jnp.einsum("srhe,ure->srhu", query_heads, fresh_keys, preferred_element_type=jnp.float32)
        * score_scale
    )
    fresh_scores = jnp.where(causal[:, None, None, :], fresh_scores, -jnp.inf)
    row_max = jnp.maximum(jnp.max(cache_scores, axis=-1), jnp.max(fresh_scores, axis=-1))
    exp_cache = jnp.exp(cache_scores - row_max[..., None])
    exp_fresh = jnp.exp(fresh_scores - row_max[..., None])
    denominator = jnp.sum(exp_cache, axis=-1) + jnp.sum(exp_fresh, axis=-1)
    weight_cache = (exp_cache / denominator[..., None]).astype(jnp.bfloat16)
    weight_fresh = (exp_fresh / denominator[..., None]).astype(jnp.bfloat16)
    head_out = jnp.einsum(
        "srht,rte->srhe", weight_cache, cache_values, preferred_element_type=jnp.float32
    )
    head_out = head_out + jnp.einsum(
        "srhu,ure->srhe", weight_fresh, fresh_values, preferred_element_type=jnp.float32
    )
    attn = head_out.reshape(step_count, slot_count, query_width).astype(jnp.bfloat16)
    partial_value = jnp.dot(
        attn.reshape(step_count * slot_count, query_width),
        out_weight,
        preferred_element_type=jnp.float32,
    )
    partial_value = partial_value.reshape(step_count, slot_count, out_weight.shape[1])
    result = lax.psum_scatter(
        partial_value.astype(jnp.bfloat16), "tp", scatter_dimension=2, tiled=True
    )
    return result


def solution(mesh):
    placed = (
        P(None, ("groups", "inst"), "tp"),
        P(None, ("groups", "inst"), None),
        P(("groups", "inst"), None),
        P("groups", None),
        P("groups", None),
        P("tp", None),
    )
    return jax.shard_map(
        body,
        mesh=mesh,
        in_specs=placed,
        out_specs=P(None, ("groups", "inst"), "tp"),
        check_vma=False,
    )
```

profile of v0, /device:TPU:0, one launch (start us, length us, event | category | flops | bytes accessed | tf_op | source)
XLA Modules:
  0.0 108.4 jit_solution(1486540661927390660)
XLA Ops:
  6.5 0.0 copy-start
  6.5 1.0 reduce_window_sum.11
  7.6 0.7 fusion.27
  8.3 0.9 select_reduce_fusion.1
  9.2 0.7 sub.19
  9.9 0.6 gather_fusion
  10.5 0.1 fusion.26
  10.6 0.1 iota_compare_fusion.1
  10.7 0.0 copy-done
  10.7 9.0 %gather_fusion.1 = bf16[2048,256]{1,0:T(8,128)(2,1)} fusion(bf16[6144,256]{1,0:T(8,128)(2,1)S(1)} %copy-done, s32[2048]{0:T(1024)S(1)} %broadcast_clamp_fusion.1), kind=kCustom, calls=%fused_computation.1 | custom fusion | bytes 2105344 | tf_op jit(solution)/shard_map/gather | solution.py:33
  19.7 2.3 %broadcast_select_fusion.1 = bf16[8,256,256]{2,1,0:T(8,128)(2,1)} fusion(bf16[8,256,256]{2,1,0:T(8,128)(2,1)} %bitcast.87, pred[8,256]{1,0:T(8,128)(4,1)S(1)} %iota_compare_fusion.1), kind=kLoop, calls=%fused_computation.31 | loop fusion | flops 524288 | bytes 2099200 | tf_op jit(solution)/shard_map/jit(_where)/select_n | solution.py:32
  22.0 7.3 %all-to-all-start = ((bf16[8,256,256]{2,1,0:T(8,128)(2,1)}), bf16[8,256,256]{2,1,0:T(8,128)(2,1)}, u32[]{:S(2)}, u32[]{:S(2)}) async-start(bf16[8,256,256]{2,1,0:T(8,128)(2,1)} %broadcast_select_fusion.1), calls=%async_computation | async-start | bytes 2097152 | tf_op jit(solution)/shard_map/all_to_all | solution.py:35
  29.3 0.0 reduce-scatter.2.cloned.1.call-start
  29.3 0.1 fusion.25
  29.4 0.6 broadcast_clamp_fusion
  30.1 0.0 copy-start.1
  30.1 0.0 copy-start.3
  30.1 35.7 %gather_fusion.3 = bf16[8192,256]{1,0:T(8,128)(2,1)} fusion(bf16[6144,256]{1,0:T(8,128)(2,1)S(1)} %copy-done, s32[8192]{0:T(1024)} %broadcast_clamp_fusion), kind=kCustom, calls=%fused_computation.3 | custom fusion | bytes 8421376 | tf_op jit(solution)/shard_map/gather | solution.py:39
  65.8 0.7 or_bitcast_fusion
  66.5 0.0 copy-done.1
  66.5 0.7 gather_fusion.4
  67.1 0.0 copy-done.3
  67.2 1.1 reshape.220
  68.2 0.7 compare_bitcast_fusion
  69.0 0.1 iota_compare_fusion
  69.0 0.8 fusion.33
  69.8 2.4 %fusion.34 = (f32[4,32,12]{2,0,1:T(4,128)S(1)}, f32[4,32,12,4]{2,3,0,1:T(4,128)S(1)}) fusion(bf16[4,32,12,128]{3,2,1,0:T(8,128)(2,1)} %reshape.220, bf16[4,32,128]{2,1,0:T(8,128)(2,1)S(1)} %get-tuple-element.12, pred[4,4]{1,0:T(4,128)(4,1)S(1)} %iota_compare_fusion.2), kind=kOutput, calls=%fused_computation.74 | convolution fusion | flops 1589760 | bytes 456720 | tf_op jit(solution)/shard_map/srhe,ure->srhu/dot_general | solution.py:57
  72.2 0.0 all-to-all-done
  72.2 4.0 %gather_fusion.2 = bf16[32,256,256]{2,1,0:T(8,128)(2,1)} fusion(bf16[8,256,256]{2,1,0:T(8,128)(2,1)} %all-to-all-done, s32[1024]{0:T(1024)S(1)} %pad_clamp_fusion), kind=kCustom, calls=%fused_computation.2 | custom fusion | bytes 8388736 | tf_op jit(solution)/shard_map/gather | solution.py:40
  76.2 0.0 copy-start.2
  76.2 4.0 %broadcast_select_fusion = bf16[32,256,256]{2,1,0:T(8,128)(2,1)S(1)} fusion(bf16[32,256,256]{2,1,0:T(8,128)(2,1)} %gather_fusion.2, bf16[32,256,256]{2,1,0:T(8,128)(2,1)} %bitcast.86, pred[32]{0:T(512)(128)(4,1)S(1)} %compare_bitcast_fusion), kind=kLoop, calls=%fused_computation.7 | loop fusion | flops 2097152 | bytes 12582944 | tf_op jit(solution)/shard_map/jit(_where)/select_n | solution.py:41
  80.3 0.0 copy-done.2
  80.3 0.9 bitcast_reduce_fusion
  81.2 0.3 fusion.22
  81.5 1.0 fusion.8
  82.5 0.4 convolution_bitcast_fusion
  82.9 1.7 %fusion.11 = bf16[4,32,12,128]{3,2,0,1:T(8,128)(2,1)} fusion(f32[4,32,12,128]{3,2,0,1:T(8,128)S(1)} %convolution_bitcast_fusion, bf16[32,256,256]{2,1,0:T(8,128)(2,1)S(1)} %broadcast_select_fusion, f32[32,256,4,12]{1,3,2,0:T(8,128)S(1)} %get-tuple-element.14, f32[4,32,12]{2,0,1:T(4,128)S(1)} %add.119, f32[4,32,12]{2,0,1:T(4,128)S(1)} %max.7, ...), kind=kOutput, calls=%fused_computation.22 | convolution fusion | flops 103022592 | bytes 5775360 | tf_op jit(solution)/shard_map/srht,rte->srhe/dot_general | solution.py:67
  84.6 1.2 %reshape.266 = bf16[4,32,1536]{2,0,1:T(4,128)(2,1)S(1)} reshape(bf16[4,32,12,128]{3,2,0,1:T(8,128)(2,1)} %fusion.11) | data formatting | bytes 786432 | tf_op jit(solution)/shard_map/convert_element_type | solution.py:73
  85.8 6.0 %fusion.2 = bf16[4,32,3072]{2,1,0:T(8,128)(2,1)} fusion(bf16[1536,3072]{1,0:T(8,128)(2,1)} %param.11, bf16[4,32,1536]{2,0,1:T(4,128)(2,1)S(1)} %reshape.266), kind=kOutput, calls=%fused_computation.8 | convolution fusion | flops 1208352768 | bytes 10616832 | tf_op jit(solution)/shard_map/dot_general | solution.py:74
  91.8 0.0 reduce-scatter.2.cloned.1.call-update
  91.8 9.8 %reduce-scatter.2.cloned.1.call-done = bf16[4,32,1536]{2,1,0:T(8,128)(2,1)} async-done(((bf16[4,32,3072]{2,1,0:T(8,128)(2,1)}), bf16[4,32,1536]{2,1,0:T(8,128)(2,1)}) %reduce-scatter.2.cloned.1.call-update) | async-done | bytes 393232 | tf_op jit(solution)/shard_map/reduce_scatter | solution.py:80
  (14 shorter events, 0.1 us)
Async XLA Ops:
  6.5 4.2 %copy-start = (bf16[6144,256]{1,0:T(8,128)(2,1)S(1)}, bf16[6144,256]{1,0:T(8,128)(2,1)}, u32[]{:S(2)}) copy-start(bf16[6144,256]{1,0:T(8,128)(2,1)} %param.8) | copy-start | bytes 9437188
  22.0 50.2 %all-to-all-start = ((bf16[8,256,256]{2,1,0:T(8,128)(2,1)}), bf16[8,256,256]{2,1,0:T(8,128)(2,1)}, u32[]{:S(2)}, u32[]{:S(2)}) async-start(bf16[8,256,256]{2,1,0:T(8,128)(2,1)} %broadcast_select_fusion.1), calls=%async_computation | async-start | bytes 2097152 | tf_op jit(solution)/shard_map/all_to_all | solution.py:35
  29.3 72.3 %reduce-scatter.2.cloned.1.call-start = ((), (), s32[]{:S(2)}) async-start(), calls=%async_computation.2 | async-start | bytes 1179648 | tf_op jit(solution)/shard_map/reduce_scatter | solution.py:80
  30.1 36.4 %copy-start.1 = (s32[8,32]{1,0:T(8,128)S(1)}, s32[8,32]{1,0:T(8,128)}, u32[]{:S(2)}) copy-start(s32[8,32]{1,0:T(8,128)} %param.9) | copy-start | bytes 3076
  30.1 37.1 %copy-start.3 = (bf16[4,32,1536]{2,1,0:T(8,128)(2,1)S(1)}, bf16[4,32,1536]{2,1,0:T(8,128)(2,1)}, u32[]{:S(2)}) copy-start(bf16[4,32,1536]{2,1,0:T(8,128)(2,1)} %param.6) | copy-start | bytes 1179652
  76.2 4.0 %copy-start.2 = (bf16[4,32,12,128]{3,2,1,0:T(8,128)(2,1)S(1)}, bf16[4,32,12,128]{3,2,1,0:T(8,128)(2,1)}, u32[]{:S(2)}) copy-start(bf16[4,32,12,128]{3,2,1,0:T(8,128)(2,1)} %reshape.220) | copy-start | bytes 1179652
Sparse Core Ops, SparseCore 0:
  91.9 9.6 reduce-scatter.1
where the time goes:
time: 110 us; the launch traced here: 108 us
  local copies, waits for them, and re-layouts  53.8 us (49%)
  between operations  13.5 us (12%)
  other arithmetic  12.6 us (11%)
  matrix products  11.4 us (10%)
  waiting for transfers between devices  9.79 us (9%)
  starting transfers between devices  7.32 us (7%)
    gather x1, local copies, waits for them, and re-layouts, body(): staying = cache_pool[own_index_rows]  35.7 us
    reduce_scatter x1, waiting for transfers between devices, body(): lax.psum_scatter(partial_value.astype(jnp.bfloat16), 'tp', scatter_dimens...  9.77 us
    gather x1, local copies, waits for them, and re-layouts, body(): cache_pool[send_index]  9 us
    all_to_all x1, starting transfers between devices, body(): lax.all_to_all(outgoing, 'inst', split_axis=0, concat_axis=0, tiled=True)  7.28 us
    dot_general x1, matrix products, body(): jnp.dot(attn.reshape(step_count * slot_count, query_width), out_weight, p...  5.96 us
    gather x1, local copies, waits for them, and re-layouts, body(): moved_rows = received[source]  4.01 us
    select_n x1, other arithmetic, body(): jnp.where((source != own_index)[:, None, None], moved_rows, staying)  4 us
    dot_general x1, matrix products, body(): jnp.einsum('srhe,ure->srhu', query_heads, fresh_keys, preferred_element_t...  2.4 us
  transfers between devices with their start and end apart: 2, of which 1 were waited for; matrix products, arithmetic and copies ran while one was open for 40% of the time, Pallas kernels for 0%

commit v1 on v0

v1 whole, which is shorter than its diff:
```python
import functools
import math

import jax
import jax.numpy as jnp
from jax import lax
from jax.experimental import pallas as pl
from jax.experimental.pallas import tpu as pltpu
from jax.sharding import PartitionSpec as P

HDIM = 128
BLK = 128
MAXB = 2
WIN = MAXB * BLK
PAD = 8
MIB = 1024 * 1024


def plan_kernel(ops, place, anchor, lengths, pool, table, *refs):
    sends, half, offs, sems = refs[:ops], refs[ops], refs[ops + 1], refs[ops + 2]
    insts, slots = anchor.shape
    blocks = pool.shape[0] // BLK
    own, core = place[0], place[1]
    for m in range(insts):
        table[0, m] = slots
        table[1, m] = 1
        offs[m] = 0
    start = jnp.int32(0)
    for j in range(slots):
        source = anchor[own, j]
        dest = (2 * own - source) & (insts - 1)
        table[0, own ^ source] = j
        table[1, own ^ source] = lengths[source, j]
        offs[own ^ dest] = start
        start = start + lengths[own, j]

    def block(at, to, sem):
        row = pl.multiple_of(jnp.minimum(at, blocks - 1) * BLK, BLK)
        copy = pltpu.make_async_copy(pool.at[pl.ds(row, BLK)], to, sem)
        copy.start()
        return copy

    copies = []
    for i in range(ops):
        at = offs[insts - 1 - 2 * i - core]
        for b in range(MAXB):
            copies.append(block(at + b, sends[i].at[pl.ds(b * BLK, BLK)], sems.at[i * MAXB + b]))
    copies.append(block(offs[1] + core, half, sems.at[ops * MAXB]))
    for copy in copies:
        copy.wait()


def attend(query, keys, values, fresh_keys, fresh_values, cached_ok, fresh_ok):
    contract = (((1,), (1,)), ((), ()))
    scale = math.log2(math.e) / math.sqrt(HDIM)
    cached = lax.dot_general(query, keys, contract, preferred_element_type=jnp.float32)
    fresh = lax.dot_general(query, fresh_keys, contract, preferred_element_type=jnp.float32)
    cached = jnp.where(cached_ok, cached, -jnp.inf)
    fresh = jnp.where(fresh_ok, fresh, -jnp.inf)
    top = jnp.maximum(
        jnp.max(cached, axis=1, keepdims=True), jnp.max(fresh, axis=1, keepdims=True)
    )
    cached = jnp.exp2((cached - top) * scale)
    fresh = jnp.exp2((fresh - top) * scale)
    total = jnp.sum(cached, axis=1, keepdims=True) + jnp.sum(fresh, axis=1, keepdims=True)
    mixed = jnp.dot(
        cached.astype(jnp.bfloat16), values, preferred_element_type=jnp.float32
    ) + jnp.dot(fresh.astype(jnp.bfloat16), fresh_values, preferred_element_type=jnp.float32)
    return mixed / total


def masks(rows, heads, slots, fresh_count):
    step = lax.broadcasted_iota(jnp.int32, (rows, fresh_count), 0) // heads
    col = lax.broadcasted_iota(jnp.int32, (rows, fresh_count), 1)
    owner = jnp.where(col // slots <= step, col % slots, -1)
    within = lax.broadcasted_iota(jnp.int32, (rows, WIN), 1)
    return owner, within


def stay_kernel(
    stride, group, place, table, lengths, queries, fresh, pool, attn, moved_q, held, spread, sem
):
    steps, slots, width = queries.shape
    heads = width // HDIM
    rows = steps * heads
    pool_rows = pool.shape[0]
    own = place[0]
    copy = pltpu.make_async_copy(pool, held.at[pl.ds(0, pool_rows)], sem.at[0])
    copy.start()
    held[pl.ds(pool_rows, BLK), :] = jnp.zeros((BLK, held.shape[1]), held.dtype)
    for s in range(steps):
        for h in range(heads):
            spread[pl.ds((s * heads + h) * stride, slots), :] = queries[
                s, :, h * HDIM : (h + 1) * HDIM
            ].astype(jnp.float32)
    for m in range(moved_q.shape[0]):
        moved_q[m] = spread[pl.ds(table[0, m], rows, stride=stride), :].astype(jnp.bfloat16)
    owner, within = masks(rows, heads, slots, fresh.shape[0])
    copy.wait()

    def some(g, start):
        for u in range(group):
            j = g * group + u
            count = lengths[own, j]
            query = spread[pl.ds(j, rows, stride=stride), :].astype(jnp.bfloat16)
            window = pl.ds(pl.multiple_of(start * BLK, BLK), WIN)
            attn[pl.ds(j, rows, stride=stride), :] = attend(
                query,
                held[window, :HDIM],
                held[window, HDIM:],
                fresh[:, :HDIM],
                fresh[:, HDIM:],
                within < count * BLK,
                owner == j,
            )
            start = start + count
        return start

    lax.fori_loop(0, slots // group, some, jnp.int32(0))


def move_kernel(
    stride, ops, chunks, place, table, moved_q, fresh, attn, weight, *refs
):
    mine, peers = refs[: ops + 1], refs[ops + 1 : 2 * ops + 2]
    partial, lhs, held, q_v, fresh_v, attn_v, weight_v, sems, weight_sems = refs[2 * ops + 2 :]
    insts, rows = moved_q.shape[0], moved_q.shape[1]
    slots = stride - PAD
    steps = lhs.shape[0] // slots
    heads = rows // steps
    half = partial.shape[1]
    core = place[1]
    other = 1 - core
    copies = []

    def bring(source, to):
        copy = pltpu.make_async_copy(source, to, sems.at[len(copies)])
        copy.start()
        copies.append(copy)

    for i in range(ops):
        bring(mine[i], held.at[insts - 1 - 2 * i - core])
        bring(peers[i], held.at[insts - 1 - 2 * i - other])
    bring(mine[ops], held.at[1, pl.ds(pl.multiple_of(core * BLK, BLK), BLK)])
    bring(peers[ops], held.at[1, pl.ds(pl.multiple_of(other * BLK, BLK), BLK)])
    bring(moved_q, q_v)
    bring(fresh, fresh_v)
    bring(attn, attn_v)
    tile = half // chunks
    first = other * half
    loads = []
    for n in range(chunks):
        load = pltpu.make_async_copy(
            weight.at[:, pl.ds(pl.multiple_of(first + n * tile, HDIM), tile)],
            weight_v.at[n],
            weight_sems.at[n],
        )
        load.start()
        loads.append(load)
    owner, within = masks(rows, heads, slots, fresh_v.shape[0])
    for copy in copies:
        copy.wait()
    for m in range(1, insts):
        j = table[0, m]
        attn_v[pl.ds(j, rows, stride=stride), :] = attend(
            q_v[m],
            held[m, :, :HDIM],
            held[m, :, HDIM:],
            fresh_v[:, :HDIM],
            fresh_v[:, HDIM:],
            within < table[1, m] * BLK,
            owner == j,
        )
    for s in range(steps):
        for h in range(heads):
            lhs[s * slots : (s + 1) * slots, h * HDIM : (h + 1) * HDIM] = attn_v[
                pl.ds((s * heads + h) * stride, slots), :
            ].astype(jnp.bfloat16)
    for n in range(chunks):
        loads[n].wait()
        partial[:, n * tile : (n + 1) * tile] = jnp.dot(
            lhs[...], weight_v[n], preferred_element_type=jnp.float32
        ).astype(jnp.bfloat16)


def own_kernel(chunks, place, lhs, weight, out, weight_v, weight_sems):
    half = out.shape[1]
    tile = half // chunks
    first = place[1] * half
    loads = []
    for n in range(chunks):
        load = pltpu.make_async_copy(
            weight.at[:, pl.ds(pl.multiple_of(first + n * tile, HDIM), tile)],
            weight_v.at[n],
            weight_sems.at[n],
        )
        load.start()
        loads.append(load)
    for n in range(chunks):
        loads[n].wait()
        out[:, n * tile : (n + 1) * tile] = jnp.dot(
            lhs[...], weight_v[n], preferred_element_type=jnp.float32
        )


def spec(space):
    return pl.BlockSpec(memory_space=space)


def body(queries, new_kv, cache_pool, lengths, anchor, out_weight):
    steps, slots, width = queries.shape
    heads = width // HDIM
    rows = steps * heads
    insts = lax.axis_size("inst")
    cores = lax.axis_size("tp")
    kvw = cache_pool.shape[1]
    depth, columns = out_weight.shape
    half = columns // cores
    ops = (insts - 2) // 2
    stride = slots + PAD
    smem, vmem, hbm = spec(pltpu.SMEM), spec(pltpu.VMEM), spec(pl.ANY)
    place = jnp.stack([lax.axis_index("inst"), lax.axis_index("tp")]).astype(jnp.int32)
    fresh = new_kv.reshape(steps * slots, kvw)
    sends = pl.pallas_call(
        functools.partial(plan_kernel, ops),
        out_shape=[jax.ShapeDtypeStruct((2, insts), jnp.int32)]
        + [jax.ShapeDtypeStruct((WIN, kvw), jnp.bfloat16)] * ops
        + [jax.ShapeDtypeStruct((BLK, kvw), jnp.bfloat16)],
        in_specs=[smem, smem, smem, hbm],
        out_specs=[smem] + [hbm] * (ops + 1),
        scratch_shapes=[pltpu.SMEM((insts,), jnp.int32), pltpu.SemaphoreType.DMA((ops * MAXB + 1,))],
    )(place, anchor, lengths, cache_pool)
    table, sends = sends[0], sends[1:]

    mine = [None] * (ops + 1)
    for i in reversed(range(ops + 1)):
        pairs = []
        for a in range(insts):
            for c in range(cores):
                m = insts - 1 - 2 * i - c if i < ops else 1
                pairs.append((a * cores + c, (a ^ m) * cores + c))
        mine[i] = lax.ppermute(sends[i], ("inst", "tp"), pairs)
    swap = [(c, cores - 1 - c) for c in range(cores)]
    peers = [lax.ppermute(block, "tp", swap) for block in mine]

    attn, moved_q = pl.pallas_call(
        functools.partial(stay_kernel, stride, 4),
        out_shape=[
            jax.ShapeDtypeStruct((rows * stride, HDIM), jnp.float32),
            jax.ShapeDtypeStruct((insts, rows, HDIM), jnp.bfloat16),
        ],
        in_specs=[smem, smem, smem, vmem, vmem, hbm],
        out_specs=[vmem, vmem],
        scratch_shapes=[
            pltpu.VMEM((cache_pool.shape[0] + BLK, kvw), jnp.bfloat16),
            pltpu.VMEM((rows * stride, HDIM), jnp.float32),
            pltpu.SemaphoreType.DMA((1,)),
        ],
        compiler_params=pltpu.CompilerParams(vmem_limit_bytes=24 * MIB),
        cost_estimate=pl.CostEstimate(
            flops=4 * slots * rows * WIN * HDIM, bytes_accessed=16 * MIB, transcendentals=0
        ),
    )(place, table, lengths, queries, fresh, cache_pool)

    chunks = 4
    tile = half // chunks
    partial, lhs = pl.pallas_call(
        functools.partial(move_kernel, stride, ops, chunks),
        out_shape=[
            jax.ShapeDtypeStruct((steps * slots, half), jnp.bfloat16),
            jax.ShapeDtypeStruct((steps * slots, width), jnp.bfloat16),
        ],
        in_specs=[smem, smem] + [hbm] * (4 + 2 * (ops + 1)),
        out_specs=[vmem, vmem],
        scratch_shapes=[
            pltpu.VMEM((insts, WIN, kvw), jnp.bfloat16),
            pltpu.VMEM((insts, rows, HDIM), jnp.bfloat16),
            pltpu.VMEM((steps * slots, kvw), jnp.bfloat16),
            pltpu.VMEM((rows * stride, HDIM), jnp.float32),
            pltpu.VMEM((chunks, depth, tile), jnp.bfloat16),
            pltpu.SemaphoreType.DMA((2 * (ops + 1) + 3,)),
            pltpu.SemaphoreType.DMA((chunks,)),
        ],
        compiler_params=pltpu.CompilerParams(vmem_limit_bytes=32 * MIB),
    )(place, table, moved_q, fresh, attn, out_weight, *mine, *peers)

    arrived = lax.ppermute(partial, "tp", swap)
    own = pl.pallas_call(
        functools.partial(own_kernel, chunks),
        out_shape=jax.ShapeDtypeStruct((steps * slots, half), jnp.float32),
        in_specs=[smem, vmem, hbm],
        out_specs=vmem,
        scratch_shapes=[
            pltpu.VMEM((chunks, depth, tile), jnp.bfloat16),
            pltpu.SemaphoreType.DMA((chunks,)),
        ],
        compiler_params=pltpu.CompilerParams(vmem_limit_bytes=24 * MIB),
        cost_estimate=pl.CostEstimate(
            flops=2 * steps * slots * width * half, bytes_accessed=6 * MIB, transcendentals=0
        ),
    )(place, lhs, out_weight)
    result = (own + arrived.astype(jnp.float32)).astype(jnp.bfloat16)
    return result.reshape(steps, slots, half)


def solution(mesh):
    placed = (
        P(None, ("groups", "inst"), "tp"),
        P(None, ("groups", "inst"), None),
        P(("groups", "inst"), None),
        P("groups", None),
        P("groups", None),
        P("tp", None),
    )
    return jax.shard_map(
        body,
        mesh=mesh,
        in_specs=placed,
        out_specs=P(None, ("groups", "inst"), "tp"),
        check_vma=False,
    )
```

time: 110 us -> 67.7 us (0.62); the launches traced: 108 us -> 67.3 us
  local copies, waits for them, and re-layouts: 53.8 us -> 11.5 us
  Pallas kernels: 0 us -> 35.8 us
  between operations: 13.5 us -> 0.1 us
  matrix products: 11.4 us -> 0 us
  other arithmetic: 12.6 us -> 1.43 us
  starting transfers between devices: 7.32 us -> 9.26 us
    gather x5 -> x0, local copies, waits for them, and re-layouts: 50 us -> none  [the longest x1 35.7 us: body(): staying = cache_pool[own_index_rows]]
    pallas_call x0 -> x4, Pallas kernels: none -> 35.8 us  [the longest x1 16.6 us: body(): pl.pallas_call(functools.partial(plan_kernel, ops), out_shape=[jax.ShapeD...]
    unnamed x10 -> x22, local copies, waits for them, and re-layouts: 0.04 us -> 11.5 us
    dot_general x5 -> x0, matrix products: 11.4 us -> none  [the longest x1 5.96 us: body(): jnp.dot(attn.reshape(step_count * slot_count, query_width), out_weight, p...]
    reduce_scatter x1 -> x0, waiting for transfers between devices: 9.77 us -> none  [body(): lax.psum_scatter(partial_value.astype(jnp.bfloat16), 'tp', scatter_dimens...]
    ppermute x0 -> x9, starting transfers between devices: none -> 9.26 us  [the longest x4 8.17 us: body(): mine[i] = lax.ppermute(sends[i], ('inst', 'tp'), pairs)]
    ppermute x0 -> x9, waiting for transfers between devices: none -> 9.19 us  [the longest x4 9.18 us: body(): mine[i] = lax.ppermute(sends[i], ('inst', 'tp'), pairs)]
    all_to_all x1 -> x0, starting transfers between devices: 7.28 us -> none  [body(): lax.all_to_all(outgoing, 'inst', split_axis=0, concat_axis=0, tiled=True)]
  transfers between devices with their start and end apart: 2 -> 9, of which waited for: 1 -> 2; matrix products, arithmetic and copies ran while one was open for 40% -> 0% of each run, Pallas kernels for 0% -> 19%
where the time goes in v1:
time: 67.7 us; the launch traced here: 67.3 us
  Pallas kernels  35.8 us (53%)
  local copies, waits for them, and re-layouts  11.5 us (17%)
  starting transfers between devices  9.26 us (14%)
  waiting for transfers between devices  9.19 us (14%)
  other arithmetic  1.43 us (2%)
    pallas_call x1, Pallas kernels, body(): pl.pallas_call(functools.partial(plan_kernel, ops), out_shape=[jax.ShapeD...  16.6 us
    unnamed x22, local copies, waits for them, and re-layouts  11.5 us
    pallas_call x1, Pallas kernels, body(): pl.pallas_call(functools.partial(stay_kernel, stride, 4), out_shape=[jax....  9.88 us
    ppermute x4, waiting for transfers between devices, body(): mine[i] = lax.ppermute(sends[i], ('inst', 'tp'), pairs)  9.18 us
    ppermute x4, starting transfers between devices, body(): mine[i] = lax.ppermute(sends[i], ('inst', 'tp'), pairs)  8.17 us
    pallas_call x1, Pallas kernels, body(): pl.pallas_call(functools.partial(move_kernel, stride, ops, chunks), out_s...  6.52 us
    pallas_call x1, Pallas kernels, body(): pl.pallas_call(functools.partial(own_kernel, chunks), out_shape=jax.Shape...  2.76 us
  transfers between devices with their start and end apart: 9, of which 2 were waited for; matrix products, arithmetic and copies ran while one was open for 0% of the time, Pallas kernels for 19%

profile of v1, /device:TPU:0, one launch (start us, length us, event | category | flops | bytes accessed | tf_op | source)
XLA Modules:
  0.0 67.3 jit_solution(8855527830104617164)
XLA Ops:
  0.0 0.6 pad_add_fusion.place
  0.6 16.6 %shard_map.64 = (s32[2,8]{1,0:T(2,128)}, bf16[256,256]{1,0:T(8,128)(2,1)}, bf16[256,256]{1,0:T(8,128)(2,1)}, bf16[256,256]{1,0:T(8,128)(2,1)}, bf16[128,256]{1,0:T(8,128)(2,1)}) custom-call(s32[2]{0:T(128)} %pad_add_fusion.place, s32[8,32]{1,0:T(8,128)} %anchor.1, s32[8,32]{1,0:T(8,128)} %lengths.3, bf16[6144,256]{1,0:T(8,128)(2,1)} %pool.3), custom_call_target="tpu_custom_call" | custom-call | tf_op jit(solution)/shard_map/pallas_call | solution.py:224
  17.3 6.1 %collective-permute-start = (bf16[256,256]{1,0:T(8,128)(2,1)}, bf16[256,256]{1,0:T(8,128)(2,1)S(1)}, u32[]{:S(2)}, u32[]{:S(2)}) collective-permute-start(bf16[256,256]{1,0:T(8,128)(2,1)} %get-tuple-element.17), channel_id=1, source_target_pairs={{0,14},{1,13},{2,12},{3,15},{4,10},{5,9},{6,8},{7,11},{8,6},{9,5},... | collective-permute-start | bytes 393224 | tf_op jit(solution)/shard_map/ppermute | solution.py:242
  23.3 0.0 collective-permute-start.1
  23.3 1.7 %collective-permute-start.2 = (bf16[256,256]{1,0:T(8,128)(2,1)}, bf16[256,256]{1,0:T(8,128)(2,1)S(1)}, u32[]{:S(2)}, u32[]{:S(2)}) collective-permute-start(bf16[256,256]{1,0:T(8,128)(2,1)} %get-tuple-element.19), channel_id=1, source_target_pairs={{0,6},{1,5},{2,4},{3,7},{4,2},{5,1},{6,0},{7,3},{8,14},{9,13},{10,... | collective-permute-start | bytes 393224 | tf_op jit(solution)/shard_map/ppermute | solution.py:242
  25.0 0.4 collective-permute-start.3
  25.4 2.5 %collective-permute-done.refs_0_ = bf16[256,256]{1,0:T(8,128)(2,1)S(1)} collective-permute-done((bf16[256,256]{1,0:T(8,128)(2,1)}, bf16[256,256]{1,0:T(8,128)(2,1)S(1)}, u32[]{:S(2)}, u32[]{:S(2)}) %collective-permute-start) | collective-permute-done | bytes 131104 | tf_op jit(solution)/shard_map/ppermute | solution.py:242
  28.0 0.0 collective-permute-start.4
  28.0 6.6 %collective-permute-done.1.refs_1_ = bf16[256,256]{1,0:T(8,128)(2,1)S(1)} collective-permute-done((bf16[256,256]{1,0:T(8,128)(2,1)}, bf16[256,256]{1,0:T(8,128)(2,1)S(1)}, u32[]{:S(2)}, u32[]{:S(2)}) %collective-permute-start.1) | collective-permute-done | bytes 131104 | tf_op jit(solution)/shard_map/ppermute | solution.py:242
  34.6 0.0 collective-permute-start.5
  34.6 0.0 collective-permute-done.2.refs_2_
  34.6 0.5 collective-permute-start.6
  35.1 0.0 collective-permute-done.3.refs_3_
  35.1 0.1 collective-permute-start.7
  35.2 0.0 copy-start.2
  35.2 1.9 %copy-done.2 = bf16[6144,256]{1,0:T(8,128)(2,1)S(1)} copy-done((bf16[6144,256]{1,0:T(8,128)(2,1)S(1)}, bf16[6144,256]{1,0:T(8,128)(2,1)}, u32[]{:S(2)}) %copy-start.2) | copy-done | bytes 3145752
  37.1 0.0 copy-start.3
  37.1 1.0 %copy-done.3 = bf16[4,32,1536]{2,1,0:T(8,128)(2,1)S(1)} copy-done((bf16[4,32,1536]{2,1,0:T(8,128)(2,1)S(1)}, bf16[4,32,1536]{2,1,0:T(8,128)(2,1)}, u32[]{:S(2)}) %copy-start.3) | copy-done | bytes 393240
  38.1 0.0 copy-start.4
  38.1 0.8 %copy-done.4 = bf16[4,32,256]{2,1,0:T(8,128)(2,1)S(1)} copy-done((bf16[4,32,256]{2,1,0:T(8,128)(2,1)S(1)}, bf16[4,32,256]{2,1,0:T(8,128)(2,1)}, u32[]{:S(2)}) %copy-start.4) | copy-done | bytes 65560
  38.9 0.0 copy-start.6
  38.9 0.7 %copy-done.6 = s32[8,32]{1,0:T(8,128)S(1)} copy-done((s32[8,32]{1,0:T(8,128)S(1)}, s32[8,32]{1,0:T(8,128)}, u32[]{:S(2)}) %copy-start.6) | copy-done | bytes 1048
  39.6 0.0 copy-start.7
  39.6 0.6 copy-done.7
  40.3 0.0 copy-start.9
  40.3 0.6 copy-done.9
  40.9 9.9 %shard_map.65 = (f32[1920,128]{1,0:T(8,128)S(1)}, bf16[8,48,128]{2,1,0:T(8,128)(2,1)S(1)}) custom-call(s32[2]{0:T(128)S(1)} %copy-done.7, s32[2,8]{1,0:T(2,128)S(1)} %copy-done.9, s32[8,32]{1,0:T(8,128)S(1)} %copy-done.6, bf16[4,32,1536]{2,1,0:T(8,128)(2,1)S(1)} %copy-done.3, bf16[128,256]{1,0:T(8,128)(2,1)S(1)} %bitcast.4, bf16[6144,256]{1,0:T(8,128)(2,1)S(1)} %copy-done.2), custom_call_target="tpu_custom_call" | custom-call | flops 201326592 | bytes 16777216 | tf_op jit(solution)/shard_map/pallas_call | solution.py:246
  50.8 0.0 collective-permute-done.7.refs_7_
  50.8 0.0 collective-permute-done.4.refs_4_
  50.8 0.0 collective-permute-done.5.refs_5_
  50.8 0.0 collective-permute-done.6.refs_6_
  50.8 0.0 copy-start
  50.8 3.7 %copy-done = bf16[1536,3072]{1,0:T(8,128)(2,1)S(1)} copy-done((bf16[1536,3072]{1,0:T(8,128)(2,1)S(1)}, bf16[1536,3072]{1,0:T(8,128)(2,1)}, u32[]{:S(2)}) %copy-start) | copy-done | bytes 9437208
  54.5 0.0 copy-start.5
  54.5 0.8 %copy-done.5 = bf16[4,32,256]{2,1,0:T(8,128)(2,1)S(1)} copy-done((bf16[4,32,256]{2,1,0:T(8,128)(2,1)S(1)}, bf16[4,32,256]{2,1,0:T(8,128)(2,1)}, u32[]{:S(2)}) %copy-start.5) | copy-done | bytes 65560
  55.4 0.0 copy-start.8
  55.4 0.6 copy-done.8
  56.0 0.0 copy-start.10
  56.0 0.6 copy-done.10
  56.6 0.0 copy-start.1
  56.6 6.5 %shard_map.66 = (bf16[128,1536]{1,0:T(8,128)(2,1)S(1)}, bf16[128,1536]{1,0:T(8,128)(2,1)S(1)}) custom-call(s32[2]{0:T(128)S(1)} %copy-done.8, s32[2,8]{1,0:T(2,128)S(1)} %copy-done.10, bf16[8,48,128]{2,1,0:T(8,128)(2,1)S(1)} %get-tuple-element.15.moved_q, bf16[128,256]{1,0:T(8,128)(2,1)S(1)} %bitcast.5, f32[1920,128]{1,0:T(8,128)S(1)} %get-tuple-element.16.attn, ...), custom_call_target="tpu_custom_call" | custom-call | tf_op jit(solution)/shard_map/pallas_call | solution.py:267
  63.2 0.5 collective-permute-start.8
  63.7 0.0 copy-done.1
  63.7 2.8 %shard_map.67 = f32[128,1536]{1,0:T(8,128)S(1)} custom-call(s32[2]{0:T(128)S(1)} %copy-done.8, bf16[128,1536]{1,0:T(8,128)(2,1)S(1)} %get-tuple-element.21.lhs, bf16[1536,3072]{1,0:T(8,128)(2,1)S(1)} %copy-done.1), custom_call_target="tpu_custom_call" | custom-call | flops 603979776 | bytes 6291456 | tf_op jit(solution)/shard_map/pallas_call | solution.py:288
  66.4 0.0 collective-permute-done.8
  66.4 0.8 %add_convert_fusion = bf16[128,1536]{1,0:T(8,128)(2,1)} fusion(f32[128,1536]{1,0:T(8,128)S(1)} %shard_map.67, bf16[128,1536]{1,0:T(8,128)(2,1)S(1)} %collective-permute-done.8), kind=kLoop, calls=%fused_computation | loop fusion | flops 589824 | bytes 1572864 | tf_op jit(solution)/shard_map/convert_element_type | solution.py:302
Async XLA Ops:
  17.3 10.7 %collective-permute-start = (bf16[256,256]{1,0:T(8,128)(2,1)}, bf16[256,256]{1,0:T(8,128)(2,1)S(1)}, u32[]{:S(2)}, u32[]{:S(2)}) collective-permute-start(bf16[256,256]{1,0:T(8,128)(2,1)} %get-tuple-element.17), channel_id=1, source_target_pairs={{0,14},{1,13},{2,12},{3,15},{4,10},{5,9},{6,8},{7,11},{8,6},{9,5},... | collective-permute-start | bytes 393224 | tf_op jit(solution)/shard_map/ppermute | solution.py:242
  23.3 11.3 %collective-permute-start.1 = (bf16[256,256]{1,0:T(8,128)(2,1)}, bf16[256,256]{1,0:T(8,128)(2,1)S(1)}, u32[]{:S(2)}, u32[]{:S(2)}) collective-permute-start(bf16[256,256]{1,0:T(8,128)(2,1)} %get-tuple-element.18), channel_id=1, source_target_pairs={{0,10},{1,9},{2,8},{3,11},{4,14},{5,13},{6,12},{7,15},{8,2},{9,1},... | collective-permute-start | bytes 393224 | tf_op jit(solution)/shard_map/ppermute | solution.py:242
  23.3 11.3 %collective-permute-start.2 = (bf16[256,256]{1,0:T(8,128)(2,1)}, bf16[256,256]{1,0:T(8,128)(2,1)S(1)}, u32[]{:S(2)}, u32[]{:S(2)}) collective-permute-start(bf16[256,256]{1,0:T(8,128)(2,1)} %get-tuple-element.19), channel_id=1, source_target_pairs={{0,6},{1,5},{2,4},{3,7},{4,2},{5,1},{6,0},{7,3},{8,14},{9,13},{10,... | collective-permute-start | bytes 393224 | tf_op jit(solution)/shard_map/ppermute | solution.py:242
  25.0 10.1 %collective-permute-start.3 = (bf16[128,256]{1,0:T(8,128)(2,1)}, bf16[128,256]{1,0:T(8,128)(2,1)S(1)}, u32[]{:S(2)}, u32[]{:S(2)}) collective-permute-start(bf16[128,256]{1,0:T(8,128)(2,1)} %get-tuple-element.20), channel_id=1, source_target_pairs={{0,2},{1,3},{2,0},{3,1},{4,6},{5,7},{6,4},{7,5},{8,10},{9,11},{10,... | collective-permute-start | bytes 196616 | tf_op jit(solution)/shard_map/ppermute | solution.py:242
  28.0 22.8 %collective-permute-start.4 = (bf16[256,256]{1,0:T(8,128)(2,1)S(1)}, bf16[256,256]{1,0:T(8,128)(2,1)S(1)}, u32[]{:S(2)}, u32[]{:S(2)}) collective-permute-start(bf16[256,256]{1,0:T(8,128)(2,1)S(1)} %collective-permute-done.refs_0_), channel_id=1, source_target_pairs={{0,1},{1,0},{2,3},{3,2},{4,5},{5,4},{6,7},{7,6},{8,9},{9,8},{10,11... | collective-permute-start | bytes 393224 | tf_op jit(solution)/shard_map/ppermute | solution.py:244
  34.6 16.2 %collective-permute-start.5 = (bf16[256,256]{1,0:T(8,128)(2,1)S(1)}, bf16[256,256]{1,0:T(8,128)(2,1)S(1)}, u32[]{:S(2)}, u32[]{:S(2)}) collective-permute-start(bf16[256,256]{1,0:T(8,128)(2,1)S(1)} %collective-permute-done.1.refs_1_), channel_id=1, source_target_pairs={{0,1},{1,0},{2,3},{3,2},{4,5},{5,4},{6,7},{7,6},{8,9},{9,8},{10,11... | collective-permute-start | bytes 393224 | tf_op jit(solution)/shard_map/ppermute | solution.py:244
  34.6 16.2 %collective-permute-start.6 = (bf16[256,256]{1,0:T(8,128)(2,1)S(1)}, bf16[256,256]{1,0:T(8,128)(2,1)S(1)}, u32[]{:S(2)}, u32[]{:S(2)}) collective-permute-start(bf16[256,256]{1,0:T(8,128)(2,1)S(1)} %collective-permute-done.2.refs_2_), channel_id=1, source_target_pairs={{0,1},{1,0},{2,3},{3,2},{4,5},{5,4},{6,7},{7,6},{8,9},{9,8},{10,11... | collective-permute-start | bytes 393224 | tf_op jit(solution)/shard_map/ppermute | solution.py:244
  35.1 15.6 %collective-permute-start.7 = (bf16[128,256]{1,0:T(8,128)(2,1)S(1)}, bf16[128,256]{1,0:T(8,128)(2,1)S(1)}, u32[]{:S(2)}, u32[]{:S(2)}) collective-permute-start(bf16[128,256]{1,0:T(8,128)(2,1)S(1)} %collective-permute-done.3.refs_3_), channel_id=1, source_target_pairs={{0,1},{1,0},{2,3},{3,2},{4,5},{5,4},{6,7},{7,6},{8,9},{9,8},{10,11... | collective-permute-start | bytes 196616 | tf_op jit(solution)/shard_map/ppermute | solution.py:244
  35.2 1.9 %copy-start.2 = (bf16[6144,256]{1,0:T(8,128)(2,1)S(1)}, bf16[6144,256]{1,0:T(8,128)(2,1)}, u32[]{:S(2)}) copy-start(bf16[6144,256]{1,0:T(8,128)(2,1)} %pool.3) | copy-start | bytes 9437188
  37.1 1.0 %copy-start.3 = (bf16[4,32,1536]{2,1,0:T(8,128)(2,1)S(1)}, bf16[4,32,1536]{2,1,0:T(8,128)(2,1)}, u32[]{:S(2)}) copy-start(bf16[4,32,1536]{2,1,0:T(8,128)(2,1)} %queries.1) | copy-start | bytes 1179652
  38.1 0.8 %copy-start.4 = (bf16[4,32,256]{2,1,0:T(8,128)(2,1)S(1)}, bf16[4,32,256]{2,1,0:T(8,128)(2,1)}, u32[]{:S(2)}) copy-start(bf16[4,32,256]{2,1,0:T(8,128)(2,1)} %param.7) | copy-start | bytes 196612
  38.9 0.7 %copy-start.6 = (s32[8,32]{1,0:T(8,128)S(1)}, s32[8,32]{1,0:T(8,128)}, u32[]{:S(2)}) copy-start(s32[8,32]{1,0:T(8,128)} %lengths.3) | copy-start | bytes 3076
  39.6 0.6 copy-start.7
  40.3 0.6 copy-start.9
  50.8 3.7 %copy-start = (bf16[1536,3072]{1,0:T(8,128)(2,1)S(1)}, bf16[1536,3072]{1,0:T(8,128)(2,1)}, u32[]{:S(2)}) copy-start(bf16[1536,3072]{1,0:T(8,128)(2,1)} %weight.3) | copy-start | bytes 28311556
  54.5 0.8 %copy-start.5 = (bf16[4,32,256]{2,1,0:T(8,128)(2,1)S(1)}, bf16[4,32,256]{2,1,0:T(8,128)(2,1)}, u32[]{:S(2)}) copy-start(bf16[4,32,256]{2,1,0:T(8,128)(2,1)} %param.7) | copy-start | bytes 196612
  55.4 0.6 copy-start.8
  56.0 0.6 copy-start.10
  56.6 7.0 %copy-start.1 = (bf16[1536,3072]{1,0:T(8,128)(2,1)S(1)}, bf16[1536,3072]{1,0:T(8,128)(2,1)}, u32[]{:S(2)}) copy-start(bf16[1536,3072]{1,0:T(8,128)(2,1)} %weight.3) | copy-start | bytes 28311556
  63.2 3.3 %collective-permute-start.8 = (bf16[128,1536]{1,0:T(8,128)(2,1)S(1)}, bf16[128,1536]{1,0:T(8,128)(2,1)S(1)}, u32[]{:S(2)}, u32[]{:S(2)}) collective-permute-start(bf16[128,1536]{1,0:T(8,128)(2,1)S(1)} %get-tuple-element.22), channel_id=1, source_target_pairs={{0,1},{1,0},{2,3},{3,2},{4,5},{5,4},{6,7},{7,6},{8,9},{9,8},{10,11... | collective-permute-start | bytes 1179656 | tf_op jit(solution)/shard_map/ppermute | solution.py:287

commit v2 on v0

v2 whole, which is shorter than its diff:
```python
import functools
import math

import jax
import jax.numpy as jnp
from jax import lax
from jax.experimental import pallas as pl
from jax.experimental.pallas import tpu as pltpu
from jax.sharding import PartitionSpec as P

HDIM = 128
BLK = 128
MAXB = 2
WIN = MAXB * BLK
PAD = 8
MIB = 1024 * 1024


def partner(insts, ops, i, core):
    return jnp.int32(1) if i == ops - 1 else insts - 1 - 2 * i - core


def start_copies(pairs, sems):
    copies = [pltpu.make_async_copy(a, b, sems.at[n]) for n, (a, b) in enumerate(pairs)]
    for copy in copies:
        copy.start()
    return copies


def plan_kernel(ops, anchor_h, lengths_h, pool, table, *refs):
    sends, (anchor, lengths, offs, sems) = refs[:ops], refs[ops:]
    insts, slots = anchor.shape
    blocks = pool.shape[0] // BLK
    own, core = lax.axis_index("inst"), lax.axis_index("tp")
    for copy in start_copies([(anchor_h, anchor), (lengths_h, lengths)], sems):
        copy.wait()
    for m in range(insts):
        table[0, m] = slots
        table[1, m] = 1
        offs[m] = 0
    start = jnp.int32(0)
    for j in range(slots):
        source = anchor[own, j]
        dest = (2 * own - source) & (insts - 1)
        table[0, own ^ source] = j
        table[1, own ^ source] = lengths[source, j]
        offs[own ^ dest] = start
        start = start + lengths[own, j]
    pairs = []
    for i in range(ops):
        at = offs[partner(insts, ops, i, core)]
        for b in range(MAXB):
            row = pl.multiple_of(jnp.minimum(at + b, blocks - 1) * BLK, BLK)
            pairs.append((pool.at[pl.ds(row, BLK)], sends[i].at[pl.ds(b * BLK, BLK)]))
    for copy in start_copies(pairs, sems):
        copy.wait()


def attend(query, keys, values, fresh, fresh_ok, cached_ok=None):
    contract = (((1,), (1,)), ((), ()))
    scale = math.log2(math.e) / math.sqrt(HDIM)
    cached = lax.dot_general(query, keys, contract, preferred_element_type=jnp.float32)
    recent = lax.dot_general(
        query, fresh[:, :HDIM], contract, preferred_element_type=jnp.float32
    )
    if cached_ok is not None:
        cached = jnp.where(cached_ok, cached, -jnp.inf)
    recent = jnp.where(fresh_ok, recent, -jnp.inf)
    top = jnp.maximum(
        jnp.max(cached, axis=1, keepdims=True), jnp.max(recent, axis=1, keepdims=True)
    )
    cached = jnp.exp2((cached - top) * scale)
    recent = jnp.exp2((recent - top) * scale)
    total = jnp.sum(cached, axis=1, keepdims=True) + jnp.sum(recent, axis=1, keepdims=True)
    mixed = jnp.dot(
        cached.astype(jnp.bfloat16), values, preferred_element_type=jnp.float32
    ) + jnp.dot(recent.astype(jnp.bfloat16), fresh[:, HDIM:], preferred_element_type=jnp.float32)
    return mixed / total


def owners(parts, steps, heads, slots):
    shape = (parts * steps * heads, steps * slots)
    step = lax.broadcasted_iota(jnp.int32, shape, 0) // heads % steps
    col = lax.broadcasted_iota(jnp.int32, shape, 1)
    return jnp.where(col // slots <= step, col % slots, -1)


def stay_kernel(
    stride, group, ops, table, queries_h, fresh_h, pool_h, lengths_h, weight_h,
    attn, own_q, sent_q, fresh, peer_w, own_w,
    queries, pool, lengths, order, starts, spread, sems,
):
    steps, slots, width = queries.shape
    insts = lengths.shape[0]
    heads = width // HDIM
    rows = steps * heads
    half = own_w.shape[1]
    own, core = lax.axis_index("inst"), lax.axis_index("tp")
    own_cols = pl.ds(pl.multiple_of(core * half, HDIM), half)
    peer_cols = pl.ds(pl.multiple_of((1 - core) * half, HDIM), half)
    loads = start_copies(
        [
            (lengths_h, lengths),
            (queries_h, queries),
            (fresh_h, fresh),
            (pool_h, pool),
            (weight_h.at[:, peer_cols], peer_w),
            (weight_h.at[:, own_cols], own_w),
        ],
        sems,
    )
    loads[0].wait()
    longer = pool.shape[0] // BLK - slots
    start, found = jnp.int32(0), jnp.int32(0)
    for j in range(slots):
        count = lengths[own, j]
        more = count - 1
        place = jnp.where(more > 0, found, longer + j - found)
        order[place] = j
        starts[place] = start
        start = start + count
        found = found + more
    loads[1].wait()
    for s in range(steps):
        for h in range(heads):
            spread[pl.ds((s * heads + h) * stride, slots), :] = queries[
                s, :, h * HDIM : (h + 1) * HDIM
            ].astype(jnp.float32)

    def rows_of(j):
        return spread[pl.ds(j, rows, stride=stride), :].astype(jnp.bfloat16)

    for i in range(ops):
        own_q[i] = rows_of(table[0, partner(insts, ops, i, core)])
    for i in range(ops - 1):
        sent_q[i] = rows_of(table[0, partner(insts, ops, i, 1 - core)])
    owner = owners(1, steps, heads, slots)
    loads[2].wait()
    loads[3].wait()

    def some(first, size, g, _):
        found = []
        for u in range(group):
            at = first + g * group + u
            j = order[at]
            window = pl.ds(pl.multiple_of(starts[at] * BLK, BLK), size)
            out = attend(
                rows_of(j), pool[window, :HDIM], pool[window, HDIM:], fresh[...], owner == j
            )
            found.append((j, out))
        for j, out in found:
            attn[pl.ds(j, rows, stride=stride), :] = out
        return 0

    lax.fori_loop(0, longer // group, functools.partial(some, 0, WIN), 0)
    lax.fori_loop(0, (slots - longer) // group, functools.partial(some, longer, BLK), 0)
    loads[4].wait()
    loads[5].wait()


def move_kernel(ops, steps, slots, table, own_q, peer_q, fresh, *refs):
    blocks, (found, sent) = refs[:ops], refs[ops:]
    rows = own_q.shape[1]
    heads = rows // steps
    insts = table.shape[1]
    core = lax.axis_index("tp")
    within = lax.broadcasted_iota(jnp.int32, (2 * rows, WIN), 1)
    owner = owners(2, steps, heads, slots)
    for i in range(ops):
        m = partner(insts, ops, i, core)
        both = i < ops - 1
        count = 2 * rows if both else rows
        query = jnp.concatenate([own_q[i], peer_q[i]]) if both else own_q[i]
        out = attend(
            query,
            blocks[i][:, :HDIM],
            blocks[i][:, HDIM:],
            fresh[...],
            owner[:count] == table[0, m],
            within[:count] < table[1, m] * BLK,
        )
        found[i] = out[:rows]
        if both:
            sent[i] = out[rows:].astype(jnp.bfloat16)


def project_kernel(ops, stride, chunks, table, attn, found, arrived, weight, partial, lhs, merged):
    rows = found.shape[1]
    insts = table.shape[1]
    slots = stride - PAD
    steps = lhs.shape[0] // slots
    heads = rows // steps
    core = lax.axis_index("tp")
    merged[...] = attn[...]
    for i in range(ops):
        j = table[0, partner(insts, ops, i, core)]
        merged[pl.ds(j, rows, stride=stride), :] = found[i]
    for i in range(ops - 1):
        j = table[0, partner(insts, ops, i, 1 - core)]
        merged[pl.ds(j, rows, stride=stride), :] = arrived[i].astype(jnp.float32)
    for s in range(steps):
        for h in range(heads):
            lhs[s * slots : (s + 1) * slots, h * HDIM : (h + 1) * HDIM] = merged[
                pl.ds((s * heads + h) * stride, slots), :
            ].astype(jnp.bfloat16)
    tile = partial.shape[1] // chunks
    for n in range(chunks):
        cols = slice(n * tile, (n + 1) * tile)
        partial[:, cols] = jnp.dot(
            lhs[...], weight[:, cols], preferred_element_type=jnp.float32
        ).astype(jnp.bfloat16)


def own_kernel(chunks, lhs, weight, out):
    tile = out.shape[1] // chunks
    for n in range(chunks):
        cols = slice(n * tile, (n + 1) * tile)
        out[:, cols] = jnp.dot(lhs[...], weight[:, cols], preferred_element_type=jnp.float32)


def call(kernel, operands, outs, scratch=(), limit=8, cost=None):
    specs = [pl.BlockSpec(memory_space=space) for space, _ in operands]
    return pl.pallas_call(
        kernel,
        out_shape=[space(shape.shape, shape.dtype) for space, shape in outs],
        in_specs=specs,
        out_specs=[pl.BlockSpec(memory_space=space) for space, _ in outs],
        scratch_shapes=list(scratch),
        compiler_params=pltpu.CompilerParams(vmem_limit_bytes=limit * MIB),
        cost_estimate=cost,
    )(*[pltpu.with_memory_space_constraint(array, space) for space, array in operands])


def body(queries, new_kv, cache_pool, lengths, anchor, out_weight):
    steps, slots, width = queries.shape
    heads = width // HDIM
    rows = steps * heads
    insts = lax.axis_size("inst")
    cores = lax.axis_size("tp")
    kvw = cache_pool.shape[1]
    depth, columns = out_weight.shape
    half = columns // cores
    ops = insts // 2
    stride = slots + PAD
    hbm, vmem, smem = pltpu.HBM, pltpu.VMEM, pltpu.SMEM
    dma = pltpu.SemaphoreType.DMA

    def bf16(*shape):
        return jax.ShapeDtypeStruct(shape, jnp.bfloat16)

    def f32(*shape):
        return jax.ShapeDtypeStruct(shape, jnp.float32)

    table, *sends = call(
        functools.partial(plan_kernel, ops),
        [(hbm, anchor), (hbm, lengths), (hbm, cache_pool)],
        [(smem, jax.ShapeDtypeStruct((2, insts), jnp.int32))] + [(vmem, bf16(WIN, kvw))] * ops,
        [
            smem(anchor.shape, jnp.int32),
            smem(lengths.shape, jnp.int32),
            smem((insts,), jnp.int32),
            dma((ops * MAXB,)),
        ],
    )
    blocks = [None] * ops
    for i in reversed(range(ops)):
        pairs = []
        for a in range(insts):
            for c in range(cores):
                m = 1 if i == ops - 1 else insts - 1 - 2 * i - c
                pairs.append((a * cores + c, (a ^ m) * cores + c))
        blocks[i] = lax.ppermute(sends[i], ("inst", "tp"), pairs)

    attn, own_q, sent_q, fresh, peer_w, own_w = call(
        functools.partial(stay_kernel, stride, 4, ops),
        [
            (smem, table),
            (hbm, queries),
            (hbm, new_kv.reshape(steps * slots, kvw)),
            (hbm, cache_pool),
            (hbm, lengths),
            (hbm, out_weight),
        ],
        [
            (vmem, f32(rows * stride, HDIM)),
            (vmem, bf16(ops, rows, HDIM)),
            (vmem, bf16(ops - 1, rows, HDIM)),
            (vmem, bf16(steps * slots, kvw)),
            (vmem, bf16(depth, half)),
            (vmem, bf16(depth, half)),
        ],
        [
            vmem(queries.shape, jnp.bfloat16),
            vmem(cache_pool.shape, jnp.bfloat16),
            smem(lengths.shape, jnp.int32),
            smem((slots,), jnp.int32),
            smem((slots,), jnp.int32),
            vmem((rows * stride, HDIM), jnp.float32),
            dma((6,)),
        ],
        limit=12,
        cost=pl.CostEstimate(
            flops=4 * slots * rows * WIN * HDIM, bytes_accessed=24 * MIB, transcendentals=0
        ),
    )
    swap = [(c, cores - 1 - c) for c in range(cores)]
    peer_q = lax.ppermute(sent_q, "tp", swap)

    found, sent = call(
        functools.partial(move_kernel, ops, steps, slots),
        [(smem, table), (vmem, own_q), (vmem, peer_q), (vmem, fresh)]
        + [(vmem, block) for block in blocks],
        [(vmem, f32(ops, rows, HDIM)), (vmem, bf16(ops - 1, rows, HDIM))],
    )
    arrived = lax.ppermute(sent, "tp", swap)
    chunks = 4
    partial, lhs = call(
        functools.partial(project_kernel, ops, stride, chunks),
        [(smem, table), (vmem, attn), (vmem, found), (vmem, arrived), (vmem, peer_w)],
        [(vmem, bf16(steps * slots, half)), (vmem, bf16(steps * slots, width))],
        [vmem((rows * stride, HDIM), jnp.float32)],
    )
    others = lax.ppermute(partial, "tp", swap)
    (own,) = call(
        functools.partial(own_kernel, chunks),
        [(vmem, lhs), (vmem, own_w)],
        [(vmem, f32(steps * slots, half))],
        cost=pl.CostEstimate(
            flops=2 * steps * slots * width * half, bytes_accessed=6 * MIB, transcendentals=0
        ),
    )
    result = (own + others.astype(jnp.float32)).astype(jnp.bfloat16)
    return result.reshape(steps, slots, half)


def solution(mesh):
    placed = (
        P(None, ("groups", "inst"), "tp"),
        P(None, ("groups", "inst"), None),
        P(("groups", "inst"), None),
        P("groups", None),
        P("groups", None),
        P("tp", None),
    )
    return jax.shard_map(
        body,
        mesh=mesh,
        in_specs=placed,
        out_specs=P(None, ("groups", "inst"), "tp"),
        check_vma=False,
    )
```

time: 110 us -> 29.2 us (0.27); the launches traced: 108 us -> 28.9 us
  local copies, waits for them, and re-layouts: 53.8 us -> 0 us
  Pallas kernels: 0 us -> 16.5 us
  between operations: 13.5 us -> 0.06 us
  other arithmetic: 12.6 us -> 0.81 us
  matrix products: 11.4 us -> 0 us
  waiting for transfers between devices: 9.79 us -> 2.81 us
  starting transfers between devices: 7.32 us -> 8.7 us
    gather x5 -> x0, local copies, waits for them, and re-layouts: 50 us -> none  [the longest x1 35.7 us: body(): staying = cache_pool[own_index_rows]]
    pallas_call x0 -> x5, Pallas kernels: none -> 16.5 us  [call(): pl.pallas_call(kernel, out_shape=[space(shape.shape, shape.dtype) for spa...]
    dot_general x5 -> x0, matrix products: 11.4 us -> none  [the longest x1 5.96 us: body(): jnp.dot(attn.reshape(step_count * slot_count, query_width), out_weight, p...]
    reduce_scatter x1 -> x0, waiting for transfers between devices: 9.77 us -> none  [body(): lax.psum_scatter(partial_value.astype(jnp.bfloat16), 'tp', scatter_dimens...]
    ppermute x0 -> x7, starting transfers between devices: none -> 8.7 us  [the longest x4 8.17 us: body(): blocks[i] = lax.ppermute(sends[i], ('inst', 'tp'), pairs)]
    all_to_all x1 -> x0, starting transfers between devices: 7.28 us -> none  [body(): lax.all_to_all(outgoing, 'inst', split_axis=0, concat_axis=0, tiled=True)]
    select_n x3 -> x0, other arithmetic: 6.3 us -> none  [the longest x1 4 us: body(): jnp.where((source != own_index)[:, None, None], moved_rows, staying)]
    ppermute x0 -> x7, waiting for transfers between devices: none -> 2.81 us  [the longest x1 1.2 us: body(): peer_q = lax.ppermute(sent_q, 'tp', swap)]
  transfers between devices with their start and end apart: 2 -> 7, of which waited for: 1 -> 3; matrix products, arithmetic and copies ran while one was open for 40% -> 0% of each run, Pallas kernels for 0% -> 42%
where the time goes in v2:
time: 29.2 us; the launch traced here: 28.9 us
  Pallas kernels  16.5 us (57%)
  starting transfers between devices  8.7 us (30%)
  waiting for transfers between devices  2.81 us (10%)
  other arithmetic  0.81 us (3%)
    pallas_call x5, Pallas kernels, call(): pl.pallas_call(kernel, out_shape=[space(shape.shape, shape.dtype) for spa...  16.5 us
    ppermute x4, starting transfers between devices, body(): blocks[i] = lax.ppermute(sends[i], ('inst', 'tp'), pairs)  8.17 us
    ppermute x1, waiting for transfers between devices, body(): peer_q = lax.ppermute(sent_q, 'tp', swap)  1.2 us
    ppermute x1, waiting for transfers between devices, body(): arrived = lax.ppermute(sent, 'tp', swap)  1.05 us
    convert_element_type x1, other arithmetic, body(): result = (own + others.astype(jnp.float32)).astype(jnp.bfloat16)  0.81 us
  transfers between devices with their start and end apart: 7, of which 3 were waited for; matrix products, arithmetic and copies ran while one was open for 0% of the time, Pallas kernels for 42%

profile of v2, /device:TPU:0, one launch (start us, length us, event | category | flops | bytes accessed | tf_op | source)
XLA Modules:
  0.0 28.9 jit_solution(4919893812022507976)
XLA Ops:
  0.0 2.1 %shard_map.64 = (s32[2,8]{1,0:T(2,128)S(4)}, bf16[256,256]{1,0:T(8,128)(2,1)S(1)}, bf16[256,256]{1,0:T(8,128)(2,1)S(1)}, bf16[256,256]{1,0:T(8,128)(2,1)S(1)}, bf16[256,256]{1,0:T(8,128)(2,1)S(1)}) custom-call(s32[8,32]{1,0:T(8,128)} %anchor_h.1, s32[8,32]{1,0:T(8,128)} %lengths_h.3, bf16[6144,256]{1,0:T(8,128)(2,1)} %pool_h.1), custom_call_target="tpu_custom_call" | custom-call | tf_op jit(solution)/shard_map/pallas_call | solution.py:223
  2.2 6.1 %collective-permute-start.1 = (bf16[256,256]{1,0:T(8,128)(2,1)S(1)}, bf16[256,256]{1,0:T(8,128)(2,1)S(1)}, u32[]{:S(2)}, u32[]{:S(2)}) collective-permute-start(bf16[256,256]{1,0:T(8,128)(2,1)S(1)} %get-tuple-element.25), channel_id=1, source_target_pairs={{0,14},{1,13},{2,12},{3,15},{4,10},{5,9},{6,8},{7,11},{8,6},{9,5},... | collective-permute-start | bytes 393224 | tf_op jit(solution)/shard_map/ppermute | solution.py:272
  8.2 0.0 collective-permute-start.2
  8.2 1.7 %collective-permute-start.3 = (bf16[256,256]{1,0:T(8,128)(2,1)S(1)}, bf16[256,256]{1,0:T(8,128)(2,1)S(1)}, u32[]{:S(2)}, u32[]{:S(2)}) collective-permute-start(bf16[256,256]{1,0:T(8,128)(2,1)S(1)} %get-tuple-element.27), channel_id=1, source_target_pairs={{0,6},{1,5},{2,4},{3,7},{4,2},{5,1},{6,0},{7,3},{8,14},{9,13},{10,... | collective-permute-start | bytes 393224 | tf_op jit(solution)/shard_map/ppermute | solution.py:272
  9.9 0.4 %collective-permute-start.4 = (bf16[256,256]{1,0:T(8,128)(2,1)S(1)}, bf16[256,256]{1,0:T(8,128)(2,1)S(1)}, u32[]{:S(2)}, u32[]{:S(2)}) collective-permute-start(bf16[256,256]{1,0:T(8,128)(2,1)S(1)} %get-tuple-element.28), channel_id=1, source_target_pairs={{0,2},{1,3},{2,0},{3,1},{4,6},{5,7},{6,4},{7,5},{8,10},{9,11},{10,... | collective-permute-start | bytes 393224 | tf_op jit(solution)/shard_map/ppermute | solution.py:272
  10.3 11.1 %shard_map.65 = (f32[1920,128]{1,0:T(8,128)S(1)}, bf16[4,48,128]{2,1,0:T(8,128)(2,1)S(1)}, bf16[3,48,128]{2,1,0:T(8,128)(2,1)S(1)}, bf16[128,256]{1,0:T(8,128)(2...) custom-call(s32[2,8]{1,0:T(2,128)S(4)} %get-tuple-element.20.table, ...), custom_call_target="tpu_custom_call" | custom-call | flops 201326592 | bytes 25165824 | tf_op jit(solution)/shard_map/pallas_call | solution.py:223
  21.5 0.1 collective-permute-start
  21.5 1.2 %collective-permute-done.peer_q = bf16[3,48,128]{2,1,0:T(8,128)(2,1)S(1)} collective-permute-done((bf16[3,48,128]{2,1,0:T(8,128)(2,1)S(1)}, bf16[3,48,128]{2,1,0:T(8,128)(2,1)S(1)}, u32[]{:S(2)}, u32[]{:S(2)}) %collective-permute-start) | collective-permute-done | bytes 36896 | tf_op jit(solution)/shard_map/ppermute | solution.py:307
  22.7 0.0 collective-permute-done.1.refs_0_
  22.7 0.0 collective-permute-done.2.refs_1_
  22.7 0.0 collective-permute-done.3.refs_2_
  22.7 0.0 collective-permute-done.4.refs_3_
  22.8 1.1 %shard_map.66 = (f32[4,48,128]{2,1,0:T(8,128)S(1)}, bf16[3,48,128]{2,1,0:T(8,128)(2,1)S(1)}) custom-call(s32[2,8]{1,0:T(2,128)S(4)} %get-tuple-element.20.table, bf16[4,48,128]{2,1,0:T(8,128)(2,1)S(1)} %get-tuple-element.22.own_q, bf16[3,48,128]{2,1,0:T(8,128)(2,1)S(1)} %collective-permute-done.peer_q, bf16[128,256]{1,0:T(8,128)(2,1)S(1)} %get-tuple-element.24.fresh, ...), custom_call_target="tpu_custom_call" | custom-call | tf_op jit(solution)/shard_map/pallas_call | solution.py:223
  23.9 0.2 collective-permute-start.5
  24.1 1.1 %collective-permute-done.5.arrived = bf16[3,48,128]{2,1,0:T(8,128)(2,1)S(1)} collective-permute-done((bf16[3,48,128]{2,1,0:T(8,128)(2,1)S(1)}, bf16[3,48,128]{2,1,0:T(8,128)(2,1)S(1)}, u32[]{:S(2)}, u32[]{:S(2)}) %collective-permute-start.5) | collective-permute-done | bytes 36896 | tf_op jit(solution)/shard_map/ppermute | solution.py:315
  25.2 1.1 %shard_map.67 = (bf16[128,1536]{1,0:T(8,128)(2,1)S(1)}, bf16[128,1536]{1,0:T(8,128)(2,1)S(1)}) custom-call(s32[2,8]{1,0:T(2,128)S(4)} %get-tuple-element.20.table, f32[1920,128]{1,0:T(8,128)S(1)} %get-tuple-element.21.attn, f32[4,48,128]{2,1,0:T(8,128)S(1)} %get-tuple-element.29.found, bf16[3,48,128]{2,1,0:T(8,128)(2,1)S(1)} %collective-permute-done.5.arrived, ...), custom_call_target="tpu_custom_call" | custom-call | tf_op jit(solution)/shard_map/pallas_call | solution.py:223
  26.3 0.2 collective-permute-start.6
  26.5 1.0 %shard_map.68 = f32[128,1536]{1,0:T(8,128)S(1)} custom-call(bf16[128,1536]{1,0:T(8,128)(2,1)S(1)} %get-tuple-element.32.lhs, bf16[1536,1536]{1,0:T(8,128)(2,1)S(1)} %get-tuple-element.33.weight), custom_call_target="tpu_custom_call" | custom-call | flops 603979776 | bytes 6291456 | tf_op jit(solution)/shard_map/pallas_call | solution.py:223
  27.5 0.6 %collective-permute-done.6 = bf16[128,1536]{1,0:T(8,128)(2,1)S(1)} collective-permute-done((bf16[128,1536]{1,0:T(8,128)(2,1)S(1)}, bf16[128,1536]{1,0:T(8,128)(2,1)S(1)}, u32[]{:S(2)}, u32[]{:S(2)}) %collective-permute-start.6) | collective-permute-done | bytes 393248 | tf_op jit(solution)/shard_map/ppermute | solution.py:323
  28.1 0.8 %add_convert_fusion = bf16[128,1536]{1,0:T(8,128)(2,1)} fusion(f32[128,1536]{1,0:T(8,128)S(1)} %shard_map.68, bf16[128,1536]{1,0:T(8,128)(2,1)S(1)} %collective-permute-done.6), kind=kLoop, calls=%fused_computation | loop fusion | flops 589824 | bytes 1572864 | tf_op jit(solution)/shard_map/convert_element_type | solution.py:332
Async XLA Ops:
  2.2 20.6 %collective-permute-start.1 = (bf16[256,256]{1,0:T(8,128)(2,1)S(1)}, bf16[256,256]{1,0:T(8,128)(2,1)S(1)}, u32[]{:S(2)}, u32[]{:S(2)}) collective-permute-start(bf16[256,256]{1,0:T(8,128)(2,1)S(1)} %get-tuple-element.25), channel_id=1, source_target_pairs={{0,14},{1,13},{2,12},{3,15},{4,10},{5,9},{6,8},{7,11},{8,6},{9,5},... | collective-permute-start | bytes 393224 | tf_op jit(solution)/shard_map/ppermute | solution.py:272
  8.2 14.5 %collective-permute-start.2 = (bf16[256,256]{1,0:T(8,128)(2,1)S(1)}, bf16[256,256]{1,0:T(8,128)(2,1)S(1)}, u32[]{:S(2)}, u32[]{:S(2)}) collective-permute-start(bf16[256,256]{1,0:T(8,128)(2,1)S(1)} %get-tuple-element.26), channel_id=1, source_target_pairs={{0,10},{1,9},{2,8},{3,11},{4,14},{5,13},{6,12},{7,15},{8,2},{9,1},... | collective-permute-start | bytes 393224 | tf_op jit(solution)/shard_map/ppermute | solution.py:272
  8.2 14.5 %collective-permute-start.3 = (bf16[256,256]{1,0:T(8,128)(2,1)S(1)}, bf16[256,256]{1,0:T(8,128)(2,1)S(1)}, u32[]{:S(2)}, u32[]{:S(2)}) collective-permute-start(bf16[256,256]{1,0:T(8,128)(2,1)S(1)} %get-tuple-element.27), channel_id=1, source_target_pairs={{0,6},{1,5},{2,4},{3,7},{4,2},{5,1},{6,0},{7,3},{8,14},{9,13},{10,... | collective-permute-start | bytes 393224 | tf_op jit(solution)/shard_map/ppermute | solution.py:272
  9.9 12.8 %collective-permute-start.4 = (bf16[256,256]{1,0:T(8,128)(2,1)S(1)}, bf16[256,256]{1,0:T(8,128)(2,1)S(1)}, u32[]{:S(2)}, u32[]{:S(2)}) collective-permute-start(bf16[256,256]{1,0:T(8,128)(2,1)S(1)} %get-tuple-element.28), channel_id=1, source_target_pairs={{0,2},{1,3},{2,0},{3,1},{4,6},{5,7},{6,4},{7,5},{8,10},{9,11},{10,... | collective-permute-start | bytes 393224 | tf_op jit(solution)/shard_map/ppermute | solution.py:272
  21.5 1.3 %collective-permute-start = (bf16[3,48,128]{2,1,0:T(8,128)(2,1)S(1)}, bf16[3,48,128]{2,1,0:T(8,128)(2,1)S(1)}, u32[]{:S(2)}, u32[]{:S(2)}) collective-permute-start(bf16[3,48,128]{2,1,0:T(8,128)(2,1)S(1)} %get-tuple-element.23), channel_id=1, source_target_pairs={{0,1},{1,0},{2,3},{3,2},{4,5},{5,4},{6,7},{7,6},{8,9},{9,8},{10,11... | collective-permute-start | bytes 110600 | tf_op jit(solution)/shard_map/ppermute | solution.py:307
  23.9 1.3 %collective-permute-start.5 = (bf16[3,48,128]{2,1,0:T(8,128)(2,1)S(1)}, bf16[3,48,128]{2,1,0:T(8,128)(2,1)S(1)}, u32[]{:S(2)}, u32[]{:S(2)}) collective-permute-start(bf16[3,48,128]{2,1,0:T(8,128)(2,1)S(1)} %get-tuple-element.30), channel_id=1, source_target_pairs={{0,1},{1,0},{2,3},{3,2},{4,5},{5,4},{6,7},{7,6},{8,9},{9,8},{10,11... | collective-permute-start | bytes 110600 | tf_op jit(solution)/shard_map/ppermute | solution.py:315
  26.3 1.8 %collective-permute-start.6 = (bf16[128,1536]{1,0:T(8,128)(2,1)S(1)}, bf16[128,1536]{1,0:T(8,128)(2,1)S(1)}, u32[]{:S(2)}, u32[]{:S(2)}) collective-permute-start(bf16[128,1536]{1,0:T(8,128)(2,1)S(1)} %get-tuple-element.34), channel_id=1, source_target_pairs={{0,1},{1,0},{2,3},{3,2},{4,5},{5,4},{6,7},{7,6},{8,9},{9,8},{10,11... | collective-permute-start | bytes 1179656 | tf_op jit(solution)/shard_map/ppermute | solution.py:323

commit v3 on v2

--- a/solution.py
+++ b/solution.py
@@ -56,44 +56,60 @@
         copy.wait()
 
 
-def attend(query, keys, values, fresh, fresh_ok, cached_ok=None):
-    contract = (((1,), (1,)), ((), ()))
+def contract_last(a, b):
+    return lax.dot_general(a, b, (((1,), (1,)), ((), ())), preferred_element_type=jnp.float32)
+
+
+def widest(score):
+    return functools.reduce(
+        jnp.maximum, [score[:, k : k + HDIM] for k in range(0, score.shape[1], HDIM)]
+    )
+
+
+def attend_all(scores, recents, values):
     scale = math.log2(math.e) / math.sqrt(HDIM)
-    cached = lax.dot_general(query, keys, contract, preferred_element_type=jnp.float32)
-    recent = lax.dot_general(
-        query, fresh[:, :HDIM], contract, preferred_element_type=jnp.float32
-    )
-    if cached_ok is not None:
-        cached = jnp.where(cached_ok, cached, -jnp.inf)
-    recent = jnp.where(fresh_ok, recent, -jnp.inf)
-    top = jnp.maximum(
-        jnp.max(cached, axis=1, keepdims=True), jnp.max(recent, axis=1, keepdims=True)
-    )
-    cached = jnp.exp2((cached - top) * scale)
-    recent = jnp.exp2((recent - top) * scale)
-    total = jnp.sum(cached, axis=1, keepdims=True) + jnp.sum(recent, axis=1, keepdims=True)
-    mixed = jnp.dot(
-        cached.astype(jnp.bfloat16), values, preferred_element_type=jnp.float32
-    ) + jnp.dot(recent.astype(jnp.bfloat16), fresh[:, HDIM:], preferred_element_type=jnp.float32)
-    return mixed / total
-
-
-def owners(parts, steps, heads, slots):
-    shape = (parts * steps * heads, steps * slots)
-    step = lax.broadcasted_iota(jnp.int32, shape, 0) // heads % steps
-    col = lax.broadcasted_iota(jnp.int32, shape, 1)
-    return jnp.where(col // slots <= step, col % slots, -1)
-
-
-def stay_kernel(
-    stride, group, ops, table, queries_h, fresh_h, pool_h, lengths_h, weight_h,
-    attn, own_q, sent_q, fresh, peer_w, own_w,
-    queries, pool, lengths, order, starts, spread, sems,
-):
+    weights = []
+    for score, recent in zip(scores, recents):
+        top = jnp.max(jnp.maximum(widest(score), recent), axis=1, keepdims=True)
+        cached = jnp.exp2((score - top) * scale)
+        late = jnp.exp2((recent - top) * scale)
+        folded = sum([cached[:, k : k + HDIM] for k in range(0, cached.shape[1], HDIM)], late)
+        share = 1.0 / jnp.sum(folded, axis=1, keepdims=True)
+        weights.append((cached.astype(jnp.bfloat16), late * share, share))
+    return [
+        (jnp.dot(cached, value, preferred_element_type=jnp.float32) * share, late)
+        for (cached, late, share), value in zip(weights, values)
+    ]
+
+
+def query_kernel(stride, ops, table, queries_h, spread, own_q, sent_q, queries, sems):
     steps, slots, width = queries.shape
-    insts = lengths.shape[0]
+    insts = table.shape[1]
     heads = width // HDIM
     rows = steps * heads
+    core = lax.axis_index("tp")
+    start_copies([(queries_h, queries)], sems)[0].wait()
+    for s in range(steps):
+        for h in range(heads):
+            spread[pl.ds((s * heads + h) * stride, slots), :] = queries[
+                s, :, h * HDIM : (h + 1) * HDIM
+            ].astype(jnp.float32)
+    for i in range(ops):
+        j = table[0, partner(insts, ops, i, core)]
+        own_q[i] = spread[pl.ds(j, rows, stride=stride), :].astype(jnp.bfloat16)
+    for i in range(ops - 1):
+        j = table[0, partner(insts, ops, i, 1 - core)]
+        sent_q[i] = spread[pl.ds(j, rows, stride=stride), :].astype(jnp.bfloat16)
+
+
+def stay_kernel(
+    stride, steps, group, spread, fresh_h, pool_h, lengths_h, weight_h,
+    attn, fresh, peer_w, own_w,
+    pool, lengths, order, starts, recent, late, sems,
+):
+    slots = lengths.shape[1]
+    rows = spread.shape[0] // stride
+    heads = rows // steps
     half = own_w.shape[1]
     own, core = lax.axis_index("inst"), lax.axis_index("tp")
     own_cols = pl.ds(pl.multiple_of(core * half, HDIM), half)
@@ -101,7 +117,6 @@
     loads = start_copies(
         [
             (lengths_h, lengths),
-            (queries_h, queries),
             (fresh_h, fresh),
             (pool_h, pool),
             (weight_h.at[:, peer_cols], peer_w),
@@ -111,77 +126,85 @@
     )
     loads[0].wait()
     longer = pool.shape[0] // BLK - slots
+    group = math.gcd(group, longer, slots - longer)
     start, found = jnp.int32(0), jnp.int32(0)
     for j in range(slots):
         count = lengths[own, j]
-        more = count - 1
-        place = jnp.where(more > 0, found, longer + j - found)
+        place = jnp.where(count > 1, found, longer + j - found)
         order[place] = j
         starts[place] = start
         start = start + count
-        found = found + more
+        found = found + count - 1
     loads[1].wait()
-    for s in range(steps):
-        for h in range(heads):
-            spread[pl.ds((s * heads + h) * stride, slots), :] = queries[
-                s, :, h * HDIM : (h + 1) * HDIM
-            ].astype(jnp.float32)
-
-    def rows_of(j):
-        return spread[pl.ds(j, rows, stride=stride), :].astype(jnp.bfloat16)
-
-    for i in range(ops):
-        own_q[i] = rows_of(table[0, partner(insts, ops, i, core)])
-    for i in range(ops - 1):
-        sent_q[i] = rows_of(table[0, partner(insts, ops, i, 1 - core)])
-    owner = owners(1, steps, heads, slots)
+    slot = lax.broadcasted_iota(jnp.int32, (slots, steps * slots), 0)
+    col = lax.broadcasted_iota(jnp.int32, (slots, steps * slots), 1)
+    for i in range(rows):
+        at = pl.ds(i * stride, slots)
+        score = contract_last(spread[at, :].astype(jnp.bfloat16), fresh[:, :HDIM])
+        mine = (col % slots == slot) & (col // slots <= i // heads)
+        recent[at, :] = jnp.where(mine, score, -jnp.inf)
     loads[2].wait()
-    loads[3].wait()
 
     def some(first, size, g, _):
-        found = []
-        for u in range(group):
-            at = first + g * group + u
-            j = order[at]
-            window = pl.ds(pl.multiple_of(starts[at] * BLK, BLK), size)
-            out = attend(
-                rows_of(j), pool[window, :HDIM], pool[window, HDIM:], fresh[...], owner == j
-            )
-            found.append((j, out))
-        for j, out in found:
-            attn[pl.ds(j, rows, stride=stride), :] = out
+        places = [first + g * group + u for u in range(group)]
+        picked = [pl.ds(order[at], rows, stride=stride) for at in places]
+        windows = [pl.ds(pl.multiple_of(starts[at] * BLK, BLK), size) for at in places]
+        queries = [spread[at, :].astype(jnp.bfloat16) for at in picked]
+        recents = [recent[at, :] for at in picked]
+        scores = [contract_last(q, pool[w, :HDIM]) for q, w in zip(queries, windows)]
+        done = attend_all(scores, recents, [pool[w, HDIM:] for w in windows])
+        for at, (mixed, weight) in zip(picked, done):
+            attn[at, :] = mixed
+            late[at, :] = weight
         return 0
 
     lax.fori_loop(0, longer // group, functools.partial(some, 0, WIN), 0)
     lax.fori_loop(0, (slots - longer) // group, functools.partial(some, longer, BLK), 0)
+    for i in range(rows):
+        at = pl.ds(i * stride, slots)
+        attn[at, :] = attn[at, :] + jnp.dot(
+            late[at, :].astype(jnp.bfloat16), fresh[:, HDIM:], preferred_element_type=jnp.float32
+        )
+    loads[3].wait()
     loads[4].wait()
-    loads[5].wait()
-
-
-def move_kernel(ops, steps, slots, table, own_q, peer_q, fresh, *refs):
+
+
+def move_kernel(ops, steps, slots, group, table, own_q, peer_q, fresh, *refs):
     blocks, (found, sent) = refs[:ops], refs[ops:]
     rows = own_q.shape[1]
     heads = rows // steps
     insts = table.shape[1]
     core = lax.axis_index("tp")
+    shape = (2 * rows, steps * slots)
+    step = lax.broadcasted_iota(jnp.int32, shape, 0) // heads % steps
+    col = lax.broadcasted_iota(jnp.int32, shape, 1)
+    owner = jnp.where(col // slots <= step, col % slots, -1)
     within = lax.broadcasted_iota(jnp.int32, (2 * rows, WIN), 1)
-    owner = owners(2, steps, heads, slots)
-    for i in range(ops):
-        m = partner(insts, ops, i, core)
-        both = i < ops - 1
-        count = 2 * rows if both else rows
-        query = jnp.concatenate([own_q[i], peer_q[i]]) if both else own_q[i]
-        out = attend(
-            query,
-            blocks[i][:, :HDIM],
-            blocks[i][:, HDIM:],
-            fresh[...],
-            owner[:count] == table[0, m],
-            within[:count] < table[1, m] * BLK,
-        )
-        found[i] = out[:rows]
-        if both:
-            sent[i] = out[rows:].astype(jnp.bfloat16)
+    for first in range(0, ops, group):
+        batch = range(first, min(first + group, ops))
+        queries, recents, scores = [], [], []
+        for i in batch:
+            query = own_q[i]
+            if i < ops - 1:
+                query = jnp.concatenate([query, peer_q[i]])
+            queries.append(query)
+        for i, query in zip(batch, queries):
+            m = partner(insts, ops, i, core)
+            score = contract_last(query, blocks[i][:, :HDIM])
+            limit = table[1, m] * BLK
+            scores.append(jnp.where(within[: query.shape[0]] < limit, score, -jnp.inf))
+        for i, query in zip(batch, queries):
+            recent = contract_last(query, fresh[:, :HDIM])
+            j = table[0, partner(insts, ops, i, core)]
+            recents.append(jnp.where(owner[: query.shape[0]] == j, recent, -jnp.inf))
+        done = attend_all(scores, recents, [blocks[i][:, HDIM:] for i in batch])
+        for i, (mixed, weight) in zip(batch, done):
+            out = mixed + jnp.dot(
+                weight.astype(jnp.bfloat16), fresh[:, HDIM:], preferred_element_type=jnp.float32
+            )
+            found[i] = out[:rows]
+            if i < ops - 1:
+                sent[i] = out[rows:].astype(jnp.bfloat16)
 
 
 def project_kernel(ops, stride, chunks, table, attn, found, arrived, weight, partial, lhs, merged):
@@ -271,11 +294,24 @@
                 pairs.append((a * cores + c, (a ^ m) * cores + c))
         blocks[i] = lax.ppermute(sends[i], ("inst", "tp"), pairs)
 
-    attn, own_q, sent_q, fresh, peer_w, own_w = call(
-        functools.partial(stay_kernel, stride, 4, ops),
-        [
-            (smem, table),
-            (hbm, queries),
+    spread, own_q, sent_q = call(
+        functools.partial(query_kernel, stride, ops),
+        [(smem, table), (hbm, queries)],
+        [
+            (vmem, f32(rows * stride, HDIM)),
+            (vmem, bf16(ops, rows, HDIM)),
+            (vmem, bf16(ops - 1, rows, HDIM)),
+        ],
+        [vmem(queries.shape, jnp.bfloat16), dma((1,))],
+        cost=pl.CostEstimate(flops=0, bytes_accessed=MIB, transcendentals=0),
+    )
+    swap = [(c, cores - 1 - c) for c in range(cores)]
+    peer_q = lax.ppermute(sent_q, "tp", swap)
+
+    attn, fresh, peer_w, own_w = call(
+        functools.partial(stay_kernel, stride, steps, 8),
+        [
+            (vmem, spread),
             (hbm, new_kv.reshape(steps * slots, kvw)),
             (hbm, cache_pool),
             (hbm, lengths),
@@ -283,31 +319,27 @@
         ],
         [
             (vmem, f32(rows * stride, HDIM)),
-            (vmem, bf16(ops, rows, HDIM)),
-            (vmem, bf16(ops - 1, rows, HDIM)),
             (vmem, bf16(steps * slots, kvw)),
             (vmem, bf16(depth, half)),
             (vmem, bf16(depth, half)),
         ],
         [
-            vmem(queries.shape, jnp.bfloat16),
             vmem(cache_pool.shape, jnp.bfloat16),
             smem(lengths.shape, jnp.int32),
             smem((slots,), jnp.int32),
             smem((slots,), jnp.int32),
             vmem((rows * stride, HDIM), jnp.float32),
-            dma((6,)),
-        ],
-        limit=12,
+            vmem((rows * stride, HDIM), jnp.float32),
+            dma((5,)),
+        ],
+        limit=16,
         cost=pl.CostEstimate(
             flops=4 * slots * rows * WIN * HDIM, bytes_accessed=24 * MIB, transcendentals=0
         ),
     )
-    swap = [(c, cores - 1 - c) for c in range(cores)]
-    peer_q = lax.ppermute(sent_q, "tp", swap)
 
     found, sent = call(
-        functools.partial(move_kernel, ops, steps, slots),
+        functools.partial(move_kernel, ops, steps, slots, 4),
         [(smem, table), (vmem, own_q), (vmem, peer_q), (vmem, fresh)]
         + [(vmem, block) for block in blocks],
         [(vmem, f32(ops, rows, HDIM)), (vmem, bf16(ops - 1, rows, HDIM))],

time: 29.2 us -> 25.1 us (0.86)
  Pallas kernels: 16.5 us -> 10.6 us
  waiting for transfers between devices: 2.81 us -> 4.83 us
    pallas_call x5 -> x6, Pallas kernels: 16.5 us -> 10.6 us  [call(): pl.pallas_call(kernel, out_shape=[space(shape.shape, shape.dtype) for spa...]
    ppermute x4, waiting for transfers between devices: 0.01 us -> 3.04 us  [body(): blocks[i] = lax.ppermute(sends[i], ('inst', 'tp'), pairs)]
    ppermute x1, waiting for transfers between devices: 1.2 us -> 0.01 us  [body(): peer_q = lax.ppermute(sent_q, 'tp', swap)]
  transfers between devices with their start and end apart: 7 -> 7, of which waited for: 3 -> 3; matrix products, arithmetic and copies ran while one was open for 0% -> 0% of each run, Pallas kernels for 42% -> 27%
where the time goes in v3:
time: 25.1 us; the launch traced here: 24.9 us
  Pallas kernels  10.6 us (42%)
  starting transfers between devices  8.54 us (34%)
  waiting for transfers between devices  4.83 us (19%)
  other arithmetic  0.81 us (3%)
    pallas_call x6, Pallas kernels, call(): pl.pallas_call(kernel, out_shape=[space(shape.shape, shape.dtype) for spa...  10.6 us
    ppermute x4, starting transfers between devices, body(): blocks[i] = lax.ppermute(sends[i], ('inst', 'tp'), pairs)  8.17 us
    ppermute x4, waiting for transfers between devices, body(): blocks[i] = lax.ppermute(sends[i], ('inst', 'tp'), pairs)  3.04 us
    ppermute x1, waiting for transfers between devices, body(): arrived = lax.ppermute(sent, 'tp', swap)  1.2 us
    convert_element_type x1, other arithmetic, body(): result = (own + others.astype(jnp.float32)).astype(jnp.bfloat16)  0.81 us
    ppermute x1, waiting for transfers between devices, body(): others = lax.ppermute(partial, 'tp', swap)  0.58 us
  transfers between devices with their start and end apart: 7, of which 3 were waited for; matrix products, arithmetic and copies ran while one was open for 0% of the time, Pallas kernels for 27%

profile of v3, /device:TPU:0, one launch (start us, length us, event | category | flops | bytes accessed | tf_op | source)
XLA Modules:
  0.0 24.9 jit_solution(6537413647618936394)
XLA Ops:
  0.0 2.1 %shard_map.64 = (s32[2,8]{1,0:T(2,128)S(4)}, bf16[256,256]{1,0:T(8,128)(2,1)S(1)}, bf16[256,256]{1,0:T(8,128)(2,1)S(1)}, bf16[256,256]{1,0:T(8,128)(2,1)S(1)}, bf16[256,256]{1,0:T(8,128)(2,1)S(1)}) custom-call(s32[8,32]{1,0:T(8,128)} %anchor_h.1, s32[8,32]{1,0:T(8,128)} %lengths_h.3, bf16[6144,256]{1,0:T(8,128)(2,1)} %pool_h.1), custom_call_target="tpu_custom_call" | custom-call | tf_op jit(solution)/shard_map/pallas_call | solution.py:246
  2.2 6.1 %collective-permute-start.1 = (bf16[256,256]{1,0:T(8,128)(2,1)S(1)}, bf16[256,256]{1,0:T(8,128)(2,1)S(1)}, u32[]{:S(2)}, u32[]{:S(2)}) collective-permute-start(bf16[256,256]{1,0:T(8,128)(2,1)S(1)} %get-tuple-element.27), channel_id=1, source_target_pairs={{0,14},{1,13},{2,12},{3,15},{4,10},{5,9},{6,8},{7,11},{8,6},{9,5},... | collective-permute-start | bytes 393224 | tf_op jit(solution)/shard_map/ppermute | solution.py:295
  8.2 0.0 collective-permute-start.2
  8.2 1.7 %collective-permute-start.3 = (bf16[256,256]{1,0:T(8,128)(2,1)S(1)}, bf16[256,256]{1,0:T(8,128)(2,1)S(1)}, u32[]{:S(2)}, u32[]{:S(2)}) collective-permute-start(bf16[256,256]{1,0:T(8,128)(2,1)S(1)} %get-tuple-element.29), channel_id=1, source_target_pairs={{0,6},{1,5},{2,4},{3,7},{4,2},{5,1},{6,0},{7,3},{8,14},{9,13},{10,... | collective-permute-start | bytes 393224 | tf_op jit(solution)/shard_map/ppermute | solution.py:295
  9.9 0.4 %collective-permute-start.4 = (bf16[256,256]{1,0:T(8,128)(2,1)S(1)}, bf16[256,256]{1,0:T(8,128)(2,1)S(1)}, u32[]{:S(2)}, u32[]{:S(2)}) collective-permute-start(bf16[256,256]{1,0:T(8,128)(2,1)S(1)} %get-tuple-element.30), channel_id=1, source_target_pairs={{0,2},{1,3},{2,0},{3,1},{4,6},{5,7},{6,4},{7,5},{8,10},{9,11},{10,... | collective-permute-start | bytes 393224 | tf_op jit(solution)/shard_map/ppermute | solution.py:295
  10.3 1.1 %shard_map.65 = (f32[1920,128]{1,0:T(8,128)S(1)}, bf16[4,48,128]{2,1,0:T(8,128)(2,1)S(1)}, bf16[3,48,128]{2,1,0:T(8,128)(2,1)S(1)}) custom-call(s32[2,8]{1,0:T(2,128)S(4)} %get-tuple-element.21.table, bf16[4,32,1536]{2,1,0:T(8,128)(2,1)} %queries_h.1), custom_call_target="tpu_custom_call" | custom-call | bytes 1048576 | tf_op jit(solution)/shard_map/pallas_call | solution.py:246
  11.4 0.1 collective-permute-start
  11.5 4.7 %shard_map.66 = (f32[1920,128]{1,0:T(8,128)S(1)}, bf16[128,256]{1,0:T(8,128)(2,1)S(1)}, bf16[1536,1536]{1,0:T(8,128)(2,1)S(1)}, bf16[1536,1536]{1,0:T(8,128)(2,1)S(1)}) custom-call(f32[1920,128]{1,0:T(8,128)S(1)} %get-tuple-element.22.spread, bf16[128,256]{1,0:T(8,128)(2,1)} %bitcast.2, bf16[6144,256]{1,0:T(8,128)(2,1)} %pool_h.1, s32[8,32]{1,0:T(8,128)} %lengths_h.3, ...), custom_call_target="tpu_custom_call" | custom-call | flops 201326592 | bytes 25165824 | tf_op jit(solution)/shard_map/pallas_call | solution.py:246
  16.2 0.0 collective-permute-done.peer_q
  16.3 0.0 collective-permute-done.1.refs_0_
  16.3 3.0 %collective-permute-done.2.refs_1_ = bf16[256,256]{1,0:T(8,128)(2,1)S(1)} collective-permute-done((bf16[256,256]{1,0:T(8,128)(2,1)S(1)}, bf16[256,256]{1,0:T(8,128)(2,1)S(1)}, u32[]{:S(2)}, u32[]{:S(2)}) %collective-permute-start.2) | collective-permute-done | bytes 131104 | tf_op jit(solution)/shard_map/ppermute | solution.py:295
  19.3 0.0 collective-permute-done.3.refs_2_
  19.3 0.0 collective-permute-done.4.refs_3_
  19.3 0.6 %shard_map.67 = (f32[4,48,128]{2,1,0:T(8,128)S(1)}, bf16[3,48,128]{2,1,0:T(8,128)(2,1)S(1)}) custom-call(s32[2,8]{1,0:T(2,128)S(4)} %get-tuple-element.21.table, bf16[4,48,128]{2,1,0:T(8,128)(2,1)S(1)} %get-tuple-element.24.own_q, bf16[3,48,128]{2,1,0:T(8,128)(2,1)S(1)} %collective-permute-done.peer_q, bf16[128,256]{1,0:T(8,128)(2,1)S(1)} %get-tuple-element.26.fresh, ...), custom_call_target="tpu_custom_call" | custom-call | tf_op jit(solution)/shard_map/pallas_call | solution.py:246
  19.9 0.1 collective-permute-start.5
  20.0 1.2 %collective-permute-done.5.arrived = bf16[3,48,128]{2,1,0:T(8,128)(2,1)S(1)} collective-permute-done((bf16[3,48,128]{2,1,0:T(8,128)(2,1)S(1)}, bf16[3,48,128]{2,1,0:T(8,128)(2,1)S(1)}, u32[]{:S(2)}, u32[]{:S(2)}) %collective-permute-start.5) | collective-permute-done | bytes 36896 | tf_op jit(solution)/shard_map/ppermute | solution.py:347
  21.2 1.1 %shard_map.68 = (bf16[128,1536]{1,0:T(8,128)(2,1)S(1)}, bf16[128,1536]{1,0:T(8,128)(2,1)S(1)}) custom-call(s32[2,8]{1,0:T(2,128)S(4)} %get-tuple-element.21.table, f32[1920,128]{1,0:T(8,128)S(1)} %get-tuple-element.23.attn, f32[4,48,128]{2,1,0:T(8,128)S(1)} %get-tuple-element.31.found, bf16[3,48,128]{2,1,0:T(8,128)(2,1)S(1)} %collective-permute-done.5.arrived, ...), custom_call_target="tpu_custom_call" | custom-call | tf_op jit(solution)/shard_map/pallas_call | solution.py:246
  22.3 0.2 collective-permute-start.6
  22.5 1.0 %shard_map.69 = f32[128,1536]{1,0:T(8,128)S(1)} custom-call(bf16[128,1536]{1,0:T(8,128)(2,1)S(1)} %get-tuple-element.34.lhs, bf16[1536,1536]{1,0:T(8,128)(2,1)S(1)} %get-tuple-element.35.weight), custom_call_target="tpu_custom_call" | custom-call | flops 603979776 | bytes 6291456 | tf_op jit(solution)/shard_map/pallas_call | solution.py:246
  23.5 0.6 %collective-permute-done.6 = bf16[128,1536]{1,0:T(8,128)(2,1)S(1)} collective-permute-done((bf16[128,1536]{1,0:T(8,128)(2,1)S(1)}, bf16[128,1536]{1,0:T(8,128)(2,1)S(1)}, u32[]{:S(2)}, u32[]{:S(2)}) %collective-permute-start.6) | collective-permute-done | bytes 393248 | tf_op jit(solution)/shard_map/ppermute | solution.py:355
  24.1 0.8 %add_convert_fusion = bf16[128,1536]{1,0:T(8,128)(2,1)} fusion(f32[128,1536]{1,0:T(8,128)S(1)} %shard_map.69, bf16[128,1536]{1,0:T(8,128)(2,1)S(1)} %collective-permute-done.6), kind=kLoop, calls=%fused_computation | loop fusion | flops 589824 | bytes 1572864 | tf_op jit(solution)/shard_map/convert_element_type | solution.py:364
Async XLA Ops:
  2.2 14.1 %collective-permute-start.1 = (bf16[256,256]{1,0:T(8,128)(2,1)S(1)}, bf16[256,256]{1,0:T(8,128)(2,1)S(1)}, u32[]{:S(2)}, u32[]{:S(2)}) collective-permute-start(bf16[256,256]{1,0:T(8,128)(2,1)S(1)} %get-tuple-element.27), channel_id=1, source_target_pairs={{0,14},{1,13},{2,12},{3,15},{4,10},{5,9},{6,8},{7,11},{8,6},{9,5},... | collective-permute-start | bytes 393224 | tf_op jit(solution)/shard_map/ppermute | solution.py:295
  8.2 11.1 %collective-permute-start.2 = (bf16[256,256]{1,0:T(8,128)(2,1)S(1)}, bf16[256,256]{1,0:T(8,128)(2,1)S(1)}, u32[]{:S(2)}, u32[]{:S(2)}) collective-permute-start(bf16[256,256]{1,0:T(8,128)(2,1)S(1)} %get-tuple-element.28), channel_id=1, source_target_pairs={{0,10},{1,9},{2,8},{3,11},{4,14},{5,13},{6,12},{7,15},{8,2},{9,1},... | collective-permute-start | bytes 393224 | tf_op jit(solution)/shard_map/ppermute | solution.py:295
  8.2 11.1 %collective-permute-start.3 = (bf16[256,256]{1,0:T(8,128)(2,1)S(1)}, bf16[256,256]{1,0:T(8,128)(2,1)S(1)}, u32[]{:S(2)}, u32[]{:S(2)}) collective-permute-start(bf16[256,256]{1,0:T(8,128)(2,1)S(1)} %get-tuple-element.29), channel_id=1, source_target_pairs={{0,6},{1,5},{2,4},{3,7},{4,2},{5,1},{6,0},{7,3},{8,14},{9,13},{10,... | collective-permute-start | bytes 393224 | tf_op jit(solution)/shard_map/ppermute | solution.py:295
  9.9 9.4 %collective-permute-start.4 = (bf16[256,256]{1,0:T(8,128)(2,1)S(1)}, bf16[256,256]{1,0:T(8,128)(2,1)S(1)}, u32[]{:S(2)}, u32[]{:S(2)}) collective-permute-start(bf16[256,256]{1,0:T(8,128)(2,1)S(1)} %get-tuple-element.30), channel_id=1, source_target_pairs={{0,2},{1,3},{2,0},{3,1},{4,6},{5,7},{6,4},{7,5},{8,10},{9,11},{10,... | collective-permute-start | bytes 393224 | tf_op jit(solution)/shard_map/ppermute | solution.py:295
  11.4 4.8 %collective-permute-start = (bf16[3,48,128]{2,1,0:T(8,128)(2,1)S(1)}, bf16[3,48,128]{2,1,0:T(8,128)(2,1)S(1)}, u32[]{:S(2)}, u32[]{:S(2)}) collective-permute-start(bf16[3,48,128]{2,1,0:T(8,128)(2,1)S(1)} %get-tuple-element.25), channel_id=1, source_target_pairs={{0,1},{1,0},{2,3},{3,2},{4,5},{5,4},{6,7},{7,6},{8,9},{9,8},{10,11... | collective-permute-start | bytes 110600 | tf_op jit(solution)/shard_map/ppermute | solution.py:309
  19.9 1.3 %collective-permute-start.5 = (bf16[3,48,128]{2,1,0:T(8,128)(2,1)S(1)}, bf16[3,48,128]{2,1,0:T(8,128)(2,1)S(1)}, u32[]{:S(2)}, u32[]{:S(2)}) collective-permute-start(bf16[3,48,128]{2,1,0:T(8,128)(2,1)S(1)} %get-tuple-element.32), channel_id=1, source_target_pairs={{0,1},{1,0},{2,3},{3,2},{4,5},{5,4},{6,7},{7,6},{8,9},{9,8},{10,11... | collective-permute-start | bytes 110600 | tf_op jit(solution)/shard_map/ppermute | solution.py:347
  22.3 1.8 %collective-permute-start.6 = (bf16[128,1536]{1,0:T(8,128)(2,1)S(1)}, bf16[128,1536]{1,0:T(8,128)(2,1)S(1)}, u32[]{:S(2)}, u32[]{:S(2)}) collective-permute-start(bf16[128,1536]{1,0:T(8,128)(2,1)S(1)} %get-tuple-element.36), channel_id=1, source_target_pairs={{0,1},{1,0},{2,3},{3,2},{4,5},{5,4},{6,7},{7,6},{8,9},{9,8},{10,11... | collective-permute-start | bytes 1179656 | tf_op jit(solution)/shard_map/ppermute | solution.py:355

commit v4 on v3

--- a/solution.py
+++ b/solution.py
@@ -27,13 +27,22 @@
     return copies
 
 
-def plan_kernel(ops, anchor_h, lengths_h, pool, table, *refs):
-    sends, (anchor, lengths, offs, sems) = refs[:ops], refs[ops:]
+def plan_kernel(
+    ops, stride, anchor_h, lengths_h, queries_h, pool_h,
+    table, pool, spread, own_q, sent_q, *refs,
+):
+    sends, (anchor, lengths, offs, queries, sems) = refs[:ops], refs[ops:]
     insts, slots = anchor.shape
+    steps, _, width = queries.shape
+    heads = width // HDIM
+    rows = steps * heads
     blocks = pool.shape[0] // BLK
     own, core = lax.axis_index("inst"), lax.axis_index("tp")
-    for copy in start_copies([(anchor_h, anchor), (lengths_h, lengths)], sems):
-        copy.wait()
+    loads = start_copies(
+        [(anchor_h, anchor), (lengths_h, lengths), (queries_h, queries), (pool_h, pool)], sems
+    )
+    loads[0].wait()
+    loads[1].wait()
     for m in range(insts):
         table[0, m] = slots
         table[1, m] = 1
@@ -46,14 +55,24 @@
         table[1, own ^ source] = lengths[source, j]
         offs[own ^ dest] = start
         start = start + lengths[own, j]
-    pairs = []
+    loads[2].wait()
+    for s in range(steps):
+        for h in range(heads):
+            spread[pl.ds((s * heads + h) * stride, slots), :] = queries[
+                s, :, h * HDIM : (h + 1) * HDIM
+            ].astype(jnp.float32)
+    for i in range(ops):
+        j = table[0, partner(insts, ops, i, core)]
+        own_q[i] = spread[pl.ds(j, rows, stride=stride), :].astype(jnp.bfloat16)
+    for i in range(ops - 1):
+        j = table[0, partner(insts, ops, i, 1 - core)]
+        sent_q[i] = spread[pl.ds(j, rows, stride=stride), :].astype(jnp.bfloat16)
+    loads[3].wait()
     for i in range(ops):
         at = offs[partner(insts, ops, i, core)]
         for b in range(MAXB):
             row = pl.multiple_of(jnp.minimum(at + b, blocks - 1) * BLK, BLK)
-            pairs.append((pool.at[pl.ds(row, BLK)], sends[i].at[pl.ds(b * BLK, BLK)]))
-    for copy in start_copies(pairs, sems):
-        copy.wait()
+            sends[i][b * BLK : (b + 1) * BLK, :] = pool[pl.ds(row, BLK), :]
 
 
 def contract_last(a, b):
@@ -82,30 +101,10 @@
     ]
 
 
-def query_kernel(stride, ops, table, queries_h, spread, own_q, sent_q, queries, sems):
-    steps, slots, width = queries.shape
-    insts = table.shape[1]
-    heads = width // HDIM
-    rows = steps * heads
-    core = lax.axis_index("tp")
-    start_copies([(queries_h, queries)], sems)[0].wait()
-    for s in range(steps):
-        for h in range(heads):
-            spread[pl.ds((s * heads + h) * stride, slots), :] = queries[
-                s, :, h * HDIM : (h + 1) * HDIM
-            ].astype(jnp.float32)
-    for i in range(ops):
-        j = table[0, partner(insts, ops, i, core)]
-        own_q[i] = spread[pl.ds(j, rows, stride=stride), :].astype(jnp.bfloat16)
-    for i in range(ops - 1):
-        j = table[0, partner(insts, ops, i, 1 - core)]
-        sent_q[i] = spread[pl.ds(j, rows, stride=stride), :].astype(jnp.bfloat16)
-
-
 def stay_kernel(
-    stride, steps, group, spread, fresh_h, pool_h, lengths_h, weight_h,
+    stride, steps, group, spread, pool, fresh_h, lengths_h, weight_h,
     attn, fresh, peer_w, own_w,
-    pool, lengths, order, starts, recent, late, sems,
+    lengths, order, starts, recent, late, sems,
 ):
     slots = lengths.shape[1]
     rows = spread.shape[0] // stride
@@ -118,7 +117,6 @@
         [
             (lengths_h, lengths),
             (fresh_h, fresh),
-            (pool_h, pool),
             (weight_h.at[:, peer_cols], peer_w),
             (weight_h.at[:, own_cols], own_w),
         ],
@@ -143,7 +141,6 @@
         score = contract_last(spread[at, :].astype(jnp.bfloat16), fresh[:, :HDIM])
         mine = (col % slots == slot) & (col // slots <= i // heads)
         recent[at, :] = jnp.where(mine, score, -jnp.inf)
-    loads[2].wait()
 
     def some(first, size, g, _):
         places = [first + g * group + u for u in range(group)]
@@ -165,8 +162,8 @@
         attn[at, :] = attn[at, :] + jnp.dot(
             late[at, :].astype(jnp.bfloat16), fresh[:, HDIM:], preferred_element_type=jnp.float32
         )
+    loads[2].wait()
     loads[3].wait()
-    loads[4].wait()
 
 
 def move_kernel(ops, steps, slots, group, table, own_q, peer_q, fresh, *refs):
@@ -214,7 +211,6 @@
     steps = lhs.shape[0] // slots
     heads = rows // steps
     core = lax.axis_index("tp")
-    merged[...] = attn[...]
     for i in range(ops):
         j = table[0, partner(insts, ops, i, core)]
         merged[pl.ds(j, rows, stride=stride), :] = found[i]
@@ -241,7 +237,19 @@
         out[:, cols] = jnp.dot(lhs[...], weight[:, cols], preferred_element_type=jnp.float32)
 
 
-def call(kernel, operands, outs, scratch=(), limit=8, cost=None):
+def add_kernel(chunks, own, others, out_h, out, sems):
+    part = out.shape[0] // chunks
+    copies = []
+    for n in range(chunks):
+        at = pl.ds(n * part, part)
+        out[at, :] = (own[at, :] + others[at, :].astype(jnp.float32)).astype(jnp.bfloat16)
+        copies.append(pltpu.make_async_copy(out.at[at], out_h.at[at], sems.at[n]))
+        copies[-1].start()
+    for copy in copies:
+        copy.wait()
+
+
+def call(kernel, operands, outs, scratch=(), limit=8, cost=None, aliases=None):
     specs = [pl.BlockSpec(memory_space=space) for space, _ in operands]
     return pl.pallas_call(
         kernel,
@@ -251,6 +259,7 @@
         scratch_shapes=list(scratch),
         compiler_params=pltpu.CompilerParams(vmem_limit_bytes=limit * MIB),
         cost_estimate=cost,
+        input_output_aliases=aliases or {},
     )(*[pltpu.with_memory_space_constraint(array, space) for space, array in operands])
 
 
@@ -274,15 +283,23 @@
     def f32(*shape):
         return jax.ShapeDtypeStruct(shape, jnp.float32)
 
-    table, *sends = call(
-        functools.partial(plan_kernel, ops),
-        [(hbm, anchor), (hbm, lengths), (hbm, cache_pool)],
-        [(smem, jax.ShapeDtypeStruct((2, insts), jnp.int32))] + [(vmem, bf16(WIN, kvw))] * ops,
+    table, pool, spread, own_q, sent_q, *sends = call(
+        functools.partial(plan_kernel, ops, stride),
+        [(hbm, anchor), (hbm, lengths), (hbm, queries), (hbm, cache_pool)],
+        [
+            (smem, jax.ShapeDtypeStruct((2, insts), jnp.int32)),
+            (vmem, bf16(*cache_pool.shape)),
+            (vmem, f32(rows * stride, HDIM)),
+            (vmem, bf16(ops, rows, HDIM)),
+            (vmem, bf16(ops - 1, rows, HDIM)),
+        ]
+        + [(vmem, bf16(WIN, kvw))] * ops,
         [
             smem(anchor.shape, jnp.int32),
             smem(lengths.shape, jnp.int32),
             smem((insts,), jnp.int32),
-            dma((ops * MAXB,)),
+            vmem(queries.shape, jnp.bfloat16),
+            dma((4,)),
         ],
     )
     blocks = [None] * ops
@@ -294,17 +311,6 @@
                 pairs.append((a * cores + c, (a ^ m) * cores + c))
         blocks[i] = lax.ppermute(sends[i], ("inst", "tp"), pairs)
 
-    spread, own_q, sent_q = call(
-        functools.partial(query_kernel, stride, ops),
-        [(smem, table), (hbm, queries)],
-        [
-            (vmem, f32(rows * stride, HDIM)),
-            (vmem, bf16(ops, rows, HDIM)),
-            (vmem, bf16(ops - 1, rows, HDIM)),
-        ],
-        [vmem(queries.shape, jnp.bfloat16), dma((1,))],
-        cost=pl.CostEstimate(flops=0, bytes_accessed=MIB, transcendentals=0),
-    )
     swap = [(c, cores - 1 - c) for c in range(cores)]
     peer_q = lax.ppermute(sent_q, "tp", swap)
 
@@ -312,8 +318,8 @@
         functools.partial(stay_kernel, stride, steps, 8),
         [
             (vmem, spread),
+            (vmem, pool),
             (hbm, new_kv.reshape(steps * slots, kvw)),
-            (hbm, cache_pool),
             (hbm, lengths),
             (hbm, out_weight),
         ],
@@ -324,13 +330,12 @@
             (vmem, bf16(depth, half)),
         ],
         [
-            vmem(cache_pool.shape, jnp.bfloat16),
             smem(lengths.shape, jnp.int32),
             smem((slots,), jnp.int32),
             smem((slots,), jnp.int32),
             vmem((rows * stride, HDIM), jnp.float32),
             vmem((rows * stride, HDIM), jnp.float32),
-            dma((5,)),
+            dma((4,)),
         ],
         limit=16,
         cost=pl.CostEstimate(
@@ -345,12 +350,16 @@
         [(vmem, f32(ops, rows, HDIM)), (vmem, bf16(ops - 1, rows, HDIM))],
     )
     arrived = lax.ppermute(sent, "tp", swap)
-    chunks = 4
-    partial, lhs = call(
+    chunks = half // WIN
+    partial, lhs, _ = call(
         functools.partial(project_kernel, ops, stride, chunks),
         [(smem, table), (vmem, attn), (vmem, found), (vmem, arrived), (vmem, peer_w)],
-        [(vmem, bf16(steps * slots, half)), (vmem, bf16(steps * slots, width))],
-        [vmem((rows * stride, HDIM), jnp.float32)],
+        [
+            (vmem, bf16(steps * slots, half)),
+            (vmem, bf16(steps * slots, width)),
+            (vmem, f32(rows * stride, HDIM)),
+        ],
+        aliases={1: 2},
     )
     others = lax.ppermute(partial, "tp", swap)
     (own,) = call(
@@ -361,7 +370,12 @@
             flops=2 * steps * slots * width * half, bytes_accessed=6 * MIB, transcendentals=0
         ),
     )
-    result = (own + others.astype(jnp.float32)).astype(jnp.bfloat16)
+    (result,) = call(
+        functools.partial(add_kernel, 4),
+        [(vmem, own), (vmem, others)],
+        [(hbm, bf16(steps * slots, half))],
+        [vmem((steps * slots, half), jnp.bfloat16), dma((4,))],
+    )
     return result.reshape(steps, slots, half)
 
 

time: 25.1 us -> 24.8 us (0.988)
  waiting for transfers between devices: 4.83 us -> 6.45 us
  Pallas kernels: 10.6 us -> 9.57 us
  other arithmetic: 0.81 us -> 0 us
    ppermute x4, waiting for transfers between devices: 3.04 us -> 4.47 us  [body(): blocks[i] = lax.ppermute(sends[i], ('inst', 'tp'), pairs)]
    pallas_call x6, Pallas kernels: 10.6 us -> 9.57 us  [call(): pl.pallas_call(kernel, out_shape=[space(shape.shape, shape.dtype) for spa...]
    convert_element_type x1 -> x0, other arithmetic: 0.81 us -> none  [body(): result = (own + others.astype(jnp.float32)).astype(jnp.bfloat16)]
  transfers between devices with their start and end apart: 7 -> 7, of which waited for: 3 -> 3; matrix products, arithmetic and copies ran while one was open for 0% -> 0% of each run, Pallas kernels for 27% -> 21%
where the time goes in v4:
time: 24.8 us; the launch traced here: 24.6 us
  Pallas kernels  9.57 us (39%)
  starting transfers between devices  8.47 us (34%)
  waiting for transfers between devices  6.45 us (26%)
    pallas_call x6, Pallas kernels, call(): pl.pallas_call(kernel, out_shape=[space(shape.shape, shape.dtype) for spa...  9.57 us
    ppermute x4, starting transfers between devices, body(): blocks[i] = lax.ppermute(sends[i], ('inst', 'tp'), pairs)  8.17 us
    ppermute x4, waiting for transfers between devices, body(): blocks[i] = lax.ppermute(sends[i], ('inst', 'tp'), pairs)  4.47 us
    ppermute x1, waiting for transfers between devices, body(): arrived = lax.ppermute(sent, 'tp', swap)  1.2 us
    ppermute x1, waiting for transfers between devices, body(): others = lax.ppermute(partial, 'tp', swap)  0.78 us
  transfers between devices with their start and end apart: 7, of which 3 were waited for; matrix products, arithmetic and copies ran while one was open for 0% of the time, Pallas kernels for 21%

profile of v4, /device:TPU:0, one launch (start us, length us, event | category | flops | bytes accessed | tf_op | source)
XLA Modules:
  0.0 24.6 jit_solution(18400490855295332731)
XLA Ops:
  0.0 2.1 %shard_map.64 = (s32[2,8]{1,0:T(2,128)S(4)}, bf16[6144,256]{1,0:T(8,128)(2,1)S(1)}, f32[1920,128]{1,0:T(8,128)S(1)}, bf16[4,48,128]{2,1,0:T(8,128)(2,1)S(1)}, bf...) custom-call(s32[8,32]{1,0:T(8,128)} %anchor_h.1, ...), custom_call_target="tpu_custom_call" | custom-call | tf_op jit(solution)/shard_map/pallas_call | solution.py:254
  2.1 6.1 %collective-permute-start.1 = (bf16[256,256]{1,0:T(8,128)(2,1)S(1)}, bf16[256,256]{1,0:T(8,128)(2,1)S(1)}, u32[]{:S(2)}, u32[]{:S(2)}) collective-permute-start(bf16[256,256]{1,0:T(8,128)(2,1)S(1)} %get-tuple-element.29), channel_id=1, source_target_pairs={{0,14},{1,13},{2,12},{3,15},{4,10},{5,9},{6,8},{7,11},{8,6},{9,5},... | collective-permute-start | bytes 393224 | tf_op jit(solution)/shard_map/ppermute | solution.py:312
  8.2 0.0 collective-permute-start.2
  8.2 1.7 %collective-permute-start.3 = (bf16[256,256]{1,0:T(8,128)(2,1)S(1)}, bf16[256,256]{1,0:T(8,128)(2,1)S(1)}, u32[]{:S(2)}, u32[]{:S(2)}) collective-permute-start(bf16[256,256]{1,0:T(8,128)(2,1)S(1)} %get-tuple-element.31), channel_id=1, source_target_pairs={{0,6},{1,5},{2,4},{3,7},{4,2},{5,1},{6,0},{7,3},{8,14},{9,13},{10,... | collective-permute-start | bytes 393224 | tf_op jit(solution)/shard_map/ppermute | solution.py:312
  9.9 0.4 %collective-permute-start.4 = (bf16[256,256]{1,0:T(8,128)(2,1)S(1)}, bf16[256,256]{1,0:T(8,128)(2,1)S(1)}, u32[]{:S(2)}, u32[]{:S(2)}) collective-permute-start(bf16[256,256]{1,0:T(8,128)(2,1)S(1)} %get-tuple-element.32), channel_id=1, source_target_pairs={{0,2},{1,3},{2,0},{3,1},{4,6},{5,7},{6,4},{7,5},{8,10},{9,11},{10,... | collective-permute-start | bytes 393224 | tf_op jit(solution)/shard_map/ppermute | solution.py:312
  10.3 0.0 collective-permute-start
  10.3 4.5 %shard_map.65 = (f32[1920,128]{1,0:T(8,128)S(1)}, bf16[128,256]{1,0:T(8,128)(2,1)S(1)}, bf16[1536,1536]{1,0:T(8,128)(2,1)S(1)}, bf16[1536,1536]{1,0:T(8,128)(2,1)S(1)}) custom-call(f32[1920,128]{1,0:T(8,128)S(1)} %get-tuple-element.23.spread, bf16[6144,256]{1,0:T(8,128)(2,1)S(1)} %get-tuple-element.24.pool, bf16[128,256]{1,0:T(8,128)(2,1)} %bitcast.2, ...), custom_call_target="tpu_custom_call" | custom-call | flops 201326592 | bytes 25165824 | tf_op jit(solution)/shard_map/pallas_call | solution.py:254
  14.8 0.0 collective-permute-done.peer_q
  14.8 0.0 collective-permute-done.1.refs_0_
  14.8 4.5 %collective-permute-done.2.refs_1_ = bf16[256,256]{1,0:T(8,128)(2,1)S(1)} collective-permute-done((bf16[256,256]{1,0:T(8,128)(2,1)S(1)}, bf16[256,256]{1,0:T(8,128)(2,1)S(1)}, u32[]{:S(2)}, u32[]{:S(2)}) %collective-permute-start.2) | collective-permute-done | bytes 131104 | tf_op jit(solution)/shard_map/ppermute | solution.py:312
  19.2 0.0 collective-permute-done.3.refs_2_
  19.2 0.0 collective-permute-done.4.refs_3_
  19.3 0.6 %shard_map.66 = (f32[4,48,128]{2,1,0:T(8,128)S(1)}, bf16[3,48,128]{2,1,0:T(8,128)(2,1)S(1)}) custom-call(s32[2,8]{1,0:T(2,128)S(4)} %get-tuple-element.22.table, bf16[4,48,128]{2,1,0:T(8,128)(2,1)S(1)} %get-tuple-element.26.own_q, bf16[3,48,128]{2,1,0:T(8,128)(2,1)S(1)} %collective-permute-done.peer_q, bf16[128,256]{1,0:T(8,128)(2,1)S(1)} %get-tuple-element.28.fresh, ...), custom_call_target="tpu_custom_call" | custom-call | tf_op jit(solution)/shard_map/pallas_call | solution.py:254
  19.8 0.1 collective-permute-start.5
  19.9 1.2 %collective-permute-done.5.arrived = bf16[3,48,128]{2,1,0:T(8,128)(2,1)S(1)} collective-permute-done((bf16[3,48,128]{2,1,0:T(8,128)(2,1)S(1)}, bf16[3,48,128]{2,1,0:T(8,128)(2,1)S(1)}, u32[]{:S(2)}, u32[]{:S(2)}) %collective-permute-start.5) | collective-permute-done | bytes 36896 | tf_op jit(solution)/shard_map/ppermute | solution.py:352
  21.1 0.9 %shard_map.67 = (bf16[128,1536]{1,0:T(8,128)(2,1)S(1)}, bf16[128,1536]{1,0:T(8,128)(2,1)S(1)}, f32[1920,128]{1,0:T(8,128)S(1)}) custom-call(s32[2,8]{1,0:T(2,128)S(4)} %get-tuple-element.22.table, f32[1920,128]{1,0:T(8,128)S(1)} %get-tuple-element.25.attn, f32[4,48,128]{2,1,0:T(8,128)S(1)} %get-tuple-element.33.found, ...), custom_call_target="tpu_custom_call", output_to_operand_aliasing={{2}: (1, {})} | custom-call | tf_op jit(solution)/shard_map/pallas_call | solution.py:254
  22.0 0.2 collective-permute-start.6
  22.2 0.8 %shard_map.68.own = f32[128,1536]{1,0:T(8,128)S(1)} custom-call(bf16[128,1536]{1,0:T(8,128)(2,1)S(1)} %get-tuple-element.36.lhs, bf16[1536,1536]{1,0:T(8,128)(2,1)S(1)} %get-tuple-element.37.weight), custom_call_target="tpu_custom_call" | custom-call | flops 603979776 | bytes 6291456 | tf_op jit(solution)/shard_map/pallas_call | solution.py:254
  23.0 0.8 %collective-permute-done.6.others = bf16[128,1536]{1,0:T(8,128)(2,1)S(1)} collective-permute-done((bf16[128,1536]{1,0:T(8,128)(2,1)S(1)}, bf16[128,1536]{1,0:T(8,128)(2,1)S(1)}, u32[]{:S(2)}, u32[]{:S(2)}) %collective-permute-start.6) | collective-permute-done | bytes 393248 | tf_op jit(solution)/shard_map/ppermute | solution.py:364
  23.8 0.8 %shard_map.69 = bf16[128,1536]{1,0:T(8,128)(2,1)} custom-call(f32[128,1536]{1,0:T(8,128)S(1)} %shard_map.68.own, bf16[128,1536]{1,0:T(8,128)(2,1)S(1)} %collective-permute-done.6.others), custom_call_target="tpu_custom_call" | custom-call | tf_op jit(solution)/shard_map/pallas_call | solution.py:254
Async XLA Ops:
  2.1 12.7 %collective-permute-start.1 = (bf16[256,256]{1,0:T(8,128)(2,1)S(1)}, bf16[256,256]{1,0:T(8,128)(2,1)S(1)}, u32[]{:S(2)}, u32[]{:S(2)}) collective-permute-start(bf16[256,256]{1,0:T(8,128)(2,1)S(1)} %get-tuple-element.29), channel_id=1, source_target_pairs={{0,14},{1,13},{2,12},{3,15},{4,10},{5,9},{6,8},{7,11},{8,6},{9,5},... | collective-permute-start | bytes 393224 | tf_op jit(solution)/shard_map/ppermute | solution.py:312
  8.2 11.1 %collective-permute-start.2 = (bf16[256,256]{1,0:T(8,128)(2,1)S(1)}, bf16[256,256]{1,0:T(8,128)(2,1)S(1)}, u32[]{:S(2)}, u32[]{:S(2)}) collective-permute-start(bf16[256,256]{1,0:T(8,128)(2,1)S(1)} %get-tuple-element.30), channel_id=1, source_target_pairs={{0,10},{1,9},{2,8},{3,11},{4,14},{5,13},{6,12},{7,15},{8,2},{9,1},... | collective-permute-start | bytes 393224 | tf_op jit(solution)/shard_map/ppermute | solution.py:312
  8.2 11.1 %collective-permute-start.3 = (bf16[256,256]{1,0:T(8,128)(2,1)S(1)}, bf16[256,256]{1,0:T(8,128)(2,1)S(1)}, u32[]{:S(2)}, u32[]{:S(2)}) collective-permute-start(bf16[256,256]{1,0:T(8,128)(2,1)S(1)} %get-tuple-element.31), channel_id=1, source_target_pairs={{0,6},{1,5},{2,4},{3,7},{4,2},{5,1},{6,0},{7,3},{8,14},{9,13},{10,... | collective-permute-start | bytes 393224 | tf_op jit(solution)/shard_map/ppermute | solution.py:312
  9.9 9.4 %collective-permute-start.4 = (bf16[256,256]{1,0:T(8,128)(2,1)S(1)}, bf16[256,256]{1,0:T(8,128)(2,1)S(1)}, u32[]{:S(2)}, u32[]{:S(2)}) collective-permute-start(bf16[256,256]{1,0:T(8,128)(2,1)S(1)} %get-tuple-element.32), channel_id=1, source_target_pairs={{0,2},{1,3},{2,0},{3,1},{4,6},{5,7},{6,4},{7,5},{8,10},{9,11},{10,... | collective-permute-start | bytes 393224 | tf_op jit(solution)/shard_map/ppermute | solution.py:312
  10.3 4.5 %collective-permute-start = (bf16[3,48,128]{2,1,0:T(8,128)(2,1)S(1)}, bf16[3,48,128]{2,1,0:T(8,128)(2,1)S(1)}, u32[]{:S(2)}, u32[]{:S(2)}) collective-permute-start(bf16[3,48,128]{2,1,0:T(8,128)(2,1)S(1)} %get-tuple-element.27), channel_id=1, source_target_pairs={{0,1},{1,0},{2,3},{3,2},{4,5},{5,4},{6,7},{7,6},{8,9},{9,8},{10,11... | collective-permute-start | bytes 110600 | tf_op jit(solution)/shard_map/ppermute | solution.py:315
  19.8 1.3 %collective-permute-start.5 = (bf16[3,48,128]{2,1,0:T(8,128)(2,1)S(1)}, bf16[3,48,128]{2,1,0:T(8,128)(2,1)S(1)}, u32[]{:S(2)}, u32[]{:S(2)}) collective-permute-start(bf16[3,48,128]{2,1,0:T(8,128)(2,1)S(1)} %get-tuple-element.34), channel_id=1, source_target_pairs={{0,1},{1,0},{2,3},{3,2},{4,5},{5,4},{6,7},{7,6},{8,9},{9,8},{10,11... | collective-permute-start | bytes 110600 | tf_op jit(solution)/shard_map/ppermute | solution.py:352
  22.0 1.8 %collective-permute-start.6 = (bf16[128,1536]{1,0:T(8,128)(2,1)S(1)}, bf16[128,1536]{1,0:T(8,128)(2,1)S(1)}, u32[]{:S(2)}, u32[]{:S(2)}) collective-permute-start(bf16[128,1536]{1,0:T(8,128)(2,1)S(1)} %get-tuple-element.38), channel_id=1, source_target_pairs={{0,1},{1,0},{2,3},{3,2},{4,5},{5,4},{6,7},{7,6},{8,9},{9,8},{10,11... | collective-permute-start | bytes 1179656 | tf_op jit(solution)/shard_map/ppermute | solution.py:364

commit v5 on v4

--- a/solution.py
+++ b/solution.py
@@ -17,7 +17,7 @@
 
 
 def partner(insts, ops, i, core):
-    return jnp.int32(1) if i == ops - 1 else insts - 1 - 2 * i - core
+    return jnp.int32(1) if i == ops - 1 else insts - 2 - 2 * i + core
 
 
 def start_copies(pairs, sems):
@@ -307,7 +307,7 @@
         pairs = []
         for a in range(insts):
             for c in range(cores):
-                m = 1 if i == ops - 1 else insts - 1 - 2 * i - c
+                m = 1 if i == ops - 1 else insts - 2 - 2 * i + c
                 pairs.append((a * cores + c, (a ^ m) * cores + c))
         blocks[i] = lax.ppermute(sends[i], ("inst", "tp"), pairs)
 

time: 24.8 us -> 24.8 us (level)
  waiting for transfers between devices: 6.45 us -> 7.21 us
  starting transfers between devices: 8.47 us -> 7.72 us
    ppermute x4, waiting for transfers between devices: 4.47 us -> 5.23 us  [body(): blocks[i] = lax.ppermute(sends[i], ('inst', 'tp'), pairs)]
    ppermute x4, starting transfers between devices: 8.17 us -> 7.42 us  [body(): blocks[i] = lax.ppermute(sends[i], ('inst', 'tp'), pairs)]
where the time goes in v5:
time: 24.8 us; the launch traced here: 24.6 us
  Pallas kernels  9.57 us (39%)
  starting transfers between devices  7.72 us (31%)
  waiting for transfers between devices  7.21 us (29%)
    pallas_call x6, Pallas kernels, call(): pl.pallas_call(kernel, out_shape=[space(shape.shape, shape.dtype) for spa...  9.57 us
    ppermute x4, starting transfers between devices, body(): blocks[i] = lax.ppermute(sends[i], ('inst', 'tp'), pairs)  7.42 us
    ppermute x4, waiting for transfers between devices, body(): blocks[i] = lax.ppermute(sends[i], ('inst', 'tp'), pairs)  5.23 us
    ppermute x1, waiting for transfers between devices, body(): arrived = lax.ppermute(sent, 'tp', swap)  1.2 us
    ppermute x1, waiting for transfers between devices, body(): others = lax.ppermute(partial, 'tp', swap)  0.78 us
  transfers between devices with their start and end apart: 7, of which 3 were waited for; matrix products, arithmetic and copies ran while one was open for 0% of the time, Pallas kernels for 21%

profile of v5, /device:TPU:0, one launch (start us, length us, event | category | flops | bytes accessed | tf_op | source)
XLA Modules:
  0.0 24.6 jit_solution(9474448439576342898)
XLA Ops:
  0.0 2.1 %shard_map.64 = (s32[2,8]{1,0:T(2,128)S(4)}, bf16[6144,256]{1,0:T(8,128)(2,1)S(1)}, f32[1920,128]{1,0:T(8,128)S(1)}, bf16[4,48,128]{2,1,0:T(8,128)(2,1)S(1)}, bf...) custom-call(s32[8,32]{1,0:T(8,128)} %anchor_h.1, ...), custom_call_target="tpu_custom_call" | custom-call | tf_op jit(solution)/shard_map/pallas_call | solution.py:254
  2.1 5.1 %collective-permute-start.1 = (bf16[256,256]{1,0:T(8,128)(2,1)S(1)}, bf16[256,256]{1,0:T(8,128)(2,1)S(1)}, u32[]{:S(2)}, u32[]{:S(2)}) collective-permute-start(bf16[256,256]{1,0:T(8,128)(2,1)S(1)} %get-tuple-element.29), channel_id=1, source_target_pairs={{0,12},{1,15},{2,14},{3,13},{4,8},{5,11},{6,10},{7,9},{8,4},{9,7},... | collective-permute-start | bytes 393224 | tf_op jit(solution)/shard_map/ppermute | solution.py:312
  7.2 0.0 collective-permute-start.2
  7.2 0.6 %collective-permute-start.3 = (bf16[256,256]{1,0:T(8,128)(2,1)S(1)}, bf16[256,256]{1,0:T(8,128)(2,1)S(1)}, u32[]{:S(2)}, u32[]{:S(2)}) collective-permute-start(bf16[256,256]{1,0:T(8,128)(2,1)S(1)} %get-tuple-element.31), channel_id=1, source_target_pairs={{0,4},{1,7},{2,6},{3,5},{4,0},{5,3},{6,2},{7,1},{8,12},{9,15},{10,... | collective-permute-start | bytes 393224 | tf_op jit(solution)/shard_map/ppermute | solution.py:312
  7.9 1.7 %collective-permute-start.4 = (bf16[256,256]{1,0:T(8,128)(2,1)S(1)}, bf16[256,256]{1,0:T(8,128)(2,1)S(1)}, u32[]{:S(2)}, u32[]{:S(2)}) collective-permute-start(bf16[256,256]{1,0:T(8,128)(2,1)S(1)} %get-tuple-element.32), channel_id=1, source_target_pairs={{0,2},{1,3},{2,0},{3,1},{4,6},{5,7},{6,4},{7,5},{8,10},{9,11},{10,... | collective-permute-start | bytes 393224 | tf_op jit(solution)/shard_map/ppermute | solution.py:312
  9.5 0.0 collective-permute-start
  9.5 4.5 %shard_map.65 = (f32[1920,128]{1,0:T(8,128)S(1)}, bf16[128,256]{1,0:T(8,128)(2,1)S(1)}, bf16[1536,1536]{1,0:T(8,128)(2,1)S(1)}, bf16[1536,1536]{1,0:T(8,128)(2,1)S(1)}) custom-call(f32[1920,128]{1,0:T(8,128)S(1)} %get-tuple-element.23.spread, bf16[6144,256]{1,0:T(8,128)(2,1)S(1)} %get-tuple-element.24.pool, bf16[128,256]{1,0:T(8,128)(2,1)} %bitcast.2, ...), custom_call_target="tpu_custom_call" | custom-call | flops 201326592 | bytes 25165824 | tf_op jit(solution)/shard_map/pallas_call | solution.py:254
  14.0 0.0 collective-permute-done.peer_q
  14.0 0.0 collective-permute-done.1.refs_0_
  14.0 5.2 %collective-permute-done.2.refs_1_ = bf16[256,256]{1,0:T(8,128)(2,1)S(1)} collective-permute-done((bf16[256,256]{1,0:T(8,128)(2,1)S(1)}, bf16[256,256]{1,0:T(8,128)(2,1)S(1)}, u32[]{:S(2)}, u32[]{:S(2)}) %collective-permute-start.2) | collective-permute-done | bytes 131104 | tf_op jit(solution)/shard_map/ppermute | solution.py:312
  19.2 0.0 collective-permute-done.3.refs_2_
  19.2 0.0 collective-permute-done.4.refs_3_
  19.3 0.6 %shard_map.66 = (f32[4,48,128]{2,1,0:T(8,128)S(1)}, bf16[3,48,128]{2,1,0:T(8,128)(2,1)S(1)}) custom-call(s32[2,8]{1,0:T(2,128)S(4)} %get-tuple-element.22.table, bf16[4,48,128]{2,1,0:T(8,128)(2,1)S(1)} %get-tuple-element.26.own_q, bf16[3,48,128]{2,1,0:T(8,128)(2,1)S(1)} %collective-permute-done.peer_q, bf16[128,256]{1,0:T(8,128)(2,1)S(1)} %get-tuple-element.28.fresh, ...), custom_call_target="tpu_custom_call" | custom-call | tf_op jit(solution)/shard_map/pallas_call | solution.py:254
  19.8 0.1 collective-permute-start.5
  19.9 1.2 %collective-permute-done.5.arrived = bf16[3,48,128]{2,1,0:T(8,128)(2,1)S(1)} collective-permute-done((bf16[3,48,128]{2,1,0:T(8,128)(2,1)S(1)}, bf16[3,48,128]{2,1,0:T(8,128)(2,1)S(1)}, u32[]{:S(2)}, u32[]{:S(2)}) %collective-permute-start.5) | collective-permute-done | bytes 36896 | tf_op jit(solution)/shard_map/ppermute | solution.py:352
  21.1 0.9 %shard_map.67 = (bf16[128,1536]{1,0:T(8,128)(2,1)S(1)}, bf16[128,1536]{1,0:T(8,128)(2,1)S(1)}, f32[1920,128]{1,0:T(8,128)S(1)}) custom-call(s32[2,8]{1,0:T(2,128)S(4)} %get-tuple-element.22.table, f32[1920,128]{1,0:T(8,128)S(1)} %get-tuple-element.25.attn, f32[4,48,128]{2,1,0:T(8,128)S(1)} %get-tuple-element.33.found, ...), custom_call_target="tpu_custom_call", output_to_operand_aliasing={{2}: (1, {})} | custom-call | tf_op jit(solution)/shard_map/pallas_call | solution.py:254
  22.0 0.2 collective-permute-start.6
  22.2 0.8 %shard_map.68.own = f32[128,1536]{1,0:T(8,128)S(1)} custom-call(bf16[128,1536]{1,0:T(8,128)(2,1)S(1)} %get-tuple-element.36.lhs, bf16[1536,1536]{1,0:T(8,128)(2,1)S(1)} %get-tuple-element.37.weight), custom_call_target="tpu_custom_call" | custom-call | flops 603979776 | bytes 6291456 | tf_op jit(solution)/shard_map/pallas_call | solution.py:254
  23.0 0.8 %collective-permute-done.6.others = bf16[128,1536]{1,0:T(8,128)(2,1)S(1)} collective-permute-done((bf16[128,1536]{1,0:T(8,128)(2,1)S(1)}, bf16[128,1536]{1,0:T(8,128)(2,1)S(1)}, u32[]{:S(2)}, u32[]{:S(2)}) %collective-permute-start.6) | collective-permute-done | bytes 393248 | tf_op jit(solution)/shard_map/ppermute | solution.py:364
  23.8 0.8 %shard_map.69 = bf16[128,1536]{1,0:T(8,128)(2,1)} custom-call(f32[128,1536]{1,0:T(8,128)S(1)} %shard_map.68.own, bf16[128,1536]{1,0:T(8,128)(2,1)S(1)} %collective-permute-done.6.others), custom_call_target="tpu_custom_call" | custom-call | tf_op jit(solution)/shard_map/pallas_call | solution.py:254
Async XLA Ops:
  2.1 11.9 %collective-permute-start.1 = (bf16[256,256]{1,0:T(8,128)(2,1)S(1)}, bf16[256,256]{1,0:T(8,128)(2,1)S(1)}, u32[]{:S(2)}, u32[]{:S(2)}) collective-permute-start(bf16[256,256]{1,0:T(8,128)(2,1)S(1)} %get-tuple-element.29), channel_id=1, source_target_pairs={{0,12},{1,15},{2,14},{3,13},{4,8},{5,11},{6,10},{7,9},{8,4},{9,7},... | collective-permute-start | bytes 393224 | tf_op jit(solution)/shard_map/ppermute | solution.py:312
  7.2 12.0 %collective-permute-start.2 = (bf16[256,256]{1,0:T(8,128)(2,1)S(1)}, bf16[256,256]{1,0:T(8,128)(2,1)S(1)}, u32[]{:S(2)}, u32[]{:S(2)}) collective-permute-start(bf16[256,256]{1,0:T(8,128)(2,1)S(1)} %get-tuple-element.30), channel_id=1, source_target_pairs={{0,8},{1,11},{2,10},{3,9},{4,12},{5,15},{6,14},{7,13},{8,0},{9,3},... | collective-permute-start | bytes 393224 | tf_op jit(solution)/shard_map/ppermute | solution.py:312
  7.2 12.0 %collective-permute-start.3 = (bf16[256,256]{1,0:T(8,128)(2,1)S(1)}, bf16[256,256]{1,0:T(8,128)(2,1)S(1)}, u32[]{:S(2)}, u32[]{:S(2)}) collective-permute-start(bf16[256,256]{1,0:T(8,128)(2,1)S(1)} %get-tuple-element.31), channel_id=1, source_target_pairs={{0,4},{1,7},{2,6},{3,5},{4,0},{5,3},{6,2},{7,1},{8,12},{9,15},{10,... | collective-permute-start | bytes 393224 | tf_op jit(solution)/shard_map/ppermute | solution.py:312
  7.9 11.4 %collective-permute-start.4 = (bf16[256,256]{1,0:T(8,128)(2,1)S(1)}, bf16[256,256]{1,0:T(8,128)(2,1)S(1)}, u32[]{:S(2)}, u32[]{:S(2)}) collective-permute-start(bf16[256,256]{1,0:T(8,128)(2,1)S(1)} %get-tuple-element.32), channel_id=1, source_target_pairs={{0,2},{1,3},{2,0},{3,1},{4,6},{5,7},{6,4},{7,5},{8,10},{9,11},{10,... | collective-permute-start | bytes 393224 | tf_op jit(solution)/shard_map/ppermute | solution.py:312
  9.5 4.5 %collective-permute-start = (bf16[3,48,128]{2,1,0:T(8,128)(2,1)S(1)}, bf16[3,48,128]{2,1,0:T(8,128)(2,1)S(1)}, u32[]{:S(2)}, u32[]{:S(2)}) collective-permute-start(bf16[3,48,128]{2,1,0:T(8,128)(2,1)S(1)} %get-tuple-element.27), channel_id=1, source_target_pairs={{0,1},{1,0},{2,3},{3,2},{4,5},{5,4},{6,7},{7,6},{8,9},{9,8},{10,11... | collective-permute-start | bytes 110600 | tf_op jit(solution)/shard_map/ppermute | solution.py:315
  19.8 1.3 %collective-permute-start.5 = (bf16[3,48,128]{2,1,0:T(8,128)(2,1)S(1)}, bf16[3,48,128]{2,1,0:T(8,128)(2,1)S(1)}, u32[]{:S(2)}, u32[]{:S(2)}) collective-permute-start(bf16[3,48,128]{2,1,0:T(8,128)(2,1)S(1)} %get-tuple-element.34), channel_id=1, source_target_pairs={{0,1},{1,0},{2,3},{3,2},{4,5},{5,4},{6,7},{7,6},{8,9},{9,8},{10,11... | collective-permute-start | bytes 110600 | tf_op jit(solution)/shard_map/ppermute | solution.py:352
  22.0 1.8 %collective-permute-start.6 = (bf16[128,1536]{1,0:T(8,128)(2,1)S(1)}, bf16[128,1536]{1,0:T(8,128)(2,1)S(1)}, u32[]{:S(2)}, u32[]{:S(2)}) collective-permute-start(bf16[128,1536]{1,0:T(8,128)(2,1)S(1)} %get-tuple-element.38), channel_id=1, source_target_pairs={{0,1},{1,0},{2,3},{3,2},{4,5},{5,4},{6,7},{7,6},{8,9},{9,8},{10,11... | collective-permute-start | bytes 1179656 | tf_op jit(solution)/shard_map/ppermute | solution.py:364

commit v6 on v5

--- a/solution.py
+++ b/solution.py
@@ -13,6 +13,7 @@
 MAXB = 2
 WIN = MAXB * BLK
 PAD = 8
+FEW = 16
 MIB = 1024 * 1024
 
 
@@ -28,10 +29,10 @@
 
 
 def plan_kernel(
-    ops, stride, anchor_h, lengths_h, queries_h, pool_h,
-    table, pool, spread, own_q, sent_q, *refs,
+    ops, asked, stride, anchor_h, lengths_h, queries_h, fresh_h, pool_h,
+    table, lists, pool, spread, fresh, own_q, sent_q, asked_f, *refs,
 ):
-    sends, (anchor, lengths, offs, queries, sems) = refs[:ops], refs[ops:]
+    sends, (anchor, lengths, offs, queries, keys, values, few, sems) = refs[:ops], refs[ops:]
     insts, slots = anchor.shape
     steps, _, width = queries.shape
     heads = width // HDIM
@@ -39,22 +40,36 @@
     blocks = pool.shape[0] // BLK
     own, core = lax.axis_index("inst"), lax.axis_index("tp")
     loads = start_copies(
-        [(anchor_h, anchor), (lengths_h, lengths), (queries_h, queries), (pool_h, pool)], sems
+        [
+            (anchor_h, anchor),
+            (lengths_h, lengths),
+            (queries_h, queries),
+            (fresh_h, fresh),
+            (pool_h, pool),
+        ],
+        sems,
     )
     loads[0].wait()
     loads[1].wait()
     for m in range(insts):
         table[0, m] = slots
         table[1, m] = 1
+        table[2, m] = 1
         offs[m] = 0
-    start = jnp.int32(0)
+    longer = blocks - slots
+    start, found = jnp.int32(0), jnp.int32(0)
     for j in range(slots):
-        source = anchor[own, j]
+        source, count = anchor[own, j], lengths[own, j]
         dest = (2 * own - source) & (insts - 1)
         table[0, own ^ source] = j
         table[1, own ^ source] = lengths[source, j]
+        table[2, own ^ dest] = count
         offs[own ^ dest] = start
-        start = start + lengths[own, j]
+        place = jnp.where(count > 1, found, longer + j - found)
+        lists[0, place] = j
+        lists[1, place] = start
+        start = start + count
+        found = found + count - 1
     loads[2].wait()
     for s in range(steps):
         for h in range(heads):
@@ -68,11 +83,57 @@
         j = table[0, partner(insts, ops, i, 1 - core)]
         sent_q[i] = spread[pl.ds(j, rows, stride=stride), :].astype(jnp.bfloat16)
     loads[3].wait()
+    keys[0 : steps * slots, :] = fresh[:, :HDIM].astype(jnp.float32)
+    values[0 : steps * slots, :] = fresh[:, HDIM:].astype(jnp.float32)
+    few[...] = jnp.zeros_like(few)
+    for n, i in enumerate(asked):
+        j = table[0, partner(insts, ops, i, core)]
+        for u in range(steps):
+            few[u : u + 1, :] = keys[pl.ds(u * slots + j, 1), :]
+            few[FEW + u : FEW + u + 1, :] = values[pl.ds(u * slots + j, 1), :]
+        asked_f[n] = few[...].astype(jnp.bfloat16)
+    loads[4].wait()
     for i in range(ops):
         at = offs[partner(insts, ops, i, core)]
         for b in range(MAXB):
             row = pl.multiple_of(jnp.minimum(at + b, blocks - 1) * BLK, BLK)
             sends[i][b * BLK : (b + 1) * BLK, :] = pool[pl.ds(row, BLK), :]
+
+
+def ask_kernel(asked, own_q, peer_q, asked_f, *outs):
+    rows = own_q.shape[1]
+    for n, i in enumerate(asked):
+        outs[n][0:rows, :] = own_q[i]
+        outs[n][rows : 2 * rows, :] = peer_q[i]
+        outs[n][2 * rows :, :] = asked_f[n]
+
+
+def answer_kernel(ops, asked, steps, after, table, *refs):
+    count = len(asked)
+    questions, windows, outs = refs[:count], refs[count : 2 * count], refs[2 * count :]
+    rows = outs[0].shape[0]
+    heads = rows // 2 // steps
+    insts = table.shape[1]
+    core = lax.axis_index("tp")
+    step = lax.broadcasted_iota(jnp.int32, (rows, HDIM), 0) // heads % steps
+    col = lax.broadcasted_iota(jnp.int32, (rows, HDIM), 1)
+    within = lax.broadcasted_iota(jnp.int32, (rows, WIN), 1)
+    empty = jnp.zeros((HDIM - FEW, HDIM), jnp.bfloat16)
+    scores, recents, lates = [], [], []
+    for n, i in enumerate(asked):
+        limit = table[2, partner(insts, ops, i, core)] * BLK
+        query = questions[n][0:rows, :]
+        score = contract_last(query, windows[n][:, :HDIM])
+        scores.append(jnp.where(within < limit, score, -jnp.inf))
+        keys = jnp.concatenate([questions[n][rows : rows + FEW, :], empty])
+        lates.append(jnp.concatenate([questions[n][rows + FEW :, :], empty]))
+        recents.append(jnp.where(col <= step, contract_last(query, keys), -jnp.inf))
+    done = attend_all(scores, recents, [window[:, HDIM:] for window in windows])
+    for n, (mixed, weight) in enumerate(done):
+        out = mixed + jnp.dot(
+            weight.astype(jnp.bfloat16), lates[n], preferred_element_type=jnp.float32
+        )
+        outs[n][...] = out.astype(jnp.bfloat16)
 
 
 def contract_last(a, b):
@@ -101,51 +162,13 @@
     ]
 
 
-def stay_kernel(
-    stride, steps, group, spread, pool, fresh_h, lengths_h, weight_h,
-    attn, fresh, peer_w, own_w,
-    lengths, order, starts, recent, late, sems,
-):
-    slots = lengths.shape[1]
-    rows = spread.shape[0] // stride
-    heads = rows // steps
-    half = own_w.shape[1]
-    own, core = lax.axis_index("inst"), lax.axis_index("tp")
-    own_cols = pl.ds(pl.multiple_of(core * half, HDIM), half)
-    peer_cols = pl.ds(pl.multiple_of((1 - core) * half, HDIM), half)
-    loads = start_copies(
-        [
-            (lengths_h, lengths),
-            (fresh_h, fresh),
-            (weight_h.at[:, peer_cols], peer_w),
-            (weight_h.at[:, own_cols], own_w),
-        ],
-        sems,
-    )
-    loads[0].wait()
-    longer = pool.shape[0] // BLK - slots
-    group = math.gcd(group, longer, slots - longer)
-    start, found = jnp.int32(0), jnp.int32(0)
-    for j in range(slots):
-        count = lengths[own, j]
-        place = jnp.where(count > 1, found, longer + j - found)
-        order[place] = j
-        starts[place] = start
-        start = start + count
-        found = found + count - 1
-    loads[1].wait()
-    slot = lax.broadcasted_iota(jnp.int32, (slots, steps * slots), 0)
-    col = lax.broadcasted_iota(jnp.int32, (slots, steps * slots), 1)
-    for i in range(rows):
-        at = pl.ds(i * stride, slots)
-        score = contract_last(spread[at, :].astype(jnp.bfloat16), fresh[:, :HDIM])
-        mine = (col % slots == slot) & (col // slots <= i // heads)
-        recent[at, :] = jnp.where(mine, score, -jnp.inf)
-
-    def some(first, size, g, _):
+def stay_requests(stride, rows, group, first, count, size, lists, spread, pool, recent, attn, late):
+    group = math.gcd(group, count)
+
+    def some(g, _):
         places = [first + g * group + u for u in range(group)]
-        picked = [pl.ds(order[at], rows, stride=stride) for at in places]
-        windows = [pl.ds(pl.multiple_of(starts[at] * BLK, BLK), size) for at in places]
+        picked = [pl.ds(lists[0, at], rows, stride=stride) for at in places]
+        windows = [pl.ds(pl.multiple_of(lists[1, at] * BLK, BLK), size) for at in places]
         queries = [spread[at, :].astype(jnp.bfloat16) for at in picked]
         recents = [recent[at, :] for at in picked]
         scores = [contract_last(q, pool[w, :HDIM]) for q, w in zip(queries, windows)]
@@ -155,18 +178,53 @@
             late[at, :] = weight
         return 0
 
-    lax.fori_loop(0, longer // group, functools.partial(some, 0, WIN), 0)
-    lax.fori_loop(0, (slots - longer) // group, functools.partial(some, longer, BLK), 0)
+    lax.fori_loop(0, count // group, some, 0)
+
+
+def long_kernel(
+    stride, steps, group, after, lists, spread, pool, fresh, weight_h,
+    attn, late, recent, peer_w, sems,
+):
+    slots = lists.shape[1]
+    rows = spread.shape[0] // stride
+    heads = rows // steps
+    half = peer_w.shape[1]
+    peer = (1 - lax.axis_index("tp")) * half
+    load = start_copies([(weight_h.at[:, pl.ds(pl.multiple_of(peer, HDIM), half)], peer_w)], sems)
+    slot = lax.broadcasted_iota(jnp.int32, (slots, steps * slots), 0)
+    col = lax.broadcasted_iota(jnp.int32, (slots, steps * slots), 1)
+    for i in range(rows):
+        at = pl.ds(i * stride, slots)
+        score = contract_last(spread[at, :].astype(jnp.bfloat16), fresh[:, :HDIM])
+        mine = (col % slots == slot) & (col // slots <= i // heads)
+        recent[at, :] = jnp.where(mine, score, -jnp.inf)
+    longer = pool.shape[0] // BLK - slots
+    stay_requests(stride, rows, group, 0, longer, WIN, lists, spread, pool, recent, attn, late)
+    load[0].wait()
+
+
+def short_kernel(
+    stride, group, after, lists, spread, pool, fresh, weight_h, recent, attn_in, late_in,
+    attn, late, own_w, sems,
+):
+    slots = lists.shape[1]
+    rows = spread.shape[0] // stride
+    half = own_w.shape[1]
+    own = lax.axis_index("tp") * half
+    load = start_copies([(weight_h.at[:, pl.ds(pl.multiple_of(own, HDIM), half)], own_w)], sems)
+    longer = pool.shape[0] // BLK - slots
+    stay_requests(
+        stride, rows, group, longer, slots - longer, BLK, lists, spread, pool, recent, attn, late
+    )
     for i in range(rows):
         at = pl.ds(i * stride, slots)
         attn[at, :] = attn[at, :] + jnp.dot(
             late[at, :].astype(jnp.bfloat16), fresh[:, HDIM:], preferred_element_type=jnp.float32
         )
-    loads[2].wait()
-    loads[3].wait()
-
-
-def move_kernel(ops, steps, slots, group, table, own_q, peer_q, fresh, *refs):
+    load[0].wait()
+
+
+def move_kernel(ops, asked, steps, slots, group, after, table, own_q, peer_q, fresh, *refs):
     blocks, (found, sent) = refs[:ops], refs[ops:]
     rows = own_q.shape[1]
     heads = rows // steps
@@ -177,8 +235,12 @@
     col = lax.broadcasted_iota(jnp.int32, shape, 1)
     owner = jnp.where(col // slots <= step, col % slots, -1)
     within = lax.broadcasted_iota(jnp.int32, (2 * rows, WIN), 1)
-    for first in range(0, ops, group):
-        batch = range(first, min(first + group, ops))
+    for i in asked:
+        found[i] = blocks[i][0:rows, :].astype(jnp.float32)
+        sent[i] = blocks[i][rows : 2 * rows, :]
+    moved = [i for i in range(ops) if i not in asked]
+    for first in range(0, len(moved), group):
+        batch = moved[first : first + group]
         queries, recents, scores = [], [], []
         for i in batch:
             query = own_q[i]
@@ -283,15 +345,25 @@
     def f32(*shape):
         return jax.ShapeDtypeStruct(shape, jnp.float32)
 
-    table, pool, spread, own_q, sent_q, *sends = call(
-        functools.partial(plan_kernel, ops, stride),
-        [(hbm, anchor), (hbm, lengths), (hbm, queries), (hbm, cache_pool)],
-        [
-            (smem, jax.ShapeDtypeStruct((2, insts), jnp.int32)),
+    asked = (1,)
+    table, lists, pool, spread, fresh, own_q, sent_q, asked_f, *sends = call(
+        functools.partial(plan_kernel, ops, asked, stride),
+        [
+            (hbm, anchor),
+            (hbm, lengths),
+            (hbm, queries),
+            (hbm, new_kv.reshape(steps * slots, kvw)),
+            (hbm, cache_pool),
+        ],
+        [
+            (smem, jax.ShapeDtypeStruct((3, insts), jnp.int32)),
+            (smem, jax.ShapeDtypeStruct((2, slots), jnp.int32)),
             (vmem, bf16(*cache_pool.shape)),
             (vmem, f32(rows * stride, HDIM)),
+            (vmem, bf16(steps * slots, kvw)),
             (vmem, bf16(ops, rows, HDIM)),
             (vmem, bf16(ops - 1, rows, HDIM)),
+            (vmem, bf16(len(asked), 2 * FEW, HDIM)),
         ]
         + [(vmem, bf16(WIN, kvw))] * ops,
         [
@@ -299,53 +371,81 @@
             smem(lengths.shape, jnp.int32),
             smem((insts,), jnp.int32),
             vmem(queries.shape, jnp.bfloat16),
-            dma((4,)),
-        ],
-    )
-    blocks = [None] * ops
-    for i in reversed(range(ops)):
+            vmem((steps * slots + PAD, HDIM), jnp.float32),
+            vmem((steps * slots + PAD, HDIM), jnp.float32),
+            vmem((2 * FEW, HDIM), jnp.float32),
+            dma((5,)),
+        ],
+    )
+    swap = [(c, cores - 1 - c) for c in range(cores)]
+    peer_q = lax.ppermute(sent_q, "tp", swap)
+
+    def exchange(i, array):
         pairs = []
         for a in range(insts):
             for c in range(cores):
                 m = 1 if i == ops - 1 else insts - 2 - 2 * i + c
                 pairs.append((a * cores + c, (a ^ m) * cores + c))
-        blocks[i] = lax.ppermute(sends[i], ("inst", "tp"), pairs)
-
-    swap = [(c, cores - 1 - c) for c in range(cores)]
-    peer_q = lax.ppermute(sent_q, "tp", swap)
-
-    attn, fresh, peer_w, own_w = call(
-        functools.partial(stay_kernel, stride, steps, 8),
-        [
+        return lax.ppermute(array, ("inst", "tp"), pairs)
+
+    blocks = [None] * ops
+    for i in reversed(range(ops)):
+        if i not in asked:
+            blocks[i] = exchange(i, sends[i])
+    questions = call(
+        functools.partial(ask_kernel, asked),
+        [(vmem, own_q), (vmem, peer_q), (vmem, asked_f)],
+        [(vmem, bf16(2 * rows + 2 * FEW, HDIM))] * len(asked),
+    )
+    asking = [exchange(i, question) for i, question in zip(asked, questions)]
+    half_cost = pl.CostEstimate(
+        flops=2 * slots * rows * WIN * HDIM, bytes_accessed=10 * MIB, transcendentals=0
+    )
+    attn, late, recent, peer_w = call(
+        functools.partial(long_kernel, stride, steps, 8),
+        [
+            (vmem, questions[0]),
+            (smem, lists),
             (vmem, spread),
             (vmem, pool),
-            (hbm, new_kv.reshape(steps * slots, kvw)),
-            (hbm, lengths),
+            (vmem, fresh),
             (hbm, out_weight),
         ],
-        [
-            (vmem, f32(rows * stride, HDIM)),
-            (vmem, bf16(steps * slots, kvw)),
-            (vmem, bf16(depth, half)),
-            (vmem, bf16(depth, half)),
-        ],
-        [
-            smem(lengths.shape, jnp.int32),
-            smem((slots,), jnp.int32),
-            smem((slots,), jnp.int32),
-            vmem((rows * stride, HDIM), jnp.float32),
-            vmem((rows * stride, HDIM), jnp.float32),
-            dma((4,)),
-        ],
-        limit=16,
-        cost=pl.CostEstimate(
-            flops=4 * slots * rows * WIN * HDIM, bytes_accessed=24 * MIB, transcendentals=0
-        ),
+        [(vmem, f32(rows * stride, HDIM))] * 3 + [(vmem, bf16(depth, half))],
+        [dma((1,))],
+        cost=half_cost,
+    )
+    answers = call(
+        functools.partial(answer_kernel, ops, asked, steps),
+        [(vmem, attn), (smem, table)]
+        + [(vmem, question) for question in asking]
+        + [(vmem, sends[i]) for i in asked],
+        [(vmem, bf16(2 * rows, HDIM))] * len(asked),
+    )
+    for i, answer in zip(asked, answers):
+        blocks[i] = exchange(i, answer)
+    attn, late, own_w = call(
+        functools.partial(short_kernel, stride, 8),
+        [
+            (vmem, answers[0]),
+            (smem, lists),
+            (vmem, spread),
+            (vmem, pool),
+            (vmem, fresh),
+            (hbm, out_weight),
+            (vmem, recent),
+            (vmem, attn),
+            (vmem, late),
+        ],
+        [(vmem, f32(rows * stride, HDIM))] * 2 + [(vmem, bf16(depth, half))],
+        [dma((1,))],
+        cost=half_cost,
+        aliases={7: 0, 8: 1},
     )
 
     found, sent = call(
-        functools.partial(move_kernel, ops, steps, slots, 4),
-        [(smem, table), (vmem, own_q), (vmem, peer_q), (vmem, fresh)]
+        functools.partial(move_kernel, ops, asked, steps, slots, 4),
+        [(vmem, own_w), (smem, table), (vmem, own_q), (vmem, peer_q), (vmem, fresh)]
         + [(vmem, block) for block in blocks],
         [(vmem, f32(ops, rows, HDIM)), (vmem, bf16(ops - 1, rows, HDIM))],
     )

time: 24.8 us -> 26.3 us (1.060)
  starting transfers between devices: 7.72 us -> 11.2 us
  waiting for transfers between devices: 7.21 us -> 3.87 us
  Pallas kernels: 9.57 us -> 10.9 us
    ppermute x4 -> x5, waiting for transfers between devices: 5.23 us -> 1.03 us  [exchange(): return lax.ppermute(array, ('inst', 'tp'), pairs)]
    ppermute x4 -> x5, starting transfers between devices: 7.42 us -> 10.6 us  [exchange(): return lax.ppermute(array, ('inst', 'tp'), pairs)]
    pallas_call x6 -> x9, Pallas kernels: 9.57 us -> 10.9 us  [call(): pl.pallas_call(kernel, out_shape=[space(shape.shape, shape.dtype) for spa...]
    ppermute x1, waiting for transfers between devices: 0.01 us -> 1.21 us  [body(): peer_q = lax.ppermute(sent_q, 'tp', swap)]
  transfers between devices with their start and end apart: 7 -> 8, of which waited for: 3 -> 4; matrix products, arithmetic and copies ran while one was open for 0% -> 0% of each run, Pallas kernels for 21% -> 25%
where the time goes in v6:
time: 26.3 us; the launch traced here: 26.1 us
  starting transfers between devices  11.2 us (43%)
  Pallas kernels  10.9 us (41%)
  waiting for transfers between devices  3.87 us (15%)
    pallas_call x9, Pallas kernels, call(): pl.pallas_call(kernel, out_shape=[space(shape.shape, shape.dtype) for spa...  10.9 us
    ppermute x5, starting transfers between devices, exchange(): return lax.ppermute(array, ('inst', 'tp'), pairs)  10.6 us
    ppermute x1, waiting for transfers between devices, body(): peer_q = lax.ppermute(sent_q, 'tp', swap)  1.21 us
    ppermute x5, waiting for transfers between devices, exchange(): return lax.ppermute(array, ('inst', 'tp'), pairs)  1.03 us
    ppermute x1, waiting for transfers between devices, body(): arrived = lax.ppermute(sent, 'tp', swap)  0.96 us
    ppermute x1, waiting for transfers between devices, body(): others = lax.ppermute(partial, 'tp', swap)  0.68 us
  transfers between devices with their start and end apart: 8, of which 4 were waited for; matrix products, arithmetic and copies ran while one was open for 0% of the time, Pallas kernels for 25%

profile of v6, /device:TPU:0, one launch (start us, length us, event | category | flops | bytes accessed | tf_op | source)
XLA Modules:
  0.0 26.1 jit_solution(7683783530529317596)
XLA Ops:
  0.0 2.1 %shard_map.64 = (s32[3,8]{1,0:T(4,128)S(4)}, s32[2,32]{1,0:T(2,128)S(4)}, bf16[6144,256]{1,0:T(8,128)(2,1)S(1)}, f32[1920,128]{1,0:T(8,128)S(1)}, bf16[128,256]{...) custom-call(s32[8,32]{1,0:T(8,128)} %anchor_h.1, ...), custom_call_target="tpu_custom_call" | custom-call | tf_op jit(solution)/shard_map/pallas_call | solution.py:316
  2.1 5.1 %collective-permute-start.2 = (bf16[256,256]{1,0:T(8,128)(2,1)S(1)}, bf16[256,256]{1,0:T(8,128)(2,1)S(1)}, u32[]{:S(2)}, u32[]{:S(2)}) collective-permute-start(bf16[256,256]{1,0:T(8,128)(2,1)S(1)} %get-tuple-element.41), channel_id=1, source_target_pairs={{0,12},{1,15},{2,14},{3,13},{4,8},{5,11},{6,10},{7,9},{8,4},{9,7},... | collective-permute-start | bytes 393224 | tf_op jit(solution)/shard_map/ppermute | solution.py:389
  7.3 0.0 collective-permute-start.4
  7.3 1.5 %collective-permute-start.5 = (bf16[256,256]{1,0:T(8,128)(2,1)S(1)}, bf16[256,256]{1,0:T(8,128)(2,1)S(1)}, u32[]{:S(2)}, u32[]{:S(2)}) collective-permute-start(bf16[256,256]{1,0:T(8,128)(2,1)S(1)} %get-tuple-element.43), channel_id=1, source_target_pairs={{0,2},{1,3},{2,0},{3,1},{4,6},{5,7},{6,4},{7,5},{8,10},{9,11},{10,... | collective-permute-start | bytes 393224 | tf_op jit(solution)/shard_map/ppermute | solution.py:389
  8.8 0.0 collective-permute-start
  8.8 1.2 %collective-permute-done.peer_q = bf16[3,48,128]{2,1,0:T(8,128)(2,1)S(1)} collective-permute-done((bf16[3,48,128]{2,1,0:T(8,128)(2,1)S(1)}, bf16[3,48,128]{2,1,0:T(8,128)(2,1)S(1)}, u32[]{:S(2)}, u32[]{:S(2)}) %collective-permute-start) | collective-permute-done | bytes 36896 | tf_op jit(solution)/shard_map/ppermute | solution.py:381
  10.0 0.8 %collective-permute-start.1 = (bf16[128,128]{1,0:T(8,128)(2,1)S(1)}, bf16[128,128]{1,0:T(8,128)(2,1)S(1)}, u32[]{:S(2)}, u32[]{:S(2)}) collective-permute-start(bf16[128,128]{1,0:T(8,128)(2,1)S(1)} %shard_map.65.after), channel_id=1, source_target_pairs={{0,8},{1,11},{2,10},{3,9},{4,12},{5,15},{6,14},{7,13},{8,0},{9,3},... | collective-permute-start | bytes 98312 | tf_op jit(solution)/shard_map/ppermute | solution.py:389
  10.8 3.0 %shard_map.66 = (f32[1920,128]{1,0:T(8,128)S(1)}, f32[1920,128]{1,0:T(8,128)S(1)}, f32[1920,128]{1,0:T(8,128)S(1)}, bf16[1536,1536]{1,0:T(8,128)(2,1)S(1)}) custom-call(bf16[128,128]{1,0:T(8,128)(2,1)S(1)} %shard_map.65.after, s32[2,32]{1,0:T(2,128)S(4)} %get-tuple-element.31.lists, f32[1920,128]{1,0:T(8,128)S(1)} %get-tuple-element.32.spread, ...), custom_call_target="tpu_custom_call" | custom-call | flops 100663296 | bytes 10485760 | tf_op jit(solution)/shard_map/pallas_call | solution.py:316
  13.8 1.0 %collective-permute-done.1.refs_0_ = bf16[128,128]{1,0:T(8,128)(2,1)S(1)} collective-permute-done((bf16[128,128]{1,0:T(8,128)(2,1)S(1)}, bf16[128,128]{1,0:T(8,128)(2,1)S(1)}, u32[]{:S(2)}, u32[]{:S(2)}) %collective-permute-start.1) | collective-permute-done | bytes 32800 | tf_op jit(solution)/shard_map/ppermute | solution.py:389
  14.8 0.5 %shard_map.67.after = bf16[96,128]{1,0:T(8,128)(2,1)S(1)} custom-call(f32[1920,128]{1,0:T(8,128)S(1)} %get-tuple-element.35.after.attn_in, s32[3,8]{1,0:T(4,128)S(4)} %get-tuple-element.27.table, bf16[128,128]{1,0:T(8,128)(2,1)S(1)} %collective-permute-done.1.refs_0_, bf16[256,256]{1,0:T(8,128)(2,1)S(1)} %get-tuple-element.36.refs_1_), custom_call_target="tpu_custom_call" | custom-call | tf_op jit(solution)/shard_map/pallas_call | solution.py:316
  15.3 3.2 %collective-permute-start.3 = (bf16[96,128]{1,0:T(8,128)(2,1)S(1)}, bf16[96,128]{1,0:T(8,128)(2,1)S(1)}, u32[]{:S(2)}, u32[]{:S(2)}) collective-permute-start(bf16[96,128]{1,0:T(8,128)(2,1)S(1)} %shard_map.67.after), channel_id=1, source_target_pairs={{0,8},{1,11},{2,10},{3,9},{4,12},{5,15},{6,14},{7,13},{8,0},{9,3},... | collective-permute-start | bytes 73736 | tf_op jit(solution)/shard_map/ppermute | solution.py:389
  18.4 2.3 %shard_map.68 = (f32[1920,128]{1,0:T(8,128)S(1)}, f32[1920,128]{1,0:T(8,128)S(1)}, bf16[1536,1536]{1,0:T(8,128)(2,1)S(1)}) custom-call(bf16[96,128]{1,0:T(8,128)(2,1)S(1)} %shard_map.67.after, s32[2,32]{1,0:T(2,128)S(4)} %get-tuple-element.31.lists, f32[1920,128]{1,0:T(8,128)S(1)} %get-tuple-element.32.spread, ...), custom_call_target="tpu_custom_call", output_to_operand_aliasing={{0}: (7, {}), {1}: (8, {})} | custom-call | flops 100663296 | bytes 10485760 | tf_op jit(solution)/shard_map/pallas_call | solution.py:316
  20.8 0.0 collective-permute-done.3.refs_1_
  20.8 0.0 collective-permute-done.2.refs_0_
  20.8 0.0 collective-permute-done.4.refs_2_
  20.8 0.0 collective-permute-done.5.refs_3_
  20.8 0.5 %shard_map.69 = (f32[4,48,128]{2,1,0:T(8,128)S(1)}, bf16[3,48,128]{2,1,0:T(8,128)(2,1)S(1)}) custom-call(bf16[1536,1536]{1,0:T(8,128)(2,1)S(1)} %get-tuple-element.40.after.weight, s32[3,8]{1,0:T(4,128)S(4)} %get-tuple-element.27.table, bf16[4,48,128]{2,1,0:T(8,128)(2,1)S(1)} %get-tuple-element.28.own_q, ...), custom_call_target="tpu_custom_call" | custom-call | tf_op jit(solution)/shard_map/pallas_call | solution.py:316
  21.4 0.3 %collective-permute-start.6 = (bf16[3,48,128]{2,1,0:T(8,128)(2,1)S(1)}, bf16[3,48,128]{2,1,0:T(8,128)(2,1)S(1)}, u32[]{:S(2)}, u32[]{:S(2)}) collective-permute-start(bf16[3,48,128]{2,1,0:T(8,128)(2,1)S(1)} %get-tuple-element.45), channel_id=1, source_target_pairs={{0,1},{1,0},{2,3},{3,2},{4,5},{5,4},{6,7},{7,6},{8,9},{9,8},{10,11... | collective-permute-start | bytes 110600 | tf_op jit(solution)/shard_map/ppermute | solution.py:452
  21.7 1.0 %collective-permute-done.6.arrived = bf16[3,48,128]{2,1,0:T(8,128)(2,1)S(1)} collective-permute-done((bf16[3,48,128]{2,1,0:T(8,128)(2,1)S(1)}, bf16[3,48,128]{2,1,0:T(8,128)(2,1)S(1)}, u32[]{:S(2)}, u32[]{:S(2)}) %collective-permute-start.6) | collective-permute-done | bytes 36896 | tf_op jit(solution)/shard_map/ppermute | solution.py:452
  22.7 0.9 %shard_map.70 = (bf16[128,1536]{1,0:T(8,128)(2,1)S(1)}, bf16[128,1536]{1,0:T(8,128)(2,1)S(1)}, f32[1920,128]{1,0:T(8,128)S(1)}) custom-call(s32[3,8]{1,0:T(4,128)S(4)} %get-tuple-element.27.table, f32[1920,128]{1,0:T(8,128)S(1)} %get-tuple-element.39.attn, f32[4,48,128]{2,1,0:T(8,128)S(1)} %get-tuple-element.44.found, ...), custom_call_target="tpu_custom_call", output_to_operand_aliasing={{2}: (1, {})} | custom-call | tf_op jit(solution)/shard_map/pallas_call | solution.py:316
  23.5 0.3 %collective-permute-start.7 = (bf16[128,1536]{1,0:T(8,128)(2,1)S(1)}, bf16[128,1536]{1,0:T(8,128)(2,1)S(1)}, u32[]{:S(2)}, u32[]{:S(2)}) collective-permute-start(bf16[128,1536]{1,0:T(8,128)(2,1)S(1)} %get-tuple-element.48), channel_id=1, source_target_pairs={{0,1},{1,0},{2,3},{3,2},{4,5},{5,4},{6,7},{7,6},{8,9},{9,8},{10,11... | collective-permute-start | bytes 1179656 | tf_op jit(solution)/shard_map/ppermute | solution.py:464
  23.9 0.8 %shard_map.71.own = f32[128,1536]{1,0:T(8,128)S(1)} custom-call(bf16[128,1536]{1,0:T(8,128)(2,1)S(1)} %get-tuple-element.47.lhs, bf16[1536,1536]{1,0:T(8,128)(2,1)S(1)} %get-tuple-element.40.after.weight), custom_call_target="tpu_custom_call" | custom-call | flops 603979776 | bytes 6291456 | tf_op jit(solution)/shard_map/pallas_call | solution.py:316
  24.7 0.7 %collective-permute-done.7.others = bf16[128,1536]{1,0:T(8,128)(2,1)S(1)} collective-permute-done((bf16[128,1536]{1,0:T(8,128)(2,1)S(1)}, bf16[128,1536]{1,0:T(8,128)(2,1)S(1)}, u32[]{:S(2)}, u32[]{:S(2)}) %collective-permute-start.7) | collective-permute-done | bytes 393248 | tf_op jit(solution)/shard_map/ppermute | solution.py:464
  25.3 0.8 %shard_map.72 = bf16[128,1536]{1,0:T(8,128)(2,1)} custom-call(f32[128,1536]{1,0:T(8,128)S(1)} %shard_map.71.own, bf16[128,1536]{1,0:T(8,128)(2,1)S(1)} %collective-permute-done.7.others), custom_call_target="tpu_custom_call" | custom-call | tf_op jit(solution)/shard_map/pallas_call | solution.py:316
  (1 shorter events, 0.0 us)
Async XLA Ops:
  2.1 18.7 %collective-permute-start.2 = (bf16[256,256]{1,0:T(8,128)(2,1)S(1)}, bf16[256,256]{1,0:T(8,128)(2,1)S(1)}, u32[]{:S(2)}, u32[]{:S(2)}) collective-permute-start(bf16[256,256]{1,0:T(8,128)(2,1)S(1)} %get-tuple-element.41), channel_id=1, source_target_pairs={{0,12},{1,15},{2,14},{3,13},{4,8},{5,11},{6,10},{7,9},{8,4},{9,7},... | collective-permute-start | bytes 393224 | tf_op jit(solution)/shard_map/ppermute | solution.py:389
  7.3 13.6 %collective-permute-start.4 = (bf16[256,256]{1,0:T(8,128)(2,1)S(1)}, bf16[256,256]{1,0:T(8,128)(2,1)S(1)}, u32[]{:S(2)}, u32[]{:S(2)}) collective-permute-start(bf16[256,256]{1,0:T(8,128)(2,1)S(1)} %get-tuple-element.42), channel_id=1, source_target_pairs={{0,4},{1,7},{2,6},{3,5},{4,0},{5,3},{6,2},{7,1},{8,12},{9,15},{10,... | collective-permute-start | bytes 393224 | tf_op jit(solution)/shard_map/ppermute | solution.py:389
  7.3 13.6 %collective-permute-start.5 = (bf16[256,256]{1,0:T(8,128)(2,1)S(1)}, bf16[256,256]{1,0:T(8,128)(2,1)S(1)}, u32[]{:S(2)}, u32[]{:S(2)}) collective-permute-start(bf16[256,256]{1,0:T(8,128)(2,1)S(1)} %get-tuple-element.43), channel_id=1, source_target_pairs={{0,2},{1,3},{2,0},{3,1},{4,6},{5,7},{6,4},{7,5},{8,10},{9,11},{10,... | collective-permute-start | bytes 393224 | tf_op jit(solution)/shard_map/ppermute | solution.py:389
  8.8 1.2 %collective-permute-start = (bf16[3,48,128]{2,1,0:T(8,128)(2,1)S(1)}, bf16[3,48,128]{2,1,0:T(8,128)(2,1)S(1)}, u32[]{:S(2)}, u32[]{:S(2)}) collective-permute-start(bf16[3,48,128]{2,1,0:T(8,128)(2,1)S(1)} %get-tuple-element.29), channel_id=1, source_target_pairs={{0,1},{1,0},{2,3},{3,2},{4,5},{5,4},{6,7},{7,6},{8,9},{9,8},{10,11... | collective-permute-start | bytes 110600 | tf_op jit(solution)/shard_map/ppermute | solution.py:381
  10.0 4.8 %collective-permute-start.1 = (bf16[128,128]{1,0:T(8,128)(2,1)S(1)}, bf16[128,128]{1,0:T(8,128)(2,1)S(1)}, u32[]{:S(2)}, u32[]{:S(2)}) collective-permute-start(bf16[128,128]{1,0:T(8,128)(2,1)S(1)} %shard_map.65.after), channel_id=1, source_target_pairs={{0,8},{1,11},{2,10},{3,9},{4,12},{5,15},{6,14},{7,13},{8,0},{9,3},... | collective-permute-start | bytes 98312 | tf_op jit(solution)/shard_map/ppermute | solution.py:389
  15.3 5.5 %collective-permute-start.3 = (bf16[96,128]{1,0:T(8,128)(2,1)S(1)}, bf16[96,128]{1,0:T(8,128)(2,1)S(1)}, u32[]{:S(2)}, u32[]{:S(2)}) collective-permute-start(bf16[96,128]{1,0:T(8,128)(2,1)S(1)} %shard_map.67.after), channel_id=1, source_target_pairs={{0,8},{1,11},{2,10},{3,9},{4,12},{5,15},{6,14},{7,13},{8,0},{9,3},... | collective-permute-start | bytes 73736 | tf_op jit(solution)/shard_map/ppermute | solution.py:389
  21.4 1.3 %collective-permute-start.6 = (bf16[3,48,128]{2,1,0:T(8,128)(2,1)S(1)}, bf16[3,48,128]{2,1,0:T(8,128)(2,1)S(1)}, u32[]{:S(2)}, u32[]{:S(2)}) collective-permute-start(bf16[3,48,128]{2,1,0:T(8,128)(2,1)S(1)} %get-tuple-element.45), channel_id=1, source_target_pairs={{0,1},{1,0},{2,3},{3,2},{4,5},{5,4},{6,7},{7,6},{8,9},{9,8},{10,11... | collective-permute-start | bytes 110600 | tf_op jit(solution)/shard_map/ppermute | solution.py:452
  23.5 1.8 %collective-permute-start.7 = (bf16[128,1536]{1,0:T(8,128)(2,1)S(1)}, bf16[128,1536]{1,0:T(8,128)(2,1)S(1)}, u32[]{:S(2)}, u32[]{:S(2)}) collective-permute-start(bf16[128,1536]{1,0:T(8,128)(2,1)S(1)} %get-tuple-element.48), channel_id=1, source_target_pairs={{0,1},{1,0},{2,3},{3,2},{4,5},{5,4},{6,7},{7,6},{8,9},{9,8},{10,11... | collective-permute-start | bytes 1179656 | tf_op jit(solution)/shard_map/ppermute | solution.py:464

commit v7 on v5

v7 whole, which is shorter than its diff:
```python
import functools
import math

import jax
import jax.numpy as jnp
from jax import lax
from jax.experimental import pallas as pl
from jax.experimental.pallas import tpu as pltpu
from jax.sharding import PartitionSpec as P

HDIM = 128
BLK = 128
MAXB = 2
WIN = MAXB * BLK
PAD = 8
MIB = 1024 * 1024


def partner(insts, ops, i, core):
    return jnp.int32(1) if i == ops - 1 else insts - 2 - 2 * i + core


def start_copies(pairs, sems):
    copies = [pltpu.make_async_copy(a, b, sems.at[n]) for n, (a, b) in enumerate(pairs)]
    for copy in copies:
        copy.start()
    return copies


def plan_kernel(
    ops, stride, anchor_h, lengths_h, queries_h, fresh_h, pool_h,
    table, lists, pool, spread, fresh, own_q, sent_q, *refs,
):
    sends, (anchor, lengths, offs, queries, sems) = refs[:ops], refs[ops:]
    insts, slots = anchor.shape
    steps, _, width = queries.shape
    heads = width // HDIM
    rows = steps * heads
    blocks = pool.shape[0] // BLK
    own, core = lax.axis_index("inst"), lax.axis_index("tp")
    loads = start_copies(
        [
            (anchor_h, anchor),
            (lengths_h, lengths),
            (queries_h, queries),
            (fresh_h, fresh),
            (pool_h, pool),
        ],
        sems,
    )
    loads[0].wait()
    loads[1].wait()
    for m in range(insts):
        table[0, m] = slots
        table[1, m] = 1
        offs[m] = 0
    longer = blocks - slots
    start, found = jnp.int32(0), jnp.int32(0)
    for j in range(slots):
        source, count = anchor[own, j], lengths[own, j]
        dest = (2 * own - source) & (insts - 1)
        table[0, own ^ source] = j
        table[1, own ^ source] = lengths[source, j]
        offs[own ^ dest] = start
        place = jnp.where(count > 1, found, longer + j - found)
        lists[0, place] = j
        lists[1, place] = start
        start = start + count
        found = found + count - 1
    loads[2].wait()
    for s in range(steps):
        for h in range(heads):
            spread[pl.ds((s * heads + h) * stride, slots), :] = queries[
                s, :, h * HDIM : (h + 1) * HDIM
            ].astype(jnp.float32)
    for i in range(ops):
        j = table[0, partner(insts, ops, i, core)]
        own_q[i] = spread[pl.ds(j, rows, stride=stride), :].astype(jnp.bfloat16)
    for i in range(ops - 1):
        j = table[0, partner(insts, ops, i, 1 - core)]
        sent_q[i] = spread[pl.ds(j, rows, stride=stride), :].astype(jnp.bfloat16)
    loads[3].wait()
    loads[4].wait()
    for i in range(ops):
        at = offs[partner(insts, ops, i, core)]
        for b in range(MAXB):
            row = pl.multiple_of(jnp.minimum(at + b, blocks - 1) * BLK, BLK)
            sends[i][b * BLK : (b + 1) * BLK, :] = pool[pl.ds(row, BLK), :]


def contract_last(a, b):
    return lax.dot_general(a, b, (((1,), (1,)), ((), ())), preferred_element_type=jnp.float32)


def widest(score):
    return functools.reduce(
        jnp.maximum, [score[:, k : k + HDIM] for k in range(0, score.shape[1], HDIM)]
    )


def attend_all(scores, recents, values):
    scale = math.log2(math.e) / math.sqrt(HDIM)
    weights = []
    for score, recent in zip(scores, recents):
        top = jnp.max(jnp.maximum(widest(score), recent), axis=1, keepdims=True)
        cached = jnp.exp2((score - top) * scale)
        late = jnp.exp2((recent - top) * scale)
        folded = sum([cached[:, k : k + HDIM] for k in range(0, cached.shape[1], HDIM)], late)
        share = 1.0 / jnp.sum(folded, axis=1, keepdims=True)
        weights.append((cached.astype(jnp.bfloat16), late * share, share))
    return [
        (jnp.dot(cached, value, preferred_element_type=jnp.float32) * share, late)
        for (cached, late, share), value in zip(weights, values)
    ]


def stay_requests(stride, rows, group, first, count, size, lists, spread, pool, recent, attn, late):
    group = math.gcd(group, count)

    def some(g, _):
        places = [first + g * group + u for u in range(group)]
        picked = [pl.ds(lists[0, at], rows, stride=stride) for at in places]
        windows = [pl.ds(pl.multiple_of(lists[1, at] * BLK, BLK), size) for at in places]
        queries = [spread[at, :].astype(jnp.bfloat16) for at in picked]
        recents = [recent[at, :] for at in picked]
        scores = [contract_last(q, pool[w, :HDIM]) for q, w in zip(queries, windows)]
        done = attend_all(scores, recents, [pool[w, HDIM:] for w in windows])
        for at, (mixed, weight) in zip(picked, done):
            attn[at, :] = mixed
            late[at, :] = weight
        return 0

    lax.fori_loop(0, count // group, some, 0)


def stay_kernel(
    stride, steps, group, lists, spread, pool, fresh, weight_h,
    attn, peer_w, own_w, recent, late, sems,
):
    slots = lists.shape[1]
    rows = spread.shape[0] // stride
    heads = rows // steps
    half = peer_w.shape[1]
    core = lax.axis_index("tp")
    own_cols = pl.ds(pl.multiple_of(core * half, HDIM), half)
    peer_cols = pl.ds(pl.multiple_of((1 - core) * half, HDIM), half)
    loads = start_copies(
        [(weight_h.at[:, peer_cols], peer_w), (weight_h.at[:, own_cols], own_w)], sems
    )
    slot = lax.broadcasted_iota(jnp.int32, (slots, steps * slots), 0)
    col = lax.broadcasted_iota(jnp.int32, (slots, steps * slots), 1)
    for i in range(rows):
        at = pl.ds(i * stride, slots)
        score = contract_last(spread[at, :].astype(jnp.bfloat16), fresh[:, :HDIM])
        mine = (col % slots == slot) & (col // slots <= i // heads)
        recent[at, :] = jnp.where(mine, score, -jnp.inf)
    longer = pool.shape[0] // BLK - slots
    state = (lists, spread, pool, recent, attn, late)
    stay_requests(stride, rows, group, 0, longer, WIN, *state)
    stay_requests(stride, rows, group, longer, slots - longer, BLK, *state)
    for i in range(rows):
        at = pl.ds(i * stride, slots)
        attn[at, :] = attn[at, :] + jnp.dot(
            late[at, :].astype(jnp.bfloat16), fresh[:, HDIM:], preferred_element_type=jnp.float32
        )
    for load in loads:
        load.wait()


def move_kernel(ops, steps, slots, through, table, own_q, peer_q, fresh, *refs):
    blocks, (found, sent, _) = refs[:ops], refs[ops:]
    rows = own_q.shape[1]
    heads = rows // steps
    insts = table.shape[1]
    core = lax.axis_index("tp")
    shape = (2 * rows, steps * slots)
    step = lax.broadcasted_iota(jnp.int32, shape, 0) // heads % steps
    col = lax.broadcasted_iota(jnp.int32, shape, 1)
    owner = jnp.where(col // slots <= step, col % slots, -1)
    within = lax.broadcasted_iota(jnp.int32, (2 * rows, WIN), 1)
    for first in range(0, ops, 4):
        batch = range(first, min(first + 4, ops))
        scores, recents = [], []
        for i in batch:
            query = own_q[i]
            if i < ops - 1:
                query = jnp.concatenate([query, peer_q[i]])
            m = partner(insts, ops, i, core)
            score = contract_last(query, blocks[i][:, :HDIM])
            fits = within[: query.shape[0]] < table[1, m] * BLK
            scores.append(jnp.where(fits, score, -jnp.inf))
            recent = contract_last(query, fresh[:, :HDIM])
            recents.append(jnp.where(owner[: query.shape[0]] == table[0, m], recent, -jnp.inf))
        done = attend_all(scores, recents, [blocks[i][:, HDIM:] for i in batch])
        for i, (mixed, weight) in zip(batch, done):
            out = mixed + jnp.dot(
                weight.astype(jnp.bfloat16), fresh[:, HDIM:], preferred_element_type=jnp.float32
            )
            found[i] = out[:rows].astype(jnp.bfloat16)
            if i < ops - 1:
                sent[i] = out[rows:].astype(jnp.bfloat16)


def dot_tiles(lhs, weight, out):
    tile = math.gcd(WIN, out.shape[1])
    for n in range(0, out.shape[1], tile):
        out[:, n : n + tile] = jnp.dot(
            lhs[...], weight[:, n : n + tile], preferred_element_type=jnp.float32
        ).astype(out.dtype)


def base_kernel(ops, stride, table, attn, peer_w, own_w, partial, own, spot, lhs):
    insts = table.shape[1]
    slots = stride - PAD
    steps = lhs.shape[0] // slots
    rows = attn.shape[0] // stride
    heads = rows // steps
    width = spot.shape[1]
    slot = lax.broadcasted_iota(jnp.int32, (slots, HDIM), 0)
    stays = slot >= 0
    row = lax.broadcasted_iota(jnp.int32, spot.shape, 0)
    col = lax.broadcasted_iota(jnp.int32, spot.shape, 1)
    goes = row < 0
    for n in range(2 * ops - 1):
        m = table_place(insts, ops, n)
        j = table[0, m]
        stays = stays & (slot != j)
        goes = goes | ((col % (2 * ops) == n) & (row % slots == j))
    goes = goes & (col // (2 * ops) == row // slots)
    spot[...] = jnp.where(goes, 1.0, 0.0).astype(jnp.bfloat16)
    for s in range(steps):
        for h in range(heads):
            value = attn[pl.ds((s * heads + h) * stride, slots), :]
            lhs[s * slots : (s + 1) * slots, h * HDIM : (h + 1) * HDIM] = jnp.where(
                stays, value, 0.0
            ).astype(jnp.bfloat16)
    dot_tiles(lhs, peer_w, partial)
    dot_tiles(lhs, own_w, own)


def table_place(insts, ops, n):
    return 1 if n // 2 == ops - 1 else insts - 2 - 2 * (n // 2) + n % 2


def project_kernel(ops, steps, weight, found, arrived, partial, lhs, spread):
    rows = found.shape[1]
    heads = rows // steps
    stride = 2 * ops
    core = lax.axis_index("tp")
    spread[pl.ds(stride - 1, rows, stride=stride), :] = jnp.zeros((rows, HDIM), jnp.float32)
    for i in range(ops):
        at = stride - 2 if i == ops - 1 else 2 * i + core
        spread[pl.ds(at, rows, stride=stride), :] = found[i].astype(jnp.float32)
    for i in range(ops - 1):
        at = 2 * i + 1 - core
        spread[pl.ds(at, rows, stride=stride), :] = arrived[i].astype(jnp.float32)
    for s in range(0, steps, 2):
        for h in range(heads):
            both = [
                spread[pl.ds(((s + t) * heads + h) * stride, stride), :] for t in range(2)
            ]
            lhs[s * stride : (s + 2) * stride, h * HDIM : (h + 1) * HDIM] = jnp.concatenate(
                both
            ).astype(jnp.bfloat16)
    dot_tiles(lhs, weight, partial)


def own_kernel(lhs, weight, out):
    dot_tiles(lhs, weight, out)


def final_kernel(chunks, spot, own, others, own_m, others_m, out_h, out, sems):
    moved = (own_m[...] + others_m[...].astype(jnp.float32)).astype(jnp.bfloat16)
    part = out.shape[0] // chunks
    copies = []
    for n in range(chunks):
        at = pl.ds(n * part, part)
        placed = jnp.dot(spot[at, :], moved, preferred_element_type=jnp.float32)
        out[at, :] = (own[at, :] + others[at, :].astype(jnp.float32) + placed).astype(jnp.bfloat16)
        copies.append(pltpu.make_async_copy(out.at[at], out_h.at[at], sems.at[n]))
        copies[-1].start()
    for copy in copies:
        copy.wait()


def call(kernel, operands, outs, scratch=(), limit=8, cost=None, aliases=None):
    specs = [pl.BlockSpec(memory_space=space) for space, _ in operands]
    return pl.pallas_call(
        kernel,
        out_shape=[space(shape.shape, shape.dtype) for space, shape in outs],
        in_specs=specs,
        out_specs=[pl.BlockSpec(memory_space=space) for space, _ in outs],
        scratch_shapes=list(scratch),
        compiler_params=pltpu.CompilerParams(vmem_limit_bytes=limit * MIB),
        cost_estimate=cost,
        input_output_aliases=aliases or {},
    )(*[pltpu.with_memory_space_constraint(array, space) for space, array in operands])


def body(queries, new_kv, cache_pool, lengths, anchor, out_weight):
    steps, slots, width = queries.shape
    heads = width // HDIM
    rows = steps * heads
    insts = lax.axis_size("inst")
    cores = lax.axis_size("tp")
    kvw = cache_pool.shape[1]
    depth, columns = out_weight.shape
    half = columns // cores
    ops = insts // 2
    stride = slots + PAD
    hbm, vmem, smem = pltpu.HBM, pltpu.VMEM, pltpu.SMEM
    dma = pltpu.SemaphoreType.DMA

    def bf16(*shape):
        return jax.ShapeDtypeStruct(shape, jnp.bfloat16)

    def f32(*shape):
        return jax.ShapeDtypeStruct(shape, jnp.float32)

    table, lists, pool, spread, fresh, own_q, sent_q, *sends = call(
        functools.partial(plan_kernel, ops, stride),
        [
            (hbm, anchor),
            (hbm, lengths),
            (hbm, queries),
            (hbm, new_kv.reshape(steps * slots, kvw)),
            (hbm, cache_pool),
        ],
        [
            (smem, jax.ShapeDtypeStruct((2, insts), jnp.int32)),
            (smem, jax.ShapeDtypeStruct((2, slots), jnp.int32)),
            (vmem, bf16(*cache_pool.shape)),
            (vmem, f32(rows * stride, HDIM)),
            (vmem, bf16(steps * slots, kvw)),
            (vmem, bf16(ops, rows, HDIM)),
            (vmem, bf16(ops - 1, rows, HDIM)),
        ]
        + [(vmem, bf16(WIN, kvw))] * ops,
        [
            smem(anchor.shape, jnp.int32),
            smem(lengths.shape, jnp.int32),
            smem((insts,), jnp.int32),
            vmem(queries.shape, jnp.bfloat16),
            dma((5,)),
        ],
    )
    swap = [(c, cores - 1 - c) for c in range(cores)]
    peer_q = lax.ppermute(sent_q, "tp", swap)

    blocks = [None] * ops
    for i in reversed(range(ops)):
        pairs = []
        for a in range(insts):
            for c in range(cores):
                pairs.append((a * cores + c, (a ^ table_place(insts, ops, 2 * i + c)) * cores + c))
        blocks[i] = lax.ppermute(sends[i], ("inst", "tp"), pairs)

    attn, peer_w, own_w = call(
        functools.partial(stay_kernel, stride, steps, 8),
        [
            (smem, lists),
            (vmem, spread),
            (vmem, pool),
            (vmem, fresh),
            (hbm, out_weight),
        ],
        [(vmem, f32(rows * stride, HDIM))] + [(vmem, bf16(depth, half))] * 2,
        [
            vmem((rows * stride, HDIM), jnp.float32),
            vmem((rows * stride, HDIM), jnp.float32),
            dma((2,)),
        ],
        cost=pl.CostEstimate(
            flops=4 * slots * rows * WIN * HDIM, bytes_accessed=20 * MIB, transcendentals=0
        ),
    )
    tokens = steps * slots
    partial, own, spot = call(
        functools.partial(base_kernel, ops, stride),
        [(smem, table), (vmem, attn), (vmem, peer_w), (vmem, own_w)],
        [(vmem, bf16(tokens, half)), (vmem, f32(tokens, half)), (vmem, bf16(tokens, 2 * ops * steps))],
        [vmem((tokens, width), jnp.bfloat16)],
        cost=pl.CostEstimate(
            flops=4 * tokens * width * half, bytes_accessed=10 * MIB, transcendentals=0
        ),
    )

    found, sent, partial = call(
        functools.partial(move_kernel, ops, steps, slots),
        [(vmem, partial), (smem, table), (vmem, own_q), (vmem, peer_q), (vmem, fresh)]
        + [(vmem, block) for block in blocks],
        [
            (vmem, bf16(ops, rows, HDIM)),
            (vmem, bf16(ops - 1, rows, HDIM)),
            (vmem, bf16(tokens, half)),
        ],
        aliases={0: 2},
    )
    others = lax.ppermute(partial, "tp", swap)
    arrived = lax.ppermute(sent, "tp", swap)
    moved = 2 * ops * steps
    partial_m, lhs_m = call(
        functools.partial(project_kernel, ops, steps),
        [(vmem, peer_w), (vmem, found), (vmem, arrived)],
        [(vmem, bf16(moved, half)), (vmem, bf16(moved, width))],
        [vmem((2 * ops * rows, HDIM), jnp.float32)],
    )
    others_m = lax.ppermute(partial_m, "tp", swap)
    (own_m,) = call(
        own_kernel,
        [(vmem, lhs_m), (vmem, own_w)],
        [(vmem, f32(moved, half))],
        cost=pl.CostEstimate(
            flops=2 * moved * width * half, bytes_accessed=6 * MIB, transcendentals=0
        ),
    )
    (result,) = call(
        functools.partial(final_kernel, 4),
        [(vmem, spot), (vmem, own), (vmem, others), (vmem, own_m), (vmem, others_m)],
        [(hbm, bf16(tokens, half))],
        [vmem((tokens, half), jnp.bfloat16), dma((4,))],
    )
    return result.reshape(steps, slots, half)


def solution(mesh):
    placed = (
        P(None, ("groups", "inst"), "tp"),
        P(None, ("groups", "inst"), None),
        P(("groups", "inst"), None),
        P("groups", None),
        P("groups", None),
        P("tp", None),
    )
    return jax.shard_map(
        body,
        mesh=mesh,
        in_specs=placed,
        out_specs=P(None, ("groups", "inst"), "tp"),
        check_vma=False,
    )
```

time: 24.8 us -> 25 us (level)
  waiting for transfers between devices: 7.21 us -> 5.73 us
  Pallas kernels: 9.57 us -> 10.8 us
  starting transfers between devices: 7.72 us -> 8.22 us
    pallas_call x6 -> x7, Pallas kernels: 9.57 us -> 10.8 us  [call(): pl.pallas_call(kernel, out_shape=[space(shape.shape, shape.dtype) for spa...]
    ppermute x4, waiting for transfers between devices: 5.23 us -> 4.19 us  [body(): blocks[i] = lax.ppermute(sends[i], ('inst', 'tp'), pairs)]
    ppermute x1, waiting for transfers between devices: 0.78 us -> 0.01 us  [body(): others = lax.ppermute(partial, 'tp', swap)]
    ppermute x1, starting transfers between devices: 0.01 us -> 0.52 us  [body(): peer_q = lax.ppermute(sent_q, 'tp', swap)]
    ppermute x4, starting transfers between devices: 7.42 us -> 6.98 us  [body(): blocks[i] = lax.ppermute(sends[i], ('inst', 'tp'), pairs)]
    ppermute x1, starting transfers between devices: 0.07 us -> 0.5 us  [body(): arrived = lax.ppermute(sent, 'tp', swap)]
    ppermute x0 -> x1, waiting for transfers between devices: none -> 0.27 us  [body(): others_m = lax.ppermute(partial_m, 'tp', swap)]
  transfers between devices with their start and end apart: 7 -> 8, of which waited for: 3 -> 3; matrix products, arithmetic and copies ran while one was open for 0% -> 0% of each run, Pallas kernels for 21% -> 29%
where the time goes in v7:
time: 25 us; the launch traced here: 24.8 us
  Pallas kernels  10.8 us (43%)
  starting transfers between devices  8.22 us (33%)
  waiting for transfers between devices  5.73 us (23%)
    pallas_call x7, Pallas kernels, call(): pl.pallas_call(kernel, out_shape=[space(shape.shape, shape.dtype) for spa...  10.8 us
    ppermute x4, starting transfers between devices, body(): blocks[i] = lax.ppermute(sends[i], ('inst', 'tp'), pairs)  6.98 us
    ppermute x4, waiting for transfers between devices, body(): blocks[i] = lax.ppermute(sends[i], ('inst', 'tp'), pairs)  4.19 us
    ppermute x1, waiting for transfers between devices, body(): arrived = lax.ppermute(sent, 'tp', swap)  1.26 us
    ppermute x1, starting transfers between devices, body(): peer_q = lax.ppermute(sent_q, 'tp', swap)  0.52 us
  transfers between devices with their start and end apart: 8, of which 3 were waited for; matrix products, arithmetic and copies ran while one was open for 0% of the time, Pallas kernels for 29%

profile of v7, /device:TPU:0, one launch (start us, length us, event | category | flops | bytes accessed | tf_op | source)
XLA Modules:
  0.0 24.8 jit_solution(837975184300789103)
XLA Ops:
  0.0 2.1 %shard_map.64 = (s32[2,8]{1,0:T(2,128)S(4)}, s32[2,32]{1,0:T(2,128)S(4)}, bf16[6144,256]{1,0:T(8,128)(2,1)S(1)}, f32[1920,128]{1,0:T(8,128)S(1)}, bf16[128,256]{...) custom-call(s32[8,32]{1,0:T(8,128)} %anchor_h.1, ...), custom_call_target="tpu_custom_call" | custom-call | tf_op jit(solution)/shard_map/pallas_call | solution.py:288
  2.1 0.5 %collective-permute-start = (bf16[3,48,128]{2,1,0:T(8,128)(2,1)S(1)}, bf16[3,48,128]{2,1,0:T(8,128)(2,1)S(1)}, u32[]{:S(2)}, u32[]{:S(2)}) collective-permute-start(bf16[3,48,128]{2,1,0:T(8,128)(2,1)S(1)} %get-tuple-element.39), channel_id=1, source_target_pairs={{0,1},{1,0},{2,3},{3,2},{4,5},{5,4},{6,7},{7,6},{8,9},{9,8},{10,11... | collective-permute-start | bytes 110600 | tf_op jit(solution)/shard_map/ppermute | solution.py:348
  2.7 4.7 %collective-permute-start.1 = (bf16[256,256]{1,0:T(8,128)(2,1)S(1)}, bf16[256,256]{1,0:T(8,128)(2,1)S(1)}, u32[]{:S(2)}, u32[]{:S(2)}) collective-permute-start(bf16[256,256]{1,0:T(8,128)(2,1)S(1)} %get-tuple-element.40), channel_id=1, source_target_pairs={{0,12},{1,15},{2,14},{3,13},{4,8},{5,11},{6,10},{7,9},{8,4},{9,7},... | collective-permute-start | bytes 393224 | tf_op jit(solution)/shard_map/ppermute | solution.py:356
  7.3 0.0 collective-permute-start.2
  7.3 0.6 %collective-permute-start.3 = (bf16[256,256]{1,0:T(8,128)(2,1)S(1)}, bf16[256,256]{1,0:T(8,128)(2,1)S(1)}, u32[]{:S(2)}, u32[]{:S(2)}) collective-permute-start(bf16[256,256]{1,0:T(8,128)(2,1)S(1)} %get-tuple-element.42), channel_id=1, source_target_pairs={{0,4},{1,7},{2,6},{3,5},{4,0},{5,3},{6,2},{7,1},{8,12},{9,15},{10,... | collective-permute-start | bytes 393224 | tf_op jit(solution)/shard_map/ppermute | solution.py:356
  8.0 1.7 %collective-permute-start.4 = (bf16[256,256]{1,0:T(8,128)(2,1)S(1)}, bf16[256,256]{1,0:T(8,128)(2,1)S(1)}, u32[]{:S(2)}, u32[]{:S(2)}) collective-permute-start(bf16[256,256]{1,0:T(8,128)(2,1)S(1)} %get-tuple-element.43), channel_id=1, source_target_pairs={{0,2},{1,3},{2,0},{3,1},{4,6},{5,7},{6,4},{7,5},{8,10},{9,11},{10,... | collective-permute-start | bytes 393224 | tf_op jit(solution)/shard_map/ppermute | solution.py:356
  9.6 3.8 %shard_map.65 = (f32[1920,128]{1,0:T(8,128)S(1)}, bf16[1536,1536]{1,0:T(8,128)(2,1)S(1)}, bf16[1536,1536]{1,0:T(8,128)(2,1)S(1)}) custom-call(s32[2,32]{1,0:T(2,128)S(4)} %get-tuple-element.28.lists, f32[1920,128]{1,0:T(8,128)S(1)} %get-tuple-element.29.spread, bf16[6144,256]{1,0:T(8,128)(2,1)S(1)} %get-tuple-element.30.pool, ...), custom_call_target="tpu_custom_call" | custom-call | flops 201326592 | bytes 20971520 | tf_op jit(solution)/shard_map/pallas_call | solution.py:288
  13.5 1.5 %shard_map.66 = (bf16[128,1536]{1,0:T(8,128)(2,1)S(1)}, f32[128,1536]{1,0:T(8,128)S(1)}, bf16[128,32]{1,0:T(8,128)(2,1)S(1)}) custom-call(s32[2,8]{1,0:T(2,128)S(4)} %get-tuple-element.27.table, f32[1920,128]{1,0:T(8,128)S(1)} %get-tuple-element.32.attn, bf16[1536,1536]{1,0:T(8,128)(2,1)S(1)} %get-tuple-element.33.peer_w.weight, ...), custom_call_target="tpu_custom_call" | custom-call | flops 1207959552 | bytes 10485760 | tf_op jit(solution)/shard_map/pallas_call | solution.py:288
  15.0 0.0 collective-permute-done.peer_q
  15.0 0.0 collective-permute-done.1.refs_0_
  15.0 4.2 %collective-permute-done.2.refs_1_ = bf16[256,256]{1,0:T(8,128)(2,1)S(1)} collective-permute-done((bf16[256,256]{1,0:T(8,128)(2,1)S(1)}, bf16[256,256]{1,0:T(8,128)(2,1)S(1)}, u32[]{:S(2)}, u32[]{:S(2)}) %collective-permute-start.2) | collective-permute-done | bytes 131104 | tf_op jit(solution)/shard_map/ppermute | solution.py:356
  19.2 0.0 collective-permute-done.3.refs_2_
  19.2 0.0 collective-permute-done.4.refs_3_
  19.2 0.6 %shard_map.67 = (bf16[4,48,128]{2,1,0:T(8,128)(2,1)S(1)}, bf16[3,48,128]{2,1,0:T(8,128)(2,1)S(1)}, bf16[128,1536]{1,0:T(8,128)(2,1)S(1)}) custom-call(bf16[128,1536]{1,0:T(8,128)(2,1)S(1)} %get-tuple-element.37.through, s32[2,8]{1,0:T(2,128)S(4)} %get-tuple-element.27.table, ...), custom_call_target="tpu_custom_call", output_to_operand_aliasing={{2}: (0, {})} | custom-call | tf_op jit(solution)/shard_map/pallas_call | solution.py:288
  19.8 0.1 collective-permute-start.5
  19.9 0.5 %collective-permute-start.6 = (bf16[3,48,128]{2,1,0:T(8,128)(2,1)S(1)}, bf16[3,48,128]{2,1,0:T(8,128)(2,1)S(1)}, u32[]{:S(2)}, u32[]{:S(2)}) collective-permute-start(bf16[3,48,128]{2,1,0:T(8,128)(2,1)S(1)} %get-tuple-element.46), channel_id=1, source_target_pairs={{0,1},{1,0},{2,3},{3,2},{4,5},{5,4},{6,7},{7,6},{8,9},{9,8},{10,11... | collective-permute-start | bytes 110600 | tf_op jit(solution)/shard_map/ppermute | solution.py:400
  20.4 1.3 %collective-permute-done.6.arrived = bf16[3,48,128]{2,1,0:T(8,128)(2,1)S(1)} collective-permute-done((bf16[3,48,128]{2,1,0:T(8,128)(2,1)S(1)}, bf16[3,48,128]{2,1,0:T(8,128)(2,1)S(1)}, u32[]{:S(2)}, u32[]{:S(2)}) %collective-permute-start.6) | collective-permute-done | bytes 36896 | tf_op jit(solution)/shard_map/ppermute | solution.py:400
  21.6 0.9 %shard_map.68 = (bf16[32,1536]{1,0:T(8,128)(2,1)S(1)}, bf16[32,1536]{1,0:T(8,128)(2,1)S(1)}) custom-call(bf16[1536,1536]{1,0:T(8,128)(2,1)S(1)} %get-tuple-element.33.peer_w.weight, bf16[4,48,128]{2,1,0:T(8,128)(2,1)S(1)} %get-tuple-element.45.found, bf16[3,48,128]{2,1,0:T(8,128)(2,1)S(1)} %collective-permute-done.6.arrived), custom_call_target="tpu_custom_call" | custom-call | tf_op jit(solution)/shard_map/pallas_call | solution.py:288
  22.5 0.2 collective-permute-start.7
  22.7 0.9 %shard_map.69.own_m = f32[32,1536]{1,0:T(8,128)S(1)} custom-call(bf16[32,1536]{1,0:T(8,128)(2,1)S(1)} %get-tuple-element.47.lhs, bf16[1536,1536]{1,0:T(8,128)(2,1)S(1)} %get-tuple-element.34.own_w.weight), custom_call_target="tpu_custom_call" | custom-call | flops 150994944 | bytes 6291456 | tf_op jit(solution)/shard_map/pallas_call | solution.py:288
  23.6 0.3 %collective-permute-done.7.others_m = bf16[32,1536]{1,0:T(8,128)(2,1)S(1)} collective-permute-done((bf16[32,1536]{1,0:T(8,128)(2,1)S(1)}, bf16[32,1536]{1,0:T(8,128)(2,1)S(1)}, u32[]{:S(2)}, u32[]{:S(2)}) %collective-permute-start.7) | collective-permute-done | bytes 98336 | tf_op jit(solution)/shard_map/ppermute | solution.py:408
  23.9 0.0 collective-permute-done.5.others
  23.9 0.9 %shard_map.70 = bf16[128,1536]{1,0:T(8,128)(2,1)} custom-call(bf16[128,32]{1,0:T(8,128)(2,1)S(1)} %get-tuple-element.35.spot, f32[128,1536]{1,0:T(8,128)S(1)} %get-tuple-element.36.own, bf16[128,1536]{1,0:T(8,128)(2,1)S(1)} %collective-permute-done.5.others, f32[32,1536]{1,0:T(8,128)S(1)} %shard_map.69.own_m, ...), custom_call_target="tpu_custom_call" | custom-call | tf_op jit(solution)/shard_map/pallas_call | solution.py:288
Async XLA Ops:
  2.1 12.9 %collective-permute-start = (bf16[3,48,128]{2,1,0:T(8,128)(2,1)S(1)}, bf16[3,48,128]{2,1,0:T(8,128)(2,1)S(1)}, u32[]{:S(2)}, u32[]{:S(2)}) collective-permute-start(bf16[3,48,128]{2,1,0:T(8,128)(2,1)S(1)} %get-tuple-element.39), channel_id=1, source_target_pairs={{0,1},{1,0},{2,3},{3,2},{4,5},{5,4},{6,7},{7,6},{8,9},{9,8},{10,11... | collective-permute-start | bytes 110600 | tf_op jit(solution)/shard_map/ppermute | solution.py:348
  2.7 12.4 %collective-permute-start.1 = (bf16[256,256]{1,0:T(8,128)(2,1)S(1)}, bf16[256,256]{1,0:T(8,128)(2,1)S(1)}, u32[]{:S(2)}, u32[]{:S(2)}) collective-permute-start(bf16[256,256]{1,0:T(8,128)(2,1)S(1)} %get-tuple-element.40), channel_id=1, source_target_pairs={{0,12},{1,15},{2,14},{3,13},{4,8},{5,11},{6,10},{7,9},{8,4},{9,7},... | collective-permute-start | bytes 393224 | tf_op jit(solution)/shard_map/ppermute | solution.py:356
  7.3 11.9 %collective-permute-start.2 = (bf16[256,256]{1,0:T(8,128)(2,1)S(1)}, bf16[256,256]{1,0:T(8,128)(2,1)S(1)}, u32[]{:S(2)}, u32[]{:S(2)}) collective-permute-start(bf16[256,256]{1,0:T(8,128)(2,1)S(1)} %get-tuple-element.41), channel_id=1, source_target_pairs={{0,8},{1,11},{2,10},{3,9},{4,12},{5,15},{6,14},{7,13},{8,0},{9,3},... | collective-permute-start | bytes 393224 | tf_op jit(solution)/shard_map/ppermute | solution.py:356
  7.3 11.9 %collective-permute-start.3 = (bf16[256,256]{1,0:T(8,128)(2,1)S(1)}, bf16[256,256]{1,0:T(8,128)(2,1)S(1)}, u32[]{:S(2)}, u32[]{:S(2)}) collective-permute-start(bf16[256,256]{1,0:T(8,128)(2,1)S(1)} %get-tuple-element.42), channel_id=1, source_target_pairs={{0,4},{1,7},{2,6},{3,5},{4,0},{5,3},{6,2},{7,1},{8,12},{9,15},{10,... | collective-permute-start | bytes 393224 | tf_op jit(solution)/shard_map/ppermute | solution.py:356
  8.0 11.2 %collective-permute-start.4 = (bf16[256,256]{1,0:T(8,128)(2,1)S(1)}, bf16[256,256]{1,0:T(8,128)(2,1)S(1)}, u32[]{:S(2)}, u32[]{:S(2)}) collective-permute-start(bf16[256,256]{1,0:T(8,128)(2,1)S(1)} %get-tuple-element.43), channel_id=1, source_target_pairs={{0,2},{1,3},{2,0},{3,1},{4,6},{5,7},{6,4},{7,5},{8,10},{9,11},{10,... | collective-permute-start | bytes 393224 | tf_op jit(solution)/shard_map/ppermute | solution.py:356
  19.8 4.1 %collective-permute-start.5 = (bf16[128,1536]{1,0:T(8,128)(2,1)S(1)}, bf16[128,1536]{1,0:T(8,128)(2,1)S(1)}, u32[]{:S(2)}, u32[]{:S(2)}) collective-permute-start(bf16[128,1536]{1,0:T(8,128)(2,1)S(1)} %get-tuple-element.44), channel_id=1, source_target_pairs={{0,1},{1,0},{2,3},{3,2},{4,5},{5,4},{6,7},{7,6},{8,9},{9,8},{10,11... | collective-permute-start | bytes 1179656 | tf_op jit(solution)/shard_map/ppermute | solution.py:399
  19.9 1.8 %collective-permute-start.6 = (bf16[3,48,128]{2,1,0:T(8,128)(2,1)S(1)}, bf16[3,48,128]{2,1,0:T(8,128)(2,1)S(1)}, u32[]{:S(2)}, u32[]{:S(2)}) collective-permute-start(bf16[3,48,128]{2,1,0:T(8,128)(2,1)S(1)} %get-tuple-element.46), channel_id=1, source_target_pairs={{0,1},{1,0},{2,3},{3,2},{4,5},{5,4},{6,7},{7,6},{8,9},{9,8},{10,11... | collective-permute-start | bytes 110600 | tf_op jit(solution)/shard_map/ppermute | solution.py:400
  22.5 1.3 %collective-permute-start.7 = (bf16[32,1536]{1,0:T(8,128)(2,1)S(1)}, bf16[32,1536]{1,0:T(8,128)(2,1)S(1)}, u32[]{:S(2)}, u32[]{:S(2)}) collective-permute-start(bf16[32,1536]{1,0:T(8,128)(2,1)S(1)} %get-tuple-element.48), channel_id=1, source_target_pairs={{0,1},{1,0},{2,3},{3,2},{4,5},{5,4},{6,7},{7,6},{8,9},{9,8},{10,11... | collective-permute-start | bytes 294920 | tf_op jit(solution)/shard_map/ppermute | solution.py:408

commit v8 on v6

--- a/solution.py
+++ b/solution.py
@@ -100,7 +100,8 @@
             sends[i][b * BLK : (b + 1) * BLK, :] = pool[pl.ds(row, BLK), :]
 
 
-def ask_kernel(asked, own_q, peer_q, asked_f, *outs):
+def ask_kernel(asked, own_q, peer_q, asked_f, *refs):
+    outs = refs[-len(asked) :]
     rows = own_q.shape[1]
     for n, i in enumerate(asked):
         outs[n][0:rows, :] = own_q[i]
@@ -108,7 +109,7 @@
         outs[n][2 * rows :, :] = asked_f[n]
 
 
-def answer_kernel(ops, asked, steps, after, table, *refs):
+def answer_kernel(ops, asked, steps, table, *refs):
     count = len(asked)
     questions, windows, outs = refs[:count], refs[count : 2 * count], refs[2 * count :]
     rows = outs[0].shape[0]
@@ -181,16 +182,20 @@
     lax.fori_loop(0, count // group, some, 0)
 
 
-def long_kernel(
+def stay_kernel(
     stride, steps, group, after, lists, spread, pool, fresh, weight_h,
-    attn, late, recent, peer_w, sems,
+    attn, peer_w, own_w, recent, late, sems,
 ):
     slots = lists.shape[1]
     rows = spread.shape[0] // stride
     heads = rows // steps
     half = peer_w.shape[1]
-    peer = (1 - lax.axis_index("tp")) * half
-    load = start_copies([(weight_h.at[:, pl.ds(pl.multiple_of(peer, HDIM), half)], peer_w)], sems)
+    core = lax.axis_index("tp")
+    own_cols = pl.ds(pl.multiple_of(core * half, HDIM), half)
+    peer_cols = pl.ds(pl.multiple_of((1 - core) * half, HDIM), half)
+    loads = start_copies(
+        [(weight_h.at[:, peer_cols], peer_w), (weight_h.at[:, own_cols], own_w)], sems
+    )
     slot = lax.broadcasted_iota(jnp.int32, (slots, steps * slots), 0)
     col = lax.broadcasted_iota(jnp.int32, (slots, steps * slots), 1)
     for i in range(rows):
@@ -199,29 +204,16 @@
         mine = (col % slots == slot) & (col // slots <= i // heads)
         recent[at, :] = jnp.where(mine, score, -jnp.inf)
     longer = pool.shape[0] // BLK - slots
-    stay_requests(stride, rows, group, 0, longer, WIN, lists, spread, pool, recent, attn, late)
-    load[0].wait()
-
-
-def short_kernel(
-    stride, group, after, lists, spread, pool, fresh, weight_h, recent, attn_in, late_in,
-    attn, late, own_w, sems,
-):
-    slots = lists.shape[1]
-    rows = spread.shape[0] // stride
-    half = own_w.shape[1]
-    own = lax.axis_index("tp") * half
-    load = start_copies([(weight_h.at[:, pl.ds(pl.multiple_of(own, HDIM), half)], own_w)], sems)
-    longer = pool.shape[0] // BLK - slots
-    stay_requests(
-        stride, rows, group, longer, slots - longer, BLK, lists, spread, pool, recent, attn, late
-    )
+    state = (lists, spread, pool, recent, attn, late)
+    stay_requests(stride, rows, group, 0, longer, WIN, *state)
+    stay_requests(stride, rows, group, longer, slots - longer, BLK, *state)
     for i in range(rows):
         at = pl.ds(i * stride, slots)
         attn[at, :] = attn[at, :] + jnp.dot(
             late[at, :].astype(jnp.bfloat16), fresh[:, HDIM:], preferred_element_type=jnp.float32
         )
-    load[0].wait()
+    for load in loads:
+        load.wait()
 
 
 def move_kernel(ops, asked, steps, slots, group, after, table, own_q, peer_q, fresh, *refs):
@@ -388,44 +380,29 @@
                 pairs.append((a * cores + c, (a ^ m) * cores + c))
         return lax.ppermute(array, ("inst", "tp"), pairs)
 
+    kept = [i for i in range(ops) if i not in asked]
+    handed = call(
+        functools.partial(ask_kernel, asked),
+        [(vmem, own_q), (vmem, peer_q), (vmem, asked_f)] + [(vmem, sends[i]) for i in kept],
+        [(vmem, bf16(WIN, kvw))] * len(kept)
+        + [(vmem, bf16(2 * rows + 2 * FEW, HDIM))] * len(asked),
+        aliases={3 + n: n for n in range(len(kept))},
+    )
     blocks = [None] * ops
-    for i in reversed(range(ops)):
-        if i not in asked:
-            blocks[i] = exchange(i, sends[i])
-    questions = call(
-        functools.partial(ask_kernel, asked),
-        [(vmem, own_q), (vmem, peer_q), (vmem, asked_f)],
-        [(vmem, bf16(2 * rows + 2 * FEW, HDIM))] * len(asked),
-    )
-    asking = [exchange(i, question) for i, question in zip(asked, questions)]
-    half_cost = pl.CostEstimate(
-        flops=2 * slots * rows * WIN * HDIM, bytes_accessed=10 * MIB, transcendentals=0
-    )
-    attn, late, recent, peer_w = call(
-        functools.partial(long_kernel, stride, steps, 8),
-        [
-            (vmem, questions[0]),
-            (smem, lists),
-            (vmem, spread),
-            (vmem, pool),
-            (vmem, fresh),
-            (hbm, out_weight),
-        ],
-        [(vmem, f32(rows * stride, HDIM))] * 3 + [(vmem, bf16(depth, half))],
-        [dma((1,))],
-        cost=half_cost,
-    )
+    for i, block in reversed(list(zip(kept, handed))):
+        blocks[i] = exchange(i, block)
+    asking = [exchange(i, question) for i, question in zip(asked, handed[len(kept) :])]
     answers = call(
         functools.partial(answer_kernel, ops, asked, steps),
-        [(vmem, attn), (smem, table)]
+        [(smem, table)]
         + [(vmem, question) for question in asking]
         + [(vmem, sends[i]) for i in asked],
         [(vmem, bf16(2 * rows, HDIM))] * len(asked),
     )
     for i, answer in zip(asked, answers):
         blocks[i] = exchange(i, answer)
-    attn, late, own_w = call(
-        functools.partial(short_kernel, stride, 8),
+    attn, peer_w, own_w = call(
+        functools.partial(stay_kernel, stride, steps, 8),
         [
             (vmem, answers[0]),
             (smem, lists),
@@ -433,14 +410,16 @@
             (vmem, pool),
             (vmem, fresh),
             (hbm, out_weight),
-            (vmem, recent),
-            (vmem, attn),
-            (vmem, late),
-        ],
-        [(vmem, f32(rows * stride, HDIM))] * 2 + [(vmem, bf16(depth, half))],
-        [dma((1,))],
-        cost=half_cost,
-        aliases={7: 0, 8: 1},
+        ],
+        [(vmem, f32(rows * stride, HDIM))] + [(vmem, bf16(depth, half))] * 2,
+        [
+            vmem((rows * stride, HDIM), jnp.float32),
+            vmem((rows * stride, HDIM), jnp.float32),
+            dma((2,)),
+        ],
+        cost=pl.CostEstimate(
+            flops=200 * slots * rows * WIN * HDIM, bytes_accessed=20 * MIB, transcendentals=0
+        ),
     )
 
     found, sent = call(

time: 26.3 us -> 25.4 us (0.966)
  the two profiles are of different devices: /device:TPU:0 before, /device:TPU:9 now
where the time goes in v8:
time: 25.4 us; the launch traced here: 25.2 us
  starting transfers between devices  10.8 us (43%)
  Pallas kernels  9.39 us (37%)
  waiting for transfers between devices  4.93 us (19%)
    ppermute x5, starting transfers between devices, exchange(): return lax.ppermute(array, ('inst', 'tp'), pairs)  9.75 us
    pallas_call x8, Pallas kernels, call(): pl.pallas_call(kernel, out_shape=[space(shape.shape, shape.dtype) for spa...  9.39 us
    ppermute x5, waiting for transfers between devices, exchange(): return lax.ppermute(array, ('inst', 'tp'), pairs)  2.1 us
    ppermute x1, waiting for transfers between devices, body(): arrived = lax.ppermute(sent, 'tp', swap)  1.2 us
    ppermute x1, waiting for transfers between devices, body(): peer_q = lax.ppermute(sent_q, 'tp', swap)  0.87 us
    ppermute x1, waiting for transfers between devices, body(): others = lax.ppermute(partial, 'tp', swap)  0.77 us
    ppermute x1, starting transfers between devices, body(): peer_q = lax.ppermute(sent_q, 'tp', swap)  0.74 us
  transfers between devices with their start and end apart: 8, of which 4 were waited for; matrix products, arithmetic and copies ran while one was open for 0% of the time, Pallas kernels for 20%

profile of v8, /device:TPU:9, one launch (start us, length us, event | category | flops | bytes accessed | tf_op | source)
XLA Modules:
  0.0 25.2 jit_solution(6367247317779634757)
XLA Ops:
  0.0 2.1 %shard_map.64 = (s32[3,8]{1,0:T(4,128)S(4)}, s32[2,32]{1,0:T(2,128)S(4)}, bf16[6144,256]{1,0:T(8,128)(2,1)S(1)}, f32[1920,128]{1,0:T(8,128)S(1)}, bf16[128,256]{...) custom-call(s32[8,32]{1,0:T(8,128)} %anchor_h.1, ...), custom_call_target="tpu_custom_call" | custom-call | tf_op jit(solution)/shard_map/pallas_call | solution.py:308
  2.1 0.7 %collective-permute-start = (bf16[3,48,128]{2,1,0:T(8,128)(2,1)S(1)}, bf16[3,48,128]{2,1,0:T(8,128)(2,1)S(1)}, u32[]{:S(2)}, u32[]{:S(2)}) collective-permute-start(bf16[3,48,128]{2,1,0:T(8,128)(2,1)S(1)} %get-tuple-element.30), channel_id=1, source_target_pairs={{0,1},{1,0},{2,3},{3,2},{4,5},{5,4},{6,7},{7,6},{8,9},{9,8},{10,11... | collective-permute-start | bytes 110600 | tf_op jit(solution)/shard_map/ppermute | solution.py:373
  2.9 0.9 %collective-permute-done.peer_q = bf16[3,48,128]{2,1,0:T(8,128)(2,1)S(1)} collective-permute-done((bf16[3,48,128]{2,1,0:T(8,128)(2,1)S(1)}, bf16[3,48,128]{2,1,0:T(8,128)(2,1)S(1)}, u32[]{:S(2)}, u32[]{:S(2)}) %collective-permute-start) | collective-permute-done | bytes 36896 | tf_op jit(solution)/shard_map/ppermute | solution.py:373
  3.8 3.3 %collective-permute-start.1 = (bf16[128,128]{1,0:T(8,128)(2,1)S(1)}, bf16[128,128]{1,0:T(8,128)(2,1)S(1)}, u32[]{:S(2)}, u32[]{:S(2)}) collective-permute-start(bf16[128,128]{1,0:T(8,128)(2,1)S(1)} %get-tuple-element.35), channel_id=1, source_target_pairs={{0,8},{1,11},{2,10},{3,9},{4,12},{5,15},{6,14},{7,13},{8,0},{9,3},... | collective-permute-start | bytes 98312 | tf_op jit(solution)/shard_map/ppermute | solution.py:381
  7.0 0.0 collective-permute-start.2
  7.0 2.1 %collective-permute-start.4 = (bf16[256,256]{1,0:T(8,128)(2,1)S(1)}, bf16[256,256]{1,0:T(8,128)(2,1)S(1)}, u32[]{:S(2)}, u32[]{:S(2)}) collective-permute-start(bf16[256,256]{1,0:T(8,128)(2,1)S(1)} %get-tuple-element.44), channel_id=1, source_target_pairs={{0,4},{1,7},{2,6},{3,5},{4,0},{5,3},{6,2},{7,1},{8,12},{9,15},{10,... | collective-permute-start | bytes 393224 | tf_op jit(solution)/shard_map/ppermute | solution.py:381
  9.2 0.2 collective-permute-start.5
  9.4 2.1 %collective-permute-done.1.refs_0_ = bf16[128,128]{1,0:T(8,128)(2,1)S(1)} collective-permute-done((bf16[128,128]{1,0:T(8,128)(2,1)S(1)}, bf16[128,128]{1,0:T(8,128)(2,1)S(1)}, u32[]{:S(2)}, u32[]{:S(2)}) %collective-permute-start.1) | collective-permute-done | bytes 32800 | tf_op jit(solution)/shard_map/ppermute | solution.py:381
  11.5 0.5 %shard_map.66.after = bf16[96,128]{1,0:T(8,128)(2,1)S(1)} custom-call(s32[3,8]{1,0:T(4,128)S(4)} %get-tuple-element.28.table, bf16[128,128]{1,0:T(8,128)(2,1)S(1)} %collective-permute-done.1.refs_0_, bf16[256,256]{1,0:T(8,128)(2,1)S(1)} %get-tuple-element.36.refs_1_), custom_call_target="tpu_custom_call" | custom-call | tf_op jit(solution)/shard_map/pallas_call | solution.py:308
  11.9 4.1 %collective-permute-start.3 = (bf16[96,128]{1,0:T(8,128)(2,1)S(1)}, bf16[96,128]{1,0:T(8,128)(2,1)S(1)}, u32[]{:S(2)}, u32[]{:S(2)}) collective-permute-start(bf16[96,128]{1,0:T(8,128)(2,1)S(1)} %shard_map.66.after), channel_id=1, source_target_pairs={{0,8},{1,11},{2,10},{3,9},{4,12},{5,15},{6,14},{7,13},{8,0},{9,3},... | collective-permute-start | bytes 73736 | tf_op jit(solution)/shard_map/ppermute | solution.py:381
  16.1 3.8 %shard_map.67 = (f32[1920,128]{1,0:T(8,128)S(1)}, bf16[1536,1536]{1,0:T(8,128)(2,1)S(1)}, bf16[1536,1536]{1,0:T(8,128)(2,1)S(1)}) custom-call(bf16[96,128]{1,0:T(8,128)(2,1)S(1)} %shard_map.66.after, s32[2,32]{1,0:T(2,128)S(4)} %get-tuple-element.37.lists, f32[1920,128]{1,0:T(8,128)S(1)} %get-tuple-element.38.spread, ...), custom_call_target="tpu_custom_call" | custom-call | flops 10066329600 | bytes 20971520 | tf_op jit(solution)/shard_map/pallas_call | solution.py:308
  19.9 0.0 collective-permute-done.3.refs_1_
  19.9 0.0 collective-permute-done.2.refs_0_
  19.9 0.0 collective-permute-done.4.refs_2_
  19.9 0.0 collective-permute-done.5.refs_3_
  19.9 0.5 %shard_map.68 = (f32[4,48,128]{2,1,0:T(8,128)S(1)}, bf16[3,48,128]{2,1,0:T(8,128)(2,1)S(1)}) custom-call(bf16[1536,1536]{1,0:T(8,128)(2,1)S(1)} %get-tuple-element.42.after.weight, s32[3,8]{1,0:T(4,128)S(4)} %get-tuple-element.28.table, bf16[4,48,128]{2,1,0:T(8,128)(2,1)S(1)} %get-tuple-element.29.own_q, ...), custom_call_target="tpu_custom_call" | custom-call | tf_op jit(solution)/shard_map/pallas_call | solution.py:308
  20.5 0.1 collective-permute-start.6
  20.5 1.2 %collective-permute-done.6.arrived = bf16[3,48,128]{2,1,0:T(8,128)(2,1)S(1)} collective-permute-done((bf16[3,48,128]{2,1,0:T(8,128)(2,1)S(1)}, bf16[3,48,128]{2,1,0:T(8,128)(2,1)S(1)}, u32[]{:S(2)}, u32[]{:S(2)}) %collective-permute-start.6) | collective-permute-done | bytes 36896 | tf_op jit(solution)/shard_map/ppermute | solution.py:431
  21.7 0.9 %shard_map.69 = (bf16[128,1536]{1,0:T(8,128)(2,1)S(1)}, bf16[128,1536]{1,0:T(8,128)(2,1)S(1)}, f32[1920,128]{1,0:T(8,128)S(1)}) custom-call(s32[3,8]{1,0:T(4,128)S(4)} %get-tuple-element.28.table, f32[1920,128]{1,0:T(8,128)S(1)} %get-tuple-element.41.attn, f32[4,48,128]{2,1,0:T(8,128)S(1)} %get-tuple-element.46.found, ...), custom_call_target="tpu_custom_call", output_to_operand_aliasing={{2}: (1, {})} | custom-call | tf_op jit(solution)/shard_map/pallas_call | solution.py:308
  22.6 0.2 collective-permute-start.7
  22.8 0.8 %shard_map.70.own = f32[128,1536]{1,0:T(8,128)S(1)} custom-call(bf16[128,1536]{1,0:T(8,128)(2,1)S(1)} %get-tuple-element.49.lhs, bf16[1536,1536]{1,0:T(8,128)(2,1)S(1)} %get-tuple-element.42.after.weight), custom_call_target="tpu_custom_call" | custom-call | flops 603979776 | bytes 6291456 | tf_op jit(solution)/shard_map/pallas_call | solution.py:308
  23.6 0.8 %collective-permute-done.7.others = bf16[128,1536]{1,0:T(8,128)(2,1)S(1)} collective-permute-done((bf16[128,1536]{1,0:T(8,128)(2,1)S(1)}, bf16[128,1536]{1,0:T(8,128)(2,1)S(1)}, u32[]{:S(2)}, u32[]{:S(2)}) %collective-permute-start.7) | collective-permute-done | bytes 393248 | tf_op jit(solution)/shard_map/ppermute | solution.py:443
  24.4 0.8 %shard_map.71 = bf16[128,1536]{1,0:T(8,128)(2,1)} custom-call(f32[128,1536]{1,0:T(8,128)S(1)} %shard_map.70.own, bf16[128,1536]{1,0:T(8,128)(2,1)S(1)} %collective-permute-done.7.others), custom_call_target="tpu_custom_call" | custom-call | tf_op jit(solution)/shard_map/pallas_call | solution.py:308
  (1 shorter events, 0.0 us)
Async XLA Ops:
  2.1 1.6 %collective-permute-start = (bf16[3,48,128]{2,1,0:T(8,128)(2,1)S(1)}, bf16[3,48,128]{2,1,0:T(8,128)(2,1)S(1)}, u32[]{:S(2)}, u32[]{:S(2)}) collective-permute-start(bf16[3,48,128]{2,1,0:T(8,128)(2,1)S(1)} %get-tuple-element.30), channel_id=1, source_target_pairs={{0,1},{1,0},{2,3},{3,2},{4,5},{5,4},{6,7},{7,6},{8,9},{9,8},{10,11... | collective-permute-start | bytes 110600 | tf_op jit(solution)/shard_map/ppermute | solution.py:373
  3.8 7.7 %collective-permute-start.1 = (bf16[128,128]{1,0:T(8,128)(2,1)S(1)}, bf16[128,128]{1,0:T(8,128)(2,1)S(1)}, u32[]{:S(2)}, u32[]{:S(2)}) collective-permute-start(bf16[128,128]{1,0:T(8,128)(2,1)S(1)} %get-tuple-element.35), channel_id=1, source_target_pairs={{0,8},{1,11},{2,10},{3,9},{4,12},{5,15},{6,14},{7,13},{8,0},{9,3},... | collective-permute-start | bytes 98312 | tf_op jit(solution)/shard_map/ppermute | solution.py:381
  7.0 12.9 %collective-permute-start.2 = (bf16[256,256]{1,0:T(8,128)(2,1)S(1)}, bf16[256,256]{1,0:T(8,128)(2,1)S(1)}, u32[]{:S(2)}, u32[]{:S(2)}) collective-permute-start(bf16[256,256]{1,0:T(8,128)(2,1)S(1)} %get-tuple-element.43), channel_id=1, source_target_pairs={{0,12},{1,15},{2,14},{3,13},{4,8},{5,11},{6,10},{7,9},{8,4},{9,7},... | collective-permute-start | bytes 393224 | tf_op jit(solution)/shard_map/ppermute | solution.py:381
  7.0 12.9 %collective-permute-start.4 = (bf16[256,256]{1,0:T(8,128)(2,1)S(1)}, bf16[256,256]{1,0:T(8,128)(2,1)S(1)}, u32[]{:S(2)}, u32[]{:S(2)}) collective-permute-start(bf16[256,256]{1,0:T(8,128)(2,1)S(1)} %get-tuple-element.44), channel_id=1, source_target_pairs={{0,4},{1,7},{2,6},{3,5},{4,0},{5,3},{6,2},{7,1},{8,12},{9,15},{10,... | collective-permute-start | bytes 393224 | tf_op jit(solution)/shard_map/ppermute | solution.py:381
  9.2 10.7 %collective-permute-start.5 = (bf16[256,256]{1,0:T(8,128)(2,1)S(1)}, bf16[256,256]{1,0:T(8,128)(2,1)S(1)}, u32[]{:S(2)}, u32[]{:S(2)}) collective-permute-start(bf16[256,256]{1,0:T(8,128)(2,1)S(1)} %get-tuple-element.45), channel_id=1, source_target_pairs={{0,2},{1,3},{2,0},{3,1},{4,6},{5,7},{6,4},{7,5},{8,10},{9,11},{10,... | collective-permute-start | bytes 393224 | tf_op jit(solution)/shard_map/ppermute | solution.py:381
  11.9 7.9 %collective-permute-start.3 = (bf16[96,128]{1,0:T(8,128)(2,1)S(1)}, bf16[96,128]{1,0:T(8,128)(2,1)S(1)}, u32[]{:S(2)}, u32[]{:S(2)}) collective-permute-start(bf16[96,128]{1,0:T(8,128)(2,1)S(1)} %shard_map.66.after), channel_id=1, source_target_pairs={{0,8},{1,11},{2,10},{3,9},{4,12},{5,15},{6,14},{7,13},{8,0},{9,3},... | collective-permute-start | bytes 73736 | tf_op jit(solution)/shard_map/ppermute | solution.py:381
  20.5 1.3 %collective-permute-start.6 = (bf16[3,48,128]{2,1,0:T(8,128)(2,1)S(1)}, bf16[3,48,128]{2,1,0:T(8,128)(2,1)S(1)}, u32[]{:S(2)}, u32[]{:S(2)}) collective-permute-start(bf16[3,48,128]{2,1,0:T(8,128)(2,1)S(1)} %get-tuple-element.47), channel_id=1, source_target_pairs={{0,1},{1,0},{2,3},{3,2},{4,5},{5,4},{6,7},{7,6},{8,9},{9,8},{10,11... | collective-permute-start | bytes 110600 | tf_op jit(solution)/shard_map/ppermute | solution.py:431
  22.6 1.8 %collective-permute-start.7 = (bf16[128,1536]{1,0:T(8,128)(2,1)S(1)}, bf16[128,1536]{1,0:T(8,128)(2,1)S(1)}, u32[]{:S(2)}, u32[]{:S(2)}) collective-permute-start(bf16[128,1536]{1,0:T(8,128)(2,1)S(1)} %get-tuple-element.50), channel_id=1, source_target_pairs={{0,1},{1,0},{2,3},{3,2},{4,5},{5,4},{6,7},{7,6},{8,9},{9,8},{10,11... | collective-permute-start | bytes 1179656 | tf_op jit(solution)/shard_map/ppermute | solution.py:443

commit v9 on v6

--- a/solution.py
+++ b/solution.py
@@ -100,7 +100,8 @@
             sends[i][b * BLK : (b + 1) * BLK, :] = pool[pl.ds(row, BLK), :]
 
 
-def ask_kernel(asked, own_q, peer_q, asked_f, *outs):
+def ask_kernel(asked, own_q, peer_q, asked_f, *refs):
+    outs = refs[-len(asked) :]
     rows = own_q.shape[1]
     for n, i in enumerate(asked):
         outs[n][0:rows, :] = own_q[i]
@@ -388,18 +389,21 @@
                 pairs.append((a * cores + c, (a ^ m) * cores + c))
         return lax.ppermute(array, ("inst", "tp"), pairs)
 
+    kept = [i for i in range(ops) if i not in asked]
+    *handed, questions = call(
+        functools.partial(ask_kernel, asked),
+        [(vmem, own_q), (vmem, peer_q), (vmem, asked_f)] + [(vmem, sends[i]) for i in kept],
+        [(vmem, bf16(WIN, kvw))] * len(kept)
+        + [(vmem, bf16(2 * rows + 2 * FEW, HDIM))] * len(asked),
+        aliases={3 + n: n for n in range(len(kept))},
+    )
+    questions = [questions]
     blocks = [None] * ops
-    for i in reversed(range(ops)):
-        if i not in asked:
-            blocks[i] = exchange(i, sends[i])
-    questions = call(
-        functools.partial(ask_kernel, asked),
-        [(vmem, own_q), (vmem, peer_q), (vmem, asked_f)],
-        [(vmem, bf16(2 * rows + 2 * FEW, HDIM))] * len(asked),
-    )
+    for i, block in zip(kept, handed):
+        blocks[i] = exchange(i, block)
     asking = [exchange(i, question) for i, question in zip(asked, questions)]
     half_cost = pl.CostEstimate(
-        flops=2 * slots * rows * WIN * HDIM, bytes_accessed=10 * MIB, transcendentals=0
+        flops=100 * slots * rows * WIN * HDIM, bytes_accessed=10 * MIB, transcendentals=0
     )
     attn, late, recent, peer_w = call(
         functools.partial(long_kernel, stride, steps, 8),

time: 26.3 us -> 25 us (0.951)
  waiting for transfers between devices: 3.87 us -> 2.33 us
  starting transfers between devices: 11.2 us -> 11.5 us
    ppermute x5, waiting for transfers between devices: 1.03 us -> 0.01 us  [exchange(): return lax.ppermute(array, ('inst', 'tp'), pairs)]
    ppermute x5, starting transfers between devices: 10.6 us -> 9.9 us  [exchange(): return lax.ppermute(array, ('inst', 'tp'), pairs)]
    ppermute x1, starting transfers between devices: 0.01 us -> 0.52 us  [body(): peer_q = lax.ppermute(sent_q, 'tp', swap)]
    ppermute x1, waiting for transfers between devices: 1.21 us -> 0.87 us  [body(): peer_q = lax.ppermute(sent_q, 'tp', swap)]
    ppermute x1, starting transfers between devices: 0.32 us -> 0.63 us  [body(): arrived = lax.ppermute(sent, 'tp', swap)]
  transfers between devices with their start and end apart: 8 -> 8, of which waited for: 4 -> 3; matrix products, arithmetic and copies ran while one was open for 0% -> 0% of each run, Pallas kernels for 25% -> 27%
where the time goes in v9:
time: 25 us; the launch traced here: 24.8 us
  starting transfers between devices  11.5 us (46%)
  Pallas kernels  10.9 us (44%)
  waiting for transfers between devices  2.33 us (9%)
    pallas_call x9, Pallas kernels, call(): pl.pallas_call(kernel, out_shape=[space(shape.shape, shape.dtype) for spa...  10.9 us
    ppermute x5, starting transfers between devices, exchange(): return lax.ppermute(array, ('inst', 'tp'), pairs)  9.9 us
    ppermute x1, waiting for transfers between devices, body(): peer_q = lax.ppermute(sent_q, 'tp', swap)  0.87 us
    ppermute x1, waiting for transfers between devices, body(): arrived = lax.ppermute(sent, 'tp', swap)  0.87 us
    ppermute x1, starting transfers between devices, body(): arrived = lax.ppermute(sent, 'tp', swap)  0.63 us
    ppermute x1, waiting for transfers between devices, body(): others = lax.ppermute(partial, 'tp', swap)  0.58 us
    ppermute x1, starting transfers between devices, body(): peer_q = lax.ppermute(sent_q, 'tp', swap)  0.52 us
  transfers between devices with their start and end apart: 8, of which 3 were waited for; matrix products, arithmetic and copies ran while one was open for 0% of the time, Pallas kernels for 27%

profile of v9, /device:TPU:0, one launch (start us, length us, event | category | flops | bytes accessed | tf_op | source)
XLA Modules:
  0.0 24.8 jit_solution(2660176763830695846)
XLA Ops:
  0.0 2.1 %shard_map.64 = (s32[3,8]{1,0:T(4,128)S(4)}, s32[2,32]{1,0:T(2,128)S(4)}, bf16[6144,256]{1,0:T(8,128)(2,1)S(1)}, f32[1920,128]{1,0:T(8,128)S(1)}, bf16[128,256]{...) custom-call(s32[8,32]{1,0:T(8,128)} %anchor_h.1, ...), custom_call_target="tpu_custom_call" | custom-call | tf_op jit(solution)/shard_map/pallas_call | solution.py:317
  2.1 0.5 %collective-permute-start = (bf16[3,48,128]{2,1,0:T(8,128)(2,1)S(1)}, bf16[3,48,128]{2,1,0:T(8,128)(2,1)S(1)}, u32[]{:S(2)}, u32[]{:S(2)}) collective-permute-start(bf16[3,48,128]{2,1,0:T(8,128)(2,1)S(1)} %get-tuple-element.33), channel_id=1, source_target_pairs={{0,1},{1,0},{2,3},{3,2},{4,5},{5,4},{6,7},{7,6},{8,9},{9,8},{10,11... | collective-permute-start | bytes 110600 | tf_op jit(solution)/shard_map/ppermute | solution.py:382
  2.7 0.9 %collective-permute-done.peer_q = bf16[3,48,128]{2,1,0:T(8,128)(2,1)S(1)} collective-permute-done((bf16[3,48,128]{2,1,0:T(8,128)(2,1)S(1)}, bf16[3,48,128]{2,1,0:T(8,128)(2,1)S(1)}, u32[]{:S(2)}, u32[]{:S(2)}) %collective-permute-start) | collective-permute-done | bytes 36896 | tf_op jit(solution)/shard_map/ppermute | solution.py:382
  3.5 3.9 %collective-permute-start.1 = (bf16[128,128]{1,0:T(8,128)(2,1)S(1)}, bf16[128,128]{1,0:T(8,128)(2,1)S(1)}, u32[]{:S(2)}, u32[]{:S(2)}) collective-permute-start(bf16[128,128]{1,0:T(8,128)(2,1)S(1)} %get-tuple-element.38.after), channel_id=1, source_target_pairs={{0,8},{1,11},{2,10},{3,9},{4,12},{5,15},{6,14},{7,13},{8,0},{9,3},... | collective-permute-start | bytes 98312 | tf_op jit(solution)/shard_map/ppermute | solution.py:390
  7.5 1.3 %collective-permute-start.2 = (bf16[256,256]{1,0:T(8,128)(2,1)S(1)}, bf16[256,256]{1,0:T(8,128)(2,1)S(1)}, u32[]{:S(2)}, u32[]{:S(2)}) collective-permute-start(bf16[256,256]{1,0:T(8,128)(2,1)S(1)} %get-tuple-element.49), channel_id=1, source_target_pairs={{0,12},{1,15},{2,14},{3,13},{4,8},{5,11},{6,10},{7,9},{8,4},{9,7},... | collective-permute-start | bytes 393224 | tf_op jit(solution)/shard_map/ppermute | solution.py:390
  8.8 0.2 collective-permute-start.4
  9.0 1.5 %collective-permute-start.5 = (bf16[256,256]{1,0:T(8,128)(2,1)S(1)}, bf16[256,256]{1,0:T(8,128)(2,1)S(1)}, u32[]{:S(2)}, u32[]{:S(2)}) collective-permute-start(bf16[256,256]{1,0:T(8,128)(2,1)S(1)} %get-tuple-element.51), channel_id=1, source_target_pairs={{0,2},{1,3},{2,0},{3,1},{4,6},{5,7},{6,4},{7,5},{8,10},{9,11},{10,... | collective-permute-start | bytes 393224 | tf_op jit(solution)/shard_map/ppermute | solution.py:390
  10.6 3.0 %shard_map.66 = (f32[1920,128]{1,0:T(8,128)S(1)}, f32[1920,128]{1,0:T(8,128)S(1)}, f32[1920,128]{1,0:T(8,128)S(1)}, bf16[1536,1536]{1,0:T(8,128)(2,1)S(1)}) custom-call(bf16[128,128]{1,0:T(8,128)(2,1)S(1)} %get-tuple-element.38.after, s32[2,32]{1,0:T(2,128)S(4)} %get-tuple-element.39.lists, f32[1920,128]{1,0:T(8,128)S(1)} %get-tuple-element.40.spread, ...), custom_call_target="tpu_custom_call" | custom-call | flops 5033164800 | bytes 10485760 | tf_op jit(solution)/shard_map/pallas_call | solution.py:317
  13.6 0.0 collective-permute-done.1.refs_0_
  13.6 0.5 %shard_map.67.after = bf16[96,128]{1,0:T(8,128)(2,1)S(1)} custom-call(f32[1920,128]{1,0:T(8,128)S(1)} %get-tuple-element.43.after.attn_in, s32[3,8]{1,0:T(4,128)S(4)} %get-tuple-element.31.table, bf16[128,128]{1,0:T(8,128)(2,1)S(1)} %collective-permute-done.1.refs_0_, bf16[256,256]{1,0:T(8,128)(2,1)S(1)} %get-tuple-element.44.refs_1_), custom_call_target="tpu_custom_call" | custom-call | tf_op jit(solution)/shard_map/pallas_call | solution.py:317
  14.1 2.9 %collective-permute-start.3 = (bf16[96,128]{1,0:T(8,128)(2,1)S(1)}, bf16[96,128]{1,0:T(8,128)(2,1)S(1)}, u32[]{:S(2)}, u32[]{:S(2)}) collective-permute-start(bf16[96,128]{1,0:T(8,128)(2,1)S(1)} %shard_map.67.after), channel_id=1, source_target_pairs={{0,8},{1,11},{2,10},{3,9},{4,12},{5,15},{6,14},{7,13},{8,0},{9,3},... | collective-permute-start | bytes 73736 | tf_op jit(solution)/shard_map/ppermute | solution.py:390
  16.9 2.3 %shard_map.68 = (f32[1920,128]{1,0:T(8,128)S(1)}, f32[1920,128]{1,0:T(8,128)S(1)}, bf16[1536,1536]{1,0:T(8,128)(2,1)S(1)}) custom-call(bf16[96,128]{1,0:T(8,128)(2,1)S(1)} %shard_map.67.after, s32[2,32]{1,0:T(2,128)S(4)} %get-tuple-element.39.lists, f32[1920,128]{1,0:T(8,128)S(1)} %get-tuple-element.40.spread, ...), custom_call_target="tpu_custom_call", output_to_operand_aliasing={{0}: (7, {}), {1}: (8, {})} | custom-call | flops 5033164800 | bytes 10485760 | tf_op jit(solution)/shard_map/pallas_call | solution.py:317
  19.3 0.0 collective-permute-done.3.refs_1_
  19.3 0.0 collective-permute-done.2.refs_0_
  19.3 0.0 collective-permute-done.4.refs_2_
  19.3 0.0 collective-permute-done.5.refs_3_
  19.3 0.5 %shard_map.69 = (f32[4,48,128]{2,1,0:T(8,128)S(1)}, bf16[3,48,128]{2,1,0:T(8,128)(2,1)S(1)}) custom-call(bf16[1536,1536]{1,0:T(8,128)(2,1)S(1)} %get-tuple-element.48.after.weight, s32[3,8]{1,0:T(4,128)S(4)} %get-tuple-element.31.table, bf16[4,48,128]{2,1,0:T(8,128)(2,1)S(1)} %get-tuple-element.32.own_q, ...), custom_call_target="tpu_custom_call" | custom-call | tf_op jit(solution)/shard_map/pallas_call | solution.py:317
  19.9 0.6 %collective-permute-start.6 = (bf16[3,48,128]{2,1,0:T(8,128)(2,1)S(1)}, bf16[3,48,128]{2,1,0:T(8,128)(2,1)S(1)}, u32[]{:S(2)}, u32[]{:S(2)}) collective-permute-start(bf16[3,48,128]{2,1,0:T(8,128)(2,1)S(1)} %get-tuple-element.53), channel_id=1, source_target_pairs={{0,1},{1,0},{2,3},{3,2},{4,5},{5,4},{6,7},{7,6},{8,9},{9,8},{10,11... | collective-permute-start | bytes 110600 | tf_op jit(solution)/shard_map/ppermute | solution.py:456
  20.5 0.9 %collective-permute-done.6.arrived = bf16[3,48,128]{2,1,0:T(8,128)(2,1)S(1)} collective-permute-done((bf16[3,48,128]{2,1,0:T(8,128)(2,1)S(1)}, bf16[3,48,128]{2,1,0:T(8,128)(2,1)S(1)}, u32[]{:S(2)}, u32[]{:S(2)}) %collective-permute-start.6) | collective-permute-done | bytes 36896 | tf_op jit(solution)/shard_map/ppermute | solution.py:456
  21.4 0.9 %shard_map.70 = (bf16[128,1536]{1,0:T(8,128)(2,1)S(1)}, bf16[128,1536]{1,0:T(8,128)(2,1)S(1)}, f32[1920,128]{1,0:T(8,128)S(1)}) custom-call(s32[3,8]{1,0:T(4,128)S(4)} %get-tuple-element.31.table, f32[1920,128]{1,0:T(8,128)S(1)} %get-tuple-element.47.attn, f32[4,48,128]{2,1,0:T(8,128)S(1)} %get-tuple-element.52.found, ...), custom_call_target="tpu_custom_call", output_to_operand_aliasing={{2}: (1, {})} | custom-call | tf_op jit(solution)/shard_map/pallas_call | solution.py:317
  22.2 0.4 %collective-permute-start.7 = (bf16[128,1536]{1,0:T(8,128)(2,1)S(1)}, bf16[128,1536]{1,0:T(8,128)(2,1)S(1)}, u32[]{:S(2)}, u32[]{:S(2)}) collective-permute-start(bf16[128,1536]{1,0:T(8,128)(2,1)S(1)} %get-tuple-element.56), channel_id=1, source_target_pairs={{0,1},{1,0},{2,3},{3,2},{4,5},{5,4},{6,7},{7,6},{8,9},{9,8},{10,11... | collective-permute-start | bytes 1179656 | tf_op jit(solution)/shard_map/ppermute | solution.py:468
  22.7 0.8 %shard_map.71.own = f32[128,1536]{1,0:T(8,128)S(1)} custom-call(bf16[128,1536]{1,0:T(8,128)(2,1)S(1)} %get-tuple-element.55.lhs, bf16[1536,1536]{1,0:T(8,128)(2,1)S(1)} %get-tuple-element.48.after.weight), custom_call_target="tpu_custom_call" | custom-call | flops 603979776 | bytes 6291456 | tf_op jit(solution)/shard_map/pallas_call | solution.py:317
  23.5 0.6 %collective-permute-done.7.others = bf16[128,1536]{1,0:T(8,128)(2,1)S(1)} collective-permute-done((bf16[128,1536]{1,0:T(8,128)(2,1)S(1)}, bf16[128,1536]{1,0:T(8,128)(2,1)S(1)}, u32[]{:S(2)}, u32[]{:S(2)}) %collective-permute-start.7) | collective-permute-done | bytes 393248 | tf_op jit(solution)/shard_map/ppermute | solution.py:468
  24.0 0.8 %shard_map.72 = bf16[128,1536]{1,0:T(8,128)(2,1)} custom-call(f32[128,1536]{1,0:T(8,128)S(1)} %shard_map.71.own, bf16[128,1536]{1,0:T(8,128)(2,1)S(1)} %collective-permute-done.7.others), custom_call_target="tpu_custom_call" | custom-call | tf_op jit(solution)/shard_map/pallas_call | solution.py:317
  (1 shorter events, 0.0 us)
Async XLA Ops:
  2.1 1.4 %collective-permute-start = (bf16[3,48,128]{2,1,0:T(8,128)(2,1)S(1)}, bf16[3,48,128]{2,1,0:T(8,128)(2,1)S(1)}, u32[]{:S(2)}, u32[]{:S(2)}) collective-permute-start(bf16[3,48,128]{2,1,0:T(8,128)(2,1)S(1)} %get-tuple-element.33), channel_id=1, source_target_pairs={{0,1},{1,0},{2,3},{3,2},{4,5},{5,4},{6,7},{7,6},{8,9},{9,8},{10,11... | collective-permute-start | bytes 110600 | tf_op jit(solution)/shard_map/ppermute | solution.py:382
  3.5 10.1 %collective-permute-start.1 = (bf16[128,128]{1,0:T(8,128)(2,1)S(1)}, bf16[128,128]{1,0:T(8,128)(2,1)S(1)}, u32[]{:S(2)}, u32[]{:S(2)}) collective-permute-start(bf16[128,128]{1,0:T(8,128)(2,1)S(1)} %get-tuple-element.38.after), channel_id=1, source_target_pairs={{0,8},{1,11},{2,10},{3,9},{4,12},{5,15},{6,14},{7,13},{8,0},{9,3},... | collective-permute-start | bytes 98312 | tf_op jit(solution)/shard_map/ppermute | solution.py:390
  7.5 11.8 %collective-permute-start.2 = (bf16[256,256]{1,0:T(8,128)(2,1)S(1)}, bf16[256,256]{1,0:T(8,128)(2,1)S(1)}, u32[]{:S(2)}, u32[]{:S(2)}) collective-permute-start(bf16[256,256]{1,0:T(8,128)(2,1)S(1)} %get-tuple-element.49), channel_id=1, source_target_pairs={{0,12},{1,15},{2,14},{3,13},{4,8},{5,11},{6,10},{7,9},{8,4},{9,7},... | collective-permute-start | bytes 393224 | tf_op jit(solution)/shard_map/ppermute | solution.py:390
  8.8 10.5 %collective-permute-start.4 = (bf16[256,256]{1,0:T(8,128)(2,1)S(1)}, bf16[256,256]{1,0:T(8,128)(2,1)S(1)}, u32[]{:S(2)}, u32[]{:S(2)}) collective-permute-start(bf16[256,256]{1,0:T(8,128)(2,1)S(1)} %get-tuple-element.50), channel_id=1, source_target_pairs={{0,4},{1,7},{2,6},{3,5},{4,0},{5,3},{6,2},{7,1},{8,12},{9,15},{10,... | collective-permute-start | bytes 393224 | tf_op jit(solution)/shard_map/ppermute | solution.py:390
  9.0 10.3 %collective-permute-start.5 = (bf16[256,256]{1,0:T(8,128)(2,1)S(1)}, bf16[256,256]{1,0:T(8,128)(2,1)S(1)}, u32[]{:S(2)}, u32[]{:S(2)}) collective-permute-start(bf16[256,256]{1,0:T(8,128)(2,1)S(1)} %get-tuple-element.51), channel_id=1, source_target_pairs={{0,2},{1,3},{2,0},{3,1},{4,6},{5,7},{6,4},{7,5},{8,10},{9,11},{10,... | collective-permute-start | bytes 393224 | tf_op jit(solution)/shard_map/ppermute | solution.py:390
  14.1 5.2 %collective-permute-start.3 = (bf16[96,128]{1,0:T(8,128)(2,1)S(1)}, bf16[96,128]{1,0:T(8,128)(2,1)S(1)}, u32[]{:S(2)}, u32[]{:S(2)}) collective-permute-start(bf16[96,128]{1,0:T(8,128)(2,1)S(1)} %shard_map.67.after), channel_id=1, source_target_pairs={{0,8},{1,11},{2,10},{3,9},{4,12},{5,15},{6,14},{7,13},{8,0},{9,3},... | collective-permute-start | bytes 73736 | tf_op jit(solution)/shard_map/ppermute | solution.py:390
  19.9 1.5 %collective-permute-start.6 = (bf16[3,48,128]{2,1,0:T(8,128)(2,1)S(1)}, bf16[3,48,128]{2,1,0:T(8,128)(2,1)S(1)}, u32[]{:S(2)}, u32[]{:S(2)}) collective-permute-start(bf16[3,48,128]{2,1,0:T(8,128)(2,1)S(1)} %get-tuple-element.53), channel_id=1, source_target_pairs={{0,1},{1,0},{2,3},{3,2},{4,5},{5,4},{6,7},{7,6},{8,9},{9,8},{10,11... | collective-permute-start | bytes 110600 | tf_op jit(solution)/shard_map/ppermute | solution.py:456
  22.2 1.8 %collective-permute-start.7 = (bf16[128,1536]{1,0:T(8,128)(2,1)S(1)}, bf16[128,1536]{1,0:T(8,128)(2,1)S(1)}, u32[]{:S(2)}, u32[]{:S(2)}) collective-permute-start(bf16[128,1536]{1,0:T(8,128)(2,1)S(1)} %get-tuple-element.56), channel_id=1, source_target_pairs={{0,1},{1,0},{2,3},{3,2},{4,5},{5,4},{6,7},{7,6},{8,9},{9,8},{10,11... | collective-permute-start | bytes 1179656 | tf_op jit(solution)/shard_map/ppermute | solution.py:468

commit v10 on v8

--- a/solution.py
+++ b/solution.py
@@ -389,7 +389,7 @@
         aliases={3 + n: n for n in range(len(kept))},
     )
     blocks = [None] * ops
-    for i, block in reversed(list(zip(kept, handed))):
+    for i, block in zip(kept, handed):
         blocks[i] = exchange(i, block)
     asking = [exchange(i, question) for i, question in zip(asked, handed[len(kept) :])]
     answers = call(

time: 25.4 us -> 25.4 us (level)
  no operation moved by 1% of the time
where the time goes in v10:
time: 25.4 us; the launch traced here: 25.2 us
  starting transfers between devices  10.8 us (43%)
  Pallas kernels  9.39 us (37%)
  waiting for transfers between devices  4.93 us (19%)
    ppermute x5, starting transfers between devices, exchange(): return lax.ppermute(array, ('inst', 'tp'), pairs)  9.75 us
    pallas_call x8, Pallas kernels, call(): pl.pallas_call(kernel, out_shape=[space(shape.shape, shape.dtype) for spa...  9.39 us
    ppermute x5, waiting for transfers between devices, exchange(): return lax.ppermute(array, ('inst', 'tp'), pairs)  2.1 us
    ppermute x1, waiting for transfers between devices, body(): arrived = lax.ppermute(sent, 'tp', swap)  1.2 us
    ppermute x1, waiting for transfers between devices, body(): peer_q = lax.ppermute(sent_q, 'tp', swap)  0.87 us
    ppermute x1, waiting for transfers between devices, body(): others = lax.ppermute(partial, 'tp', swap)  0.77 us
    ppermute x1, starting transfers between devices, body(): peer_q = lax.ppermute(sent_q, 'tp', swap)  0.74 us
  transfers between devices with their start and end apart: 8, of which 4 were waited for; matrix products, arithmetic and copies ran while one was open for 0% of the time, Pallas kernels for 20%

profile of v10, /device:TPU:9, one launch (start us, length us, event | category | flops | bytes accessed | tf_op | source)
XLA Modules:
  0.0 25.2 jit_solution(6367247317779634757)
XLA Ops:
  0.0 2.1 %shard_map.64 = (s32[3,8]{1,0:T(4,128)S(4)}, s32[2,32]{1,0:T(2,128)S(4)}, bf16[6144,256]{1,0:T(8,128)(2,1)S(1)}, f32[1920,128]{1,0:T(8,128)S(1)}, bf16[128,256]{...) custom-call(s32[8,32]{1,0:T(8,128)} %anchor_h.1, ...), custom_call_target="tpu_custom_call" | custom-call | tf_op jit(solution)/shard_map/pallas_call | solution.py:308
  2.1 0.7 %collective-permute-start = (bf16[3,48,128]{2,1,0:T(8,128)(2,1)S(1)}, bf16[3,48,128]{2,1,0:T(8,128)(2,1)S(1)}, u32[]{:S(2)}, u32[]{:S(2)}) collective-permute-start(bf16[3,48,128]{2,1,0:T(8,128)(2,1)S(1)} %get-tuple-element.30), channel_id=1, source_target_pairs={{0,1},{1,0},{2,3},{3,2},{4,5},{5,4},{6,7},{7,6},{8,9},{9,8},{10,11... | collective-permute-start | bytes 110600 | tf_op jit(solution)/shard_map/ppermute | solution.py:373
  2.9 0.9 %collective-permute-done.peer_q = bf16[3,48,128]{2,1,0:T(8,128)(2,1)S(1)} collective-permute-done((bf16[3,48,128]{2,1,0:T(8,128)(2,1)S(1)}, bf16[3,48,128]{2,1,0:T(8,128)(2,1)S(1)}, u32[]{:S(2)}, u32[]{:S(2)}) %collective-permute-start) | collective-permute-done | bytes 36896 | tf_op jit(solution)/shard_map/ppermute | solution.py:373
  3.8 3.3 %collective-permute-start.1 = (bf16[128,128]{1,0:T(8,128)(2,1)S(1)}, bf16[128,128]{1,0:T(8,128)(2,1)S(1)}, u32[]{:S(2)}, u32[]{:S(2)}) collective-permute-start(bf16[128,128]{1,0:T(8,128)(2,1)S(1)} %get-tuple-element.35), channel_id=1, source_target_pairs={{0,8},{1,11},{2,10},{3,9},{4,12},{5,15},{6,14},{7,13},{8,0},{9,3},... | collective-permute-start | bytes 98312 | tf_op jit(solution)/shard_map/ppermute | solution.py:381
  7.0 0.0 collective-permute-start.2
  7.0 2.1 %collective-permute-start.4 = (bf16[256,256]{1,0:T(8,128)(2,1)S(1)}, bf16[256,256]{1,0:T(8,128)(2,1)S(1)}, u32[]{:S(2)}, u32[]{:S(2)}) collective-permute-start(bf16[256,256]{1,0:T(8,128)(2,1)S(1)} %get-tuple-element.44), channel_id=1, source_target_pairs={{0,4},{1,7},{2,6},{3,5},{4,0},{5,3},{6,2},{7,1},{8,12},{9,15},{10,... | collective-permute-start | bytes 393224 | tf_op jit(solution)/shard_map/ppermute | solution.py:381
  9.2 0.2 collective-permute-start.5
  9.4 2.1 %collective-permute-done.1.refs_0_ = bf16[128,128]{1,0:T(8,128)(2,1)S(1)} collective-permute-done((bf16[128,128]{1,0:T(8,128)(2,1)S(1)}, bf16[128,128]{1,0:T(8,128)(2,1)S(1)}, u32[]{:S(2)}, u32[]{:S(2)}) %collective-permute-start.1) | collective-permute-done | bytes 32800 | tf_op jit(solution)/shard_map/ppermute | solution.py:381
  11.5 0.5 %shard_map.66.after = bf16[96,128]{1,0:T(8,128)(2,1)S(1)} custom-call(s32[3,8]{1,0:T(4,128)S(4)} %get-tuple-element.28.table, bf16[128,128]{1,0:T(8,128)(2,1)S(1)} %collective-permute-done.1.refs_0_, bf16[256,256]{1,0:T(8,128)(2,1)S(1)} %get-tuple-element.36.refs_1_), custom_call_target="tpu_custom_call" | custom-call | tf_op jit(solution)/shard_map/pallas_call | solution.py:308
  11.9 4.1 %collective-permute-start.3 = (bf16[96,128]{1,0:T(8,128)(2,1)S(1)}, bf16[96,128]{1,0:T(8,128)(2,1)S(1)}, u32[]{:S(2)}, u32[]{:S(2)}) collective-permute-start(bf16[96,128]{1,0:T(8,128)(2,1)S(1)} %shard_map.66.after), channel_id=1, source_target_pairs={{0,8},{1,11},{2,10},{3,9},{4,12},{5,15},{6,14},{7,13},{8,0},{9,3},... | collective-permute-start | bytes 73736 | tf_op jit(solution)/shard_map/ppermute | solution.py:381
  16.1 3.8 %shard_map.67 = (f32[1920,128]{1,0:T(8,128)S(1)}, bf16[1536,1536]{1,0:T(8,128)(2,1)S(1)}, bf16[1536,1536]{1,0:T(8,128)(2,1)S(1)}) custom-call(bf16[96,128]{1,0:T(8,128)(2,1)S(1)} %shard_map.66.after, s32[2,32]{1,0:T(2,128)S(4)} %get-tuple-element.37.lists, f32[1920,128]{1,0:T(8,128)S(1)} %get-tuple-element.38.spread, ...), custom_call_target="tpu_custom_call" | custom-call | flops 10066329600 | bytes 20971520 | tf_op jit(solution)/shard_map/pallas_call | solution.py:308
  19.9 0.0 collective-permute-done.3.refs_1_
  19.9 0.0 collective-permute-done.2.refs_0_
  19.9 0.0 collective-permute-done.4.refs_2_
  19.9 0.0 collective-permute-done.5.refs_3_
  19.9 0.5 %shard_map.68 = (f32[4,48,128]{2,1,0:T(8,128)S(1)}, bf16[3,48,128]{2,1,0:T(8,128)(2,1)S(1)}) custom-call(bf16[1536,1536]{1,0:T(8,128)(2,1)S(1)} %get-tuple-element.42.after.weight, s32[3,8]{1,0:T(4,128)S(4)} %get-tuple-element.28.table, bf16[4,48,128]{2,1,0:T(8,128)(2,1)S(1)} %get-tuple-element.29.own_q, ...), custom_call_target="tpu_custom_call" | custom-call | tf_op jit(solution)/shard_map/pallas_call | solution.py:308
  20.5 0.1 collective-permute-start.6
  20.5 1.2 %collective-permute-done.6.arrived = bf16[3,48,128]{2,1,0:T(8,128)(2,1)S(1)} collective-permute-done((bf16[3,48,128]{2,1,0:T(8,128)(2,1)S(1)}, bf16[3,48,128]{2,1,0:T(8,128)(2,1)S(1)}, u32[]{:S(2)}, u32[]{:S(2)}) %collective-permute-start.6) | collective-permute-done | bytes 36896 | tf_op jit(solution)/shard_map/ppermute | solution.py:431
  21.7 0.9 %shard_map.69 = (bf16[128,1536]{1,0:T(8,128)(2,1)S(1)}, bf16[128,1536]{1,0:T(8,128)(2,1)S(1)}, f32[1920,128]{1,0:T(8,128)S(1)}) custom-call(s32[3,8]{1,0:T(4,128)S(4)} %get-tuple-element.28.table, f32[1920,128]{1,0:T(8,128)S(1)} %get-tuple-element.41.attn, f32[4,48,128]{2,1,0:T(8,128)S(1)} %get-tuple-element.46.found, ...), custom_call_target="tpu_custom_call", output_to_operand_aliasing={{2}: (1, {})} | custom-call | tf_op jit(solution)/shard_map/pallas_call | solution.py:308
  22.6 0.2 collective-permute-start.7
  22.8 0.8 %shard_map.70.own = f32[128,1536]{1,0:T(8,128)S(1)} custom-call(bf16[128,1536]{1,0:T(8,128)(2,1)S(1)} %get-tuple-element.49.lhs, bf16[1536,1536]{1,0:T(8,128)(2,1)S(1)} %get-tuple-element.42.after.weight), custom_call_target="tpu_custom_call" | custom-call | flops 603979776 | bytes 6291456 | tf_op jit(solution)/shard_map/pallas_call | solution.py:308
  23.6 0.8 %collective-permute-done.7.others = bf16[128,1536]{1,0:T(8,128)(2,1)S(1)} collective-permute-done((bf16[128,1536]{1,0:T(8,128)(2,1)S(1)}, bf16[128,1536]{1,0:T(8,128)(2,1)S(1)}, u32[]{:S(2)}, u32[]{:S(2)}) %collective-permute-start.7) | collective-permute-done | bytes 393248 | tf_op jit(solution)/shard_map/ppermute | solution.py:443
  24.4 0.8 %shard_map.71 = bf16[128,1536]{1,0:T(8,128)(2,1)} custom-call(f32[128,1536]{1,0:T(8,128)S(1)} %shard_map.70.own, bf16[128,1536]{1,0:T(8,128)(2,1)S(1)} %collective-permute-done.7.others), custom_call_target="tpu_custom_call" | custom-call | tf_op jit(solution)/shard_map/pallas_call | solution.py:308
  (1 shorter events, 0.0 us)
Async XLA Ops:
  2.1 1.6 %collective-permute-start = (bf16[3,48,128]{2,1,0:T(8,128)(2,1)S(1)}, bf16[3,48,128]{2,1,0:T(8,128)(2,1)S(1)}, u32[]{:S(2)}, u32[]{:S(2)}) collective-permute-start(bf16[3,48,128]{2,1,0:T(8,128)(2,1)S(1)} %get-tuple-element.30), channel_id=1, source_target_pairs={{0,1},{1,0},{2,3},{3,2},{4,5},{5,4},{6,7},{7,6},{8,9},{9,8},{10,11... | collective-permute-start | bytes 110600 | tf_op jit(solution)/shard_map/ppermute | solution.py:373
  3.8 7.7 %collective-permute-start.1 = (bf16[128,128]{1,0:T(8,128)(2,1)S(1)}, bf16[128,128]{1,0:T(8,128)(2,1)S(1)}, u32[]{:S(2)}, u32[]{:S(2)}) collective-permute-start(bf16[128,128]{1,0:T(8,128)(2,1)S(1)} %get-tuple-element.35), channel_id=1, source_target_pairs={{0,8},{1,11},{2,10},{3,9},{4,12},{5,15},{6,14},{7,13},{8,0},{9,3},... | collective-permute-start | bytes 98312 | tf_op jit(solution)/shard_map/ppermute | solution.py:381
  7.0 12.9 %collective-permute-start.2 = (bf16[256,256]{1,0:T(8,128)(2,1)S(1)}, bf16[256,256]{1,0:T(8,128)(2,1)S(1)}, u32[]{:S(2)}, u32[]{:S(2)}) collective-permute-start(bf16[256,256]{1,0:T(8,128)(2,1)S(1)} %get-tuple-element.43), channel_id=1, source_target_pairs={{0,12},{1,15},{2,14},{3,13},{4,8},{5,11},{6,10},{7,9},{8,4},{9,7},... | collective-permute-start | bytes 393224 | tf_op jit(solution)/shard_map/ppermute | solution.py:381
  7.0 12.9 %collective-permute-start.4 = (bf16[256,256]{1,0:T(8,128)(2,1)S(1)}, bf16[256,256]{1,0:T(8,128)(2,1)S(1)}, u32[]{:S(2)}, u32[]{:S(2)}) collective-permute-start(bf16[256,256]{1,0:T(8,128)(2,1)S(1)} %get-tuple-element.44), channel_id=1, source_target_pairs={{0,4},{1,7},{2,6},{3,5},{4,0},{5,3},{6,2},{7,1},{8,12},{9,15},{10,... | collective-permute-start | bytes 393224 | tf_op jit(solution)/shard_map/ppermute | solution.py:381
  9.2 10.7 %collective-permute-start.5 = (bf16[256,256]{1,0:T(8,128)(2,1)S(1)}, bf16[256,256]{1,0:T(8,128)(2,1)S(1)}, u32[]{:S(2)}, u32[]{:S(2)}) collective-permute-start(bf16[256,256]{1,0:T(8,128)(2,1)S(1)} %get-tuple-element.45), channel_id=1, source_target_pairs={{0,2},{1,3},{2,0},{3,1},{4,6},{5,7},{6,4},{7,5},{8,10},{9,11},{10,... | collective-permute-start | bytes 393224 | tf_op jit(solution)/shard_map/ppermute | solution.py:381
  11.9 7.9 %collective-permute-start.3 = (bf16[96,128]{1,0:T(8,128)(2,1)S(1)}, bf16[96,128]{1,0:T(8,128)(2,1)S(1)}, u32[]{:S(2)}, u32[]{:S(2)}) collective-permute-start(bf16[96,128]{1,0:T(8,128)(2,1)S(1)} %shard_map.66.after), channel_id=1, source_target_pairs={{0,8},{1,11},{2,10},{3,9},{4,12},{5,15},{6,14},{7,13},{8,0},{9,3},... | collective-permute-start | bytes 73736 | tf_op jit(solution)/shard_map/ppermute | solution.py:381
  20.5 1.3 %collective-permute-start.6 = (bf16[3,48,128]{2,1,0:T(8,128)(2,1)S(1)}, bf16[3,48,128]{2,1,0:T(8,128)(2,1)S(1)}, u32[]{:S(2)}, u32[]{:S(2)}) collective-permute-start(bf16[3,48,128]{2,1,0:T(8,128)(2,1)S(1)} %get-tuple-element.47), channel_id=1, source_target_pairs={{0,1},{1,0},{2,3},{3,2},{4,5},{5,4},{6,7},{7,6},{8,9},{9,8},{10,11... | collective-permute-start | bytes 110600 | tf_op jit(solution)/shard_map/ppermute | solution.py:431
  22.6 1.8 %collective-permute-start.7 = (bf16[128,1536]{1,0:T(8,128)(2,1)S(1)}, bf16[128,1536]{1,0:T(8,128)(2,1)S(1)}, u32[]{:S(2)}, u32[]{:S(2)}) collective-permute-start(bf16[128,1536]{1,0:T(8,128)(2,1)S(1)} %get-tuple-element.50), channel_id=1, source_target_pairs={{0,1},{1,0},{2,3},{3,2},{4,5},{5,4},{6,7},{7,6},{8,9},{9,8},{10,11... | collective-permute-start | bytes 1179656 | tf_op jit(solution)/shard_map/ppermute | solution.py:443

commit v11 on v10

--- a/solution.py
+++ b/solution.py
@@ -13,7 +13,7 @@
 MAXB = 2
 WIN = MAXB * BLK
 PAD = 8
-FEW = 16
+PARTS = 4
 MIB = 1024 * 1024
 
 
@@ -28,24 +28,17 @@
     return copies
 
 
-def plan_kernel(
-    ops, asked, stride, anchor_h, lengths_h, queries_h, fresh_h, pool_h,
-    table, lists, pool, spread, fresh, own_q, sent_q, asked_f, *refs,
-):
-    sends, (anchor, lengths, offs, queries, keys, values, few, sems) = refs[:ops], refs[ops:]
+def plan_kernel(ops, anchor_h, lengths_h, pool_h, table, lists, pool, *refs):
+    sends, (anchor, lengths, offs, sems) = refs[:ops], refs[ops:]
     insts, slots = anchor.shape
-    steps, _, width = queries.shape
-    heads = width // HDIM
-    rows = steps * heads
     blocks = pool.shape[0] // BLK
     own, core = lax.axis_index("inst"), lax.axis_index("tp")
+    part = pool.shape[0] // PARTS
     loads = start_copies(
-        [
-            (anchor_h, anchor),
-            (lengths_h, lengths),
-            (queries_h, queries),
-            (fresh_h, fresh),
-            (pool_h, pool),
+        [(anchor_h, anchor), (lengths_h, lengths)]
+        + [
+            (pool_h.at[pl.ds(n * part, part)], pool.at[pl.ds(n * part, part)])
+            for n in range(PARTS)
         ],
         sems,
     )
@@ -54,7 +47,6 @@
     for m in range(insts):
         table[0, m] = slots
         table[1, m] = 1
-        table[2, m] = 1
         offs[m] = 0
     longer = blocks - slots
     start, found = jnp.int32(0), jnp.int32(0)
@@ -63,14 +55,31 @@
         dest = (2 * own - source) & (insts - 1)
         table[0, own ^ source] = j
         table[1, own ^ source] = lengths[source, j]
-        table[2, own ^ dest] = count
         offs[own ^ dest] = start
         place = jnp.where(count > 1, found, longer + j - found)
         lists[0, place] = j
         lists[1, place] = start
         start = start + count
         found = found + count - 1
-    loads[2].wait()
+    for load in loads[2:]:
+        load.wait()
+    for i in range(ops):
+        at = offs[partner(insts, ops, i, core)]
+        for b in range(MAXB):
+            row = pl.multiple_of(jnp.minimum(at + b, blocks - 1) * BLK, BLK)
+            sends[i][b * BLK : (b + 1) * BLK, :] = pool[pl.ds(row, BLK), :]
+
+
+def query_kernel(
+    stride, ops, table, queries_h, fresh_h, spread, fresh, own_q, sent_q, queries, sems
+):
+    steps, slots, width = queries.shape
+    insts = table.shape[1]
+    heads = width // HDIM
+    rows = steps * heads
+    core = lax.axis_index("tp")
+    loads = start_copies([(queries_h, queries), (fresh_h, fresh)], sems)
+    loads[0].wait()
     for s in range(steps):
         for h in range(heads):
             spread[pl.ds((s * heads + h) * stride, slots), :] = queries[
@@ -82,59 +91,7 @@
     for i in range(ops - 1):
         j = table[0, partner(insts, ops, i, 1 - core)]
         sent_q[i] = spread[pl.ds(j, rows, stride=stride), :].astype(jnp.bfloat16)
-    loads[3].wait()
-    keys[0 : steps * slots, :] = fresh[:, :HDIM].astype(jnp.float32)
-    values[0 : steps * slots, :] = fresh[:, HDIM:].astype(jnp.float32)
-    few[...] = jnp.zeros_like(few)
-    for n, i in enumerate(asked):
-        j = table[0, partner(insts, ops, i, core)]
-        for u in range(steps):
-            few[u : u + 1, :] = keys[pl.ds(u * slots + j, 1), :]
-            few[FEW + u : FEW + u + 1, :] = values[pl.ds(u * slots + j, 1), :]
-        asked_f[n] = few[...].astype(jnp.bfloat16)
-    loads[4].wait()
-    for i in range(ops):
-        at = offs[partner(insts, ops, i, core)]
-        for b in range(MAXB):
-            row = pl.multiple_of(jnp.minimum(at + b, blocks - 1) * BLK, BLK)
-            sends[i][b * BLK : (b + 1) * BLK, :] = pool[pl.ds(row, BLK), :]
-
-
-def ask_kernel(asked, own_q, peer_q, asked_f, *refs):
-    outs = refs[-len(asked) :]
-    rows = own_q.shape[1]
-    for n, i in enumerate(asked):
-        outs[n][0:rows, :] = own_q[i]
-        outs[n][rows : 2 * rows, :] = peer_q[i]
-        outs[n][2 * rows :, :] = asked_f[n]
-
-
-def answer_kernel(ops, asked, steps, table, *refs):
-    count = len(asked)
-    questions, windows, outs = refs[:count], refs[count : 2 * count], refs[2 * count :]
-    rows = outs[0].shape[0]
-    heads = rows // 2 // steps
-    insts = table.shape[1]
-    core = lax.axis_index("tp")
-    step = lax.broadcasted_iota(jnp.int32, (rows, HDIM), 0) // heads % steps
-    col = lax.broadcasted_iota(jnp.int32, (rows, HDIM), 1)
-    within = lax.broadcasted_iota(jnp.int32, (rows, WIN), 1)
-    empty = jnp.zeros((HDIM - FEW, HDIM), jnp.bfloat16)
-    scores, recents, lates = [], [], []
-    for n, i in enumerate(asked):
-        limit = table[2, partner(insts, ops, i, core)] * BLK
-        query = questions[n][0:rows, :]
-        score = contract_last(query, windows[n][:, :HDIM])
-        scores.append(jnp.where(within < limit, score, -jnp.inf))
-        keys = jnp.concatenate([questions[n][rows : rows + FEW, :], empty])
-        lates.append(jnp.concatenate([questions[n][rows + FEW :, :], empty]))
-        recents.append(jnp.where(col <= step, contract_last(query, keys), -jnp.inf))
-    done = attend_all(scores, recents, [window[:, HDIM:] for window in windows])
-    for n, (mixed, weight) in enumerate(done):
-        out = mixed + jnp.dot(
-            weight.astype(jnp.bfloat16), lates[n], preferred_element_type=jnp.float32
-        )
-        outs[n][...] = out.astype(jnp.bfloat16)
+    loads[1].wait()
 
 
 def contract_last(a, b):
@@ -183,7 +140,7 @@
 
 
 def stay_kernel(
-    stride, steps, group, after, lists, spread, pool, fresh, weight_h,
+    stride, steps, group, lists, spread, pool, fresh, weight_h,
     attn, peer_w, own_w, recent, late, sems,
 ):
     slots = lists.shape[1]
@@ -216,8 +173,7 @@
         load.wait()
 
 
-def move_kernel(ops, asked, steps, slots, group, after, table, own_q, peer_q, fresh, *refs):
-    blocks, (found, sent) = refs[:ops], refs[ops:]
+def recent_kernel(ops, steps, slots, after, table, own_q, peer_q, fresh, query, recent):
     rows = own_q.shape[1]
     heads = rows // steps
     insts = table.shape[1]
@@ -226,28 +182,31 @@
     step = lax.broadcasted_iota(jnp.int32, shape, 0) // heads % steps
     col = lax.broadcasted_iota(jnp.int32, shape, 1)
     owner = jnp.where(col // slots <= step, col % slots, -1)
+    for i in range(ops):
+        count = 2 * rows if i < ops - 1 else rows
+        query[i, 0:rows, :] = own_q[i]
+        if i < ops - 1:
+            query[i, rows:, :] = peer_q[i]
+        score = contract_last(query[i, 0:count, :], fresh[:, :HDIM])
+        j = table[0, partner(insts, ops, i, core)]
+        recent[i, 0:count, :] = jnp.where(owner[:count] == j, score, -jnp.inf)
+
+
+def move_kernel(ops, table, query, recent, fresh, *refs):
+    blocks, (found, sent) = refs[:ops], refs[ops:]
+    rows = found.shape[1]
+    insts = table.shape[1]
+    core = lax.axis_index("tp")
     within = lax.broadcasted_iota(jnp.int32, (2 * rows, WIN), 1)
-    for i in asked:
-        found[i] = blocks[i][0:rows, :].astype(jnp.float32)
-        sent[i] = blocks[i][rows : 2 * rows, :]
-    moved = [i for i in range(ops) if i not in asked]
-    for first in range(0, len(moved), group):
-        batch = moved[first : first + group]
-        queries, recents, scores = [], [], []
-        for i in batch:
-            query = own_q[i]
-            if i < ops - 1:
-                query = jnp.concatenate([query, peer_q[i]])
-            queries.append(query)
-        for i, query in zip(batch, queries):
-            m = partner(insts, ops, i, core)
-            score = contract_last(query, blocks[i][:, :HDIM])
-            limit = table[1, m] * BLK
-            scores.append(jnp.where(within[: query.shape[0]] < limit, score, -jnp.inf))
-        for i, query in zip(batch, queries):
-            recent = contract_last(query, fresh[:, :HDIM])
-            j = table[0, partner(insts, ops, i, core)]
-            recents.append(jnp.where(owner[: query.shape[0]] == j, recent, -jnp.inf))
+    for first in range(0, ops, 4):
+        batch = range(first, min(first + 4, ops))
+        counts = [2 * rows if i < ops - 1 else rows for i in batch]
+        scores = []
+        for i, count in zip(batch, counts):
+            score = contract_last(query[i, 0:count, :], blocks[i][:, :HDIM])
+            limit = table[1, partner(insts, ops, i, core)] * BLK
+            scores.append(jnp.where(within[:count] < limit, score, -jnp.inf))
+        recents = [recent[i, 0:count, :] for i, count in zip(batch, counts)]
         done = attend_all(scores, recents, [blocks[i][:, HDIM:] for i in batch])
         for i, (mixed, weight) in zip(batch, done):
             out = mixed + jnp.dot(
@@ -337,80 +296,49 @@
     def f32(*shape):
         return jax.ShapeDtypeStruct(shape, jnp.float32)
 
-    asked = (1,)
-    table, lists, pool, spread, fresh, own_q, sent_q, asked_f, *sends = call(
-        functools.partial(plan_kernel, ops, asked, stride),
+    table, lists, pool, *sends = call(
+        functools.partial(plan_kernel, ops),
+        [(hbm, anchor), (hbm, lengths), (hbm, cache_pool)],
         [
-            (hbm, anchor),
-            (hbm, lengths),
-            (hbm, queries),
-            (hbm, new_kv.reshape(steps * slots, kvw)),
-            (hbm, cache_pool),
-        ],
-        [
-            (smem, jax.ShapeDtypeStruct((3, insts), jnp.int32)),
+            (smem, jax.ShapeDtypeStruct((2, insts), jnp.int32)),
             (smem, jax.ShapeDtypeStruct((2, slots), jnp.int32)),
             (vmem, bf16(*cache_pool.shape)),
-            (vmem, f32(rows * stride, HDIM)),
-            (vmem, bf16(steps * slots, kvw)),
-            (vmem, bf16(ops, rows, HDIM)),
-            (vmem, bf16(ops - 1, rows, HDIM)),
-            (vmem, bf16(len(asked), 2 * FEW, HDIM)),
         ]
         + [(vmem, bf16(WIN, kvw))] * ops,
         [
             smem(anchor.shape, jnp.int32),
             smem(lengths.shape, jnp.int32),
             smem((insts,), jnp.int32),
-            vmem(queries.shape, jnp.bfloat16),
-            vmem((steps * slots + PAD, HDIM), jnp.float32),
-            vmem((steps * slots + PAD, HDIM), jnp.float32),
-            vmem((2 * FEW, HDIM), jnp.float32),
-            dma((5,)),
+            dma((2 + PARTS,)),
         ],
     )
-    swap = [(c, cores - 1 - c) for c in range(cores)]
-    peer_q = lax.ppermute(sent_q, "tp", swap)
-
-    def exchange(i, array):
+    blocks = [None] * ops
+    for i in reversed(range(ops)):
         pairs = []
         for a in range(insts):
             for c in range(cores):
                 m = 1 if i == ops - 1 else insts - 2 - 2 * i + c
                 pairs.append((a * cores + c, (a ^ m) * cores + c))
-        return lax.ppermute(array, ("inst", "tp"), pairs)
-
-    kept = [i for i in range(ops) if i not in asked]
-    handed = call(
-        functools.partial(ask_kernel, asked),
-        [(vmem, own_q), (vmem, peer_q), (vmem, asked_f)] + [(vmem, sends[i]) for i in kept],
-        [(vmem, bf16(WIN, kvw))] * len(kept)
-        + [(vmem, bf16(2 * rows + 2 * FEW, HDIM))] * len(asked),
-        aliases={3 + n: n for n in range(len(kept))},
-    )
-    blocks = [None] * ops
-    for i, block in zip(kept, handed):
-        blocks[i] = exchange(i, block)
-    asking = [exchange(i, question) for i, question in zip(asked, handed[len(kept) :])]
-    answers = call(
-        functools.partial(answer_kernel, ops, asked, steps),
-        [(smem, table)]
-        + [(vmem, question) for question in asking]
-        + [(vmem, sends[i]) for i in asked],
-        [(vmem, bf16(2 * rows, HDIM))] * len(asked),
-    )
-    for i, answer in zip(asked, answers):
-        blocks[i] = exchange(i, answer)
+        blocks[i] = lax.ppermute(sends[i], ("inst", "tp"), pairs)
+
+    spread, fresh, own_q, sent_q = call(
+        functools.partial(query_kernel, stride, ops),
+        [(smem, table), (hbm, queries), (hbm, new_kv.reshape(steps * slots, kvw))],
+        [
+            (vmem, f32(rows * stride, HDIM)),
+            (vmem, bf16(steps * slots, kvw)),
+            (vmem, bf16(ops, rows, HDIM)),
+            (vmem, bf16(ops - 1, rows, HDIM)),
+        ],
+        [vmem(queries.shape, jnp.bfloat16), dma((2,))],
+        cost=pl.CostEstimate(flops=0, bytes_accessed=MIB, transcendentals=0),
+    )
+    swap = [(c, cores - 1 - c) for c in range(cores)]
+    peer_q = lax.ppermute(sent_q, "tp", swap)
+
     attn, peer_w, own_w = call(
         functools.partial(stay_kernel, stride, steps, 8),
-        [
-            (vmem, answers[0]),
-            (smem, lists),
-            (vmem, spread),
-            (vmem, pool),
-            (vmem, fresh),
-            (hbm, out_weight),
-        ],
+        [(smem, lists), (vmem, spread), (vmem, pool), (vmem, fresh), (hbm, out_weight)],
         [(vmem, f32(rows * stride, HDIM))] + [(vmem, bf16(depth, half))] * 2,
         [
             vmem((rows * stride, HDIM), jnp.float32),
@@ -418,13 +346,17 @@
             dma((2,)),
         ],
         cost=pl.CostEstimate(
-            flops=200 * slots * rows * WIN * HDIM, bytes_accessed=20 * MIB, transcendentals=0
+            flops=4 * slots * rows * WIN * HDIM, bytes_accessed=20 * MIB, transcendentals=0
         ),
     )
-
+    query, recent = call(
+        functools.partial(recent_kernel, ops, steps, slots),
+        [(vmem, own_w), (smem, table), (vmem, own_q), (vmem, peer_q), (vmem, fresh)],
+        [(vmem, bf16(ops, 2 * rows, HDIM)), (vmem, f32(ops, 2 * rows, steps * slots))],
+    )
     found, sent = call(
-        functools.partial(move_kernel, ops, asked, steps, slots, 4),
-        [(vmem, own_w), (smem, table), (vmem, own_q), (vmem, peer_q), (vmem, fresh)]
+        functools.partial(move_kernel, ops),
+        [(smem, table), (vmem, query), (vmem, recent), (vmem, fresh)]
         + [(vmem, block) for block in blocks],
         [(vmem, f32(ops, rows, HDIM)), (vmem, bf16(ops - 1, rows, HDIM))],
     )

time: 25.4 us -> 24.5 us (0.965)
  the two profiles are of different devices: /device:TPU:9 before, /device:TPU:0 now
where the time goes in v11:
time: 24.5 us; the launch traced here: 24.3 us
  Pallas kernels  9.99 us (41%)
  starting transfers between devices  7.79 us (32%)
  waiting for transfers between devices  6.47 us (26%)
    pallas_call x8, Pallas kernels, call(): pl.pallas_call(kernel, out_shape=[space(shape.shape, shape.dtype) for spa...  9.99 us
    ppermute x4, starting transfers between devices, body(): blocks[i] = lax.ppermute(sends[i], ('inst', 'tp'), pairs)  7.42 us
    ppermute x4, waiting for transfers between devices, body(): blocks[i] = lax.ppermute(sends[i], ('inst', 'tp'), pairs)  4.49 us
    ppermute x1, waiting for transfers between devices, body(): arrived = lax.ppermute(sent, 'tp', swap)  1.2 us
    ppermute x1, waiting for transfers between devices, body(): others = lax.ppermute(partial, 'tp', swap)  0.77 us
  transfers between devices with their start and end apart: 7, of which 3 were waited for; matrix products, arithmetic and copies ran while one was open for 0% of the time, Pallas kernels for 24%

profile of v11, /device:TPU:0, one launch (start us, length us, event | category | flops | bytes accessed | tf_op | source)
XLA Modules:
  0.0 24.3 jit_solution(6017767710071213501)
XLA Ops:
  0.0 1.9 %shard_map.64 = (s32[2,8]{1,0:T(2,128)S(4)}, s32[2,32]{1,0:T(2,128)S(4)}, bf16[6144,256]{1,0:T(8,128)(2,1)S(1)}, bf16[256,256]{1,0:T(8,128)(2,1)S(1)}, bf16[256,...) custom-call(s32[8,32]{1,0:T(8,128)} %anchor_h.1, s32[8,32]{1,0:T(8,128)} %lengths_h.1, ...), custom_call_target="tpu_custom_call" | custom-call | tf_op jit(solution)/shard_map/pallas_call | solution.py:267
  1.9 5.1 %collective-permute-start.1 = (bf16[256,256]{1,0:T(8,128)(2,1)S(1)}, bf16[256,256]{1,0:T(8,128)(2,1)S(1)}, u32[]{:S(2)}, u32[]{:S(2)}) collective-permute-start(bf16[256,256]{1,0:T(8,128)(2,1)S(1)} %get-tuple-element.36), channel_id=1, source_target_pairs={{0,12},{1,15},{2,14},{3,13},{4,8},{5,11},{6,10},{7,9},{8,4},{9,7},... | collective-permute-start | bytes 393224 | tf_op jit(solution)/shard_map/ppermute | solution.py:322
  7.1 0.0 collective-permute-start.2
  7.1 0.6 %collective-permute-start.3 = (bf16[256,256]{1,0:T(8,128)(2,1)S(1)}, bf16[256,256]{1,0:T(8,128)(2,1)S(1)}, u32[]{:S(2)}, u32[]{:S(2)}) collective-permute-start(bf16[256,256]{1,0:T(8,128)(2,1)S(1)} %get-tuple-element.38), channel_id=1, source_target_pairs={{0,4},{1,7},{2,6},{3,5},{4,0},{5,3},{6,2},{7,1},{8,12},{9,15},{10,... | collective-permute-start | bytes 393224 | tf_op jit(solution)/shard_map/ppermute | solution.py:322
  7.7 1.7 %collective-permute-start.4 = (bf16[256,256]{1,0:T(8,128)(2,1)S(1)}, bf16[256,256]{1,0:T(8,128)(2,1)S(1)}, u32[]{:S(2)}, u32[]{:S(2)}) collective-permute-start(bf16[256,256]{1,0:T(8,128)(2,1)S(1)} %get-tuple-element.39), channel_id=1, source_target_pairs={{0,2},{1,3},{2,0},{3,1},{4,6},{5,7},{6,4},{7,5},{8,10},{9,11},{10,... | collective-permute-start | bytes 393224 | tf_op jit(solution)/shard_map/ppermute | solution.py:322
  9.4 1.1 %shard_map.65 = (f32[1920,128]{1,0:T(8,128)S(1)}, bf16[128,256]{1,0:T(8,128)(2,1)S(1)}, bf16[4,48,128]{2,1,0:T(8,128)(2,1)S(1)}, bf16[3,48,128]{2,1,0:T(8,128)(2,1)S(1)}) custom-call(s32[2,8]{1,0:T(2,128)S(4)} %get-tuple-element.25.table, bf16[4,32,1536]{2,1,0:T(8,128)(2,1)} %queries_h.1, bf16[128,256]{1,0:T(8,128)(2,1)} %bitcast.2), custom_call_target="tpu_custom_call" | custom-call | bytes 1048576 | tf_op jit(solution)/shard_map/pallas_call | solution.py:267
  10.5 0.1 collective-permute-start
  10.6 3.8 %shard_map.66 = (f32[1920,128]{1,0:T(8,128)S(1)}, bf16[1536,1536]{1,0:T(8,128)(2,1)S(1)}, bf16[1536,1536]{1,0:T(8,128)(2,1)S(1)}) custom-call(s32[2,32]{1,0:T(2,128)S(4)} %get-tuple-element.26.lists, f32[1920,128]{1,0:T(8,128)S(1)} %get-tuple-element.27.spread, bf16[6144,256]{1,0:T(8,128)(2,1)S(1)} %get-tuple-element.28.pool, ...), custom_call_target="tpu_custom_call" | custom-call | flops 201326592 | bytes 20971520 | tf_op jit(solution)/shard_map/pallas_call | solution.py:267
  14.4 0.0 collective-permute-done.peer_q
  14.4 0.2 shard_map.67
  14.6 0.0 collective-permute-done.1.refs_0_
  14.6 4.5 %collective-permute-done.2.refs_1_ = bf16[256,256]{1,0:T(8,128)(2,1)S(1)} collective-permute-done((bf16[256,256]{1,0:T(8,128)(2,1)S(1)}, bf16[256,256]{1,0:T(8,128)(2,1)S(1)}, u32[]{:S(2)}, u32[]{:S(2)}) %collective-permute-start.2) | collective-permute-done | bytes 131104 | tf_op jit(solution)/shard_map/ppermute | solution.py:322
  19.1 0.0 collective-permute-done.3.refs_2_
  19.1 0.0 collective-permute-done.4.refs_3_
  19.1 0.5 %shard_map.68 = (f32[4,48,128]{2,1,0:T(8,128)S(1)}, bf16[3,48,128]{2,1,0:T(8,128)(2,1)S(1)}) custom-call(s32[2,8]{1,0:T(2,128)S(4)} %get-tuple-element.25.table, bf16[4,96,128]{2,1,0:T(8,128)(2,1)S(1)} %get-tuple-element.34.query, f32[4,96,128]{2,1,0:T(8,128)S(1)} %get-tuple-element.35.recent, bf16[128,256]{1,0:T(8,128)(2,1)S(1)} %get-tuple-element.29.fresh, ...), custom_call_target="tpu_custom_call" | custom-call | tf_op jit(solution)/shard_map/pallas_call | solution.py:267
  19.6 0.1 collective-permute-start.5
  19.7 1.2 %collective-permute-done.5.arrived = bf16[3,48,128]{2,1,0:T(8,128)(2,1)S(1)} collective-permute-done((bf16[3,48,128]{2,1,0:T(8,128)(2,1)S(1)}, bf16[3,48,128]{2,1,0:T(8,128)(2,1)S(1)}, u32[]{:S(2)}, u32[]{:S(2)}) %collective-permute-start.5) | collective-permute-done | bytes 36896 | tf_op jit(solution)/shard_map/ppermute | solution.py:363
  20.9 0.8 %shard_map.69 = (bf16[128,1536]{1,0:T(8,128)(2,1)S(1)}, bf16[128,1536]{1,0:T(8,128)(2,1)S(1)}, f32[1920,128]{1,0:T(8,128)S(1)}) custom-call(s32[2,8]{1,0:T(2,128)S(4)} %get-tuple-element.25.table, f32[1920,128]{1,0:T(8,128)S(1)} %get-tuple-element.30.attn, f32[4,48,128]{2,1,0:T(8,128)S(1)} %get-tuple-element.40.found, ...), custom_call_target="tpu_custom_call", output_to_operand_aliasing={{2}: (1, {})} | custom-call | tf_op jit(solution)/shard_map/pallas_call | solution.py:267
  21.8 0.2 collective-permute-start.6
  22.0 0.8 %shard_map.70.own = f32[128,1536]{1,0:T(8,128)S(1)} custom-call(bf16[128,1536]{1,0:T(8,128)(2,1)S(1)} %get-tuple-element.43.lhs, bf16[1536,1536]{1,0:T(8,128)(2,1)S(1)} %get-tuple-element.31.after.weight), custom_call_target="tpu_custom_call" | custom-call | flops 603979776 | bytes 6291456 | tf_op jit(solution)/shard_map/pallas_call | solution.py:267
  22.8 0.8 %collective-permute-done.6.others = bf16[128,1536]{1,0:T(8,128)(2,1)S(1)} collective-permute-done((bf16[128,1536]{1,0:T(8,128)(2,1)S(1)}, bf16[128,1536]{1,0:T(8,128)(2,1)S(1)}, u32[]{:S(2)}, u32[]{:S(2)}) %collective-permute-start.6) | collective-permute-done | bytes 393248 | tf_op jit(solution)/shard_map/ppermute | solution.py:375
  23.5 0.8 %shard_map.71 = bf16[128,1536]{1,0:T(8,128)(2,1)} custom-call(f32[128,1536]{1,0:T(8,128)S(1)} %shard_map.70.own, bf16[128,1536]{1,0:T(8,128)(2,1)S(1)} %collective-permute-done.6.others), custom_call_target="tpu_custom_call" | custom-call | tf_op jit(solution)/shard_map/pallas_call | solution.py:267
Async XLA Ops:
  1.9 12.7 %collective-permute-start.1 = (bf16[256,256]{1,0:T(8,128)(2,1)S(1)}, bf16[256,256]{1,0:T(8,128)(2,1)S(1)}, u32[]{:S(2)}, u32[]{:S(2)}) collective-permute-start(bf16[256,256]{1,0:T(8,128)(2,1)S(1)} %get-tuple-element.36), channel_id=1, source_target_pairs={{0,12},{1,15},{2,14},{3,13},{4,8},{5,11},{6,10},{7,9},{8,4},{9,7},... | collective-permute-start | bytes 393224 | tf_op jit(solution)/shard_map/ppermute | solution.py:322
  7.1 12.0 %collective-permute-start.2 = (bf16[256,256]{1,0:T(8,128)(2,1)S(1)}, bf16[256,256]{1,0:T(8,128)(2,1)S(1)}, u32[]{:S(2)}, u32[]{:S(2)}) collective-permute-start(bf16[256,256]{1,0:T(8,128)(2,1)S(1)} %get-tuple-element.37), channel_id=1, source_target_pairs={{0,8},{1,11},{2,10},{3,9},{4,12},{5,15},{6,14},{7,13},{8,0},{9,3},... | collective-permute-start | bytes 393224 | tf_op jit(solution)/shard_map/ppermute | solution.py:322
  7.1 12.0 %collective-permute-start.3 = (bf16[256,256]{1,0:T(8,128)(2,1)S(1)}, bf16[256,256]{1,0:T(8,128)(2,1)S(1)}, u32[]{:S(2)}, u32[]{:S(2)}) collective-permute-start(bf16[256,256]{1,0:T(8,128)(2,1)S(1)} %get-tuple-element.38), channel_id=1, source_target_pairs={{0,4},{1,7},{2,6},{3,5},{4,0},{5,3},{6,2},{7,1},{8,12},{9,15},{10,... | collective-permute-start | bytes 393224 | tf_op jit(solution)/shard_map/ppermute | solution.py:322
  7.7 11.4 %collective-permute-start.4 = (bf16[256,256]{1,0:T(8,128)(2,1)S(1)}, bf16[256,256]{1,0:T(8,128)(2,1)S(1)}, u32[]{:S(2)}, u32[]{:S(2)}) collective-permute-start(bf16[256,256]{1,0:T(8,128)(2,1)S(1)} %get-tuple-element.39), channel_id=1, source_target_pairs={{0,2},{1,3},{2,0},{3,1},{4,6},{5,7},{6,4},{7,5},{8,10},{9,11},{10,... | collective-permute-start | bytes 393224 | tf_op jit(solution)/shard_map/ppermute | solution.py:322
  10.5 3.9 %collective-permute-start = (bf16[3,48,128]{2,1,0:T(8,128)(2,1)S(1)}, bf16[3,48,128]{2,1,0:T(8,128)(2,1)S(1)}, u32[]{:S(2)}, u32[]{:S(2)}) collective-permute-start(bf16[3,48,128]{2,1,0:T(8,128)(2,1)S(1)} %get-tuple-element.33), channel_id=1, source_target_pairs={{0,1},{1,0},{2,3},{3,2},{4,5},{5,4},{6,7},{7,6},{8,9},{9,8},{10,11... | collective-permute-start | bytes 110600 | tf_op jit(solution)/shard_map/ppermute | solution.py:337
  19.6 1.3 %collective-permute-start.5 = (bf16[3,48,128]{2,1,0:T(8,128)(2,1)S(1)}, bf16[3,48,128]{2,1,0:T(8,128)(2,1)S(1)}, u32[]{:S(2)}, u32[]{:S(2)}) collective-permute-start(bf16[3,48,128]{2,1,0:T(8,128)(2,1)S(1)} %get-tuple-element.41), channel_id=1, source_target_pairs={{0,1},{1,0},{2,3},{3,2},{4,5},{5,4},{6,7},{7,6},{8,9},{9,8},{10,11... | collective-permute-start | bytes 110600 | tf_op jit(solution)/shard_map/ppermute | solution.py:363
  21.8 1.8 %collective-permute-start.6 = (bf16[128,1536]{1,0:T(8,128)(2,1)S(1)}, bf16[128,1536]{1,0:T(8,128)(2,1)S(1)}, u32[]{:S(2)}, u32[]{:S(2)}) collective-permute-start(bf16[128,1536]{1,0:T(8,128)(2,1)S(1)} %get-tuple-element.44), channel_id=1, source_target_pairs={{0,1},{1,0},{2,3},{3,2},{4,5},{5,4},{6,7},{7,6},{8,9},{9,8},{10,11... | collective-permute-start | bytes 1179656 | tf_op jit(solution)/shard_map/ppermute | solution.py:375

commit v12 on v11

--- a/solution.py
+++ b/solution.py
@@ -217,45 +217,87 @@
                 sent[i] = out[rows:].astype(jnp.bfloat16)
 
 
-def project_kernel(ops, stride, chunks, table, attn, found, arrived, weight, partial, lhs, merged):
+def spots(insts, ops, core, slots, shape):
+    row = lax.broadcasted_iota(jnp.int32, shape, 0)
+    col = lax.broadcasted_iota(jnp.int32, shape, 1)
+    same = row // slots == col // ops
+
+    def of(table):
+        hit = row < 0
+        for i in range(ops - 1):
+            j = table[0, partner(insts, ops, i, core)]
+            hit = hit | ((col % ops == i) & (row % slots == j))
+        return jnp.where(hit & same, 1.0, 0.0).astype(jnp.bfloat16)
+
+    return of
+
+
+def dot_tiles(lhs, weight, out):
+    tile = math.gcd(WIN, out.shape[1])
+    for n in range(0, out.shape[1], tile):
+        out[:, n : n + tile] = jnp.dot(
+            lhs[...], weight[:, n : n + tile], preferred_element_type=jnp.float32
+        ).astype(out.dtype)
+
+
+def project_kernel(
+    ops, stride, table, attn, found, weight, partial, lhs, spot_in, spot_out, merged
+):
     rows = found.shape[1]
     insts = table.shape[1]
     slots = stride - PAD
     steps = lhs.shape[0] // slots
     heads = rows // steps
     core = lax.axis_index("tp")
+    merged[...] = attn[...]
     for i in range(ops):
         j = table[0, partner(insts, ops, i, core)]
         merged[pl.ds(j, rows, stride=stride), :] = found[i]
     for i in range(ops - 1):
         j = table[0, partner(insts, ops, i, 1 - core)]
-        merged[pl.ds(j, rows, stride=stride), :] = arrived[i].astype(jnp.float32)
+        merged[pl.ds(j, rows, stride=stride), :] = jnp.zeros((rows, HDIM), jnp.float32)
     for s in range(steps):
         for h in range(heads):
             lhs[s * slots : (s + 1) * slots, h * HDIM : (h + 1) * HDIM] = merged[
                 pl.ds((s * heads + h) * stride, slots), :
             ].astype(jnp.bfloat16)
-    tile = partial.shape[1] // chunks
-    for n in range(chunks):
-        cols = slice(n * tile, (n + 1) * tile)
-        partial[:, cols] = jnp.dot(
-            lhs[...], weight[:, cols], preferred_element_type=jnp.float32
-        ).astype(jnp.bfloat16)
-
-
-def own_kernel(chunks, lhs, weight, out):
-    tile = out.shape[1] // chunks
-    for n in range(chunks):
-        cols = slice(n * tile, (n + 1) * tile)
-        out[:, cols] = jnp.dot(lhs[...], weight[:, cols], preferred_element_type=jnp.float32)
-
-
-def add_kernel(chunks, own, others, out_h, out, sems):
+    dot_tiles(lhs, weight, partial)
+    spot_in[...] = spots(insts, ops, 1 - core, slots, spot_in.shape)(table)
+    spot_out[...] = spots(insts, ops, core, slots, spot_out.shape)(table)
+
+
+def late_kernel(ops, steps, arrived, weight, partial, lhs, spread):
+    rows = arrived.shape[1]
+    heads = rows // steps
+    count = steps * ops
+    spread[...] = jnp.zeros_like(spread)
+    for i in range(ops - 1):
+        value = arrived[i].astype(jnp.float32)
+        for s in range(steps):
+            spread[pl.ds(s * ops + i, heads, stride=count), :] = value[s * heads : (s + 1) * heads]
+    for h in range(heads):
+        lhs[:, h * HDIM : (h + 1) * HDIM] = spread[h * count : (h + 1) * count, :].astype(
+            jnp.bfloat16
+        )
+    dot_tiles(lhs, weight, partial)
+
+
+def own_kernel(lhs, late, spot, weight, out, full):
+    tile = math.gcd(WIN, full.shape[1])
+    for n in range(0, full.shape[1], tile):
+        cols = slice(n, n + tile)
+        placed = jnp.dot(spot[...], late[:, cols], preferred_element_type=jnp.float32)
+        full[:, cols] = lhs[:, cols] + placed.astype(jnp.bfloat16)
+    dot_tiles(full, weight, out)
+
+
+def add_kernel(chunks, spot, own, others, late, out_h, out, sems):
     part = out.shape[0] // chunks
     copies = []
     for n in range(chunks):
         at = pl.ds(n * part, part)
-        out[at, :] = (own[at, :] + others[at, :].astype(jnp.float32)).astype(jnp.bfloat16)
+        placed = jnp.dot(spot[at, :], late[...], preferred_element_type=jnp.float32)
+        out[at, :] = (own[at, :] + others[at, :].astype(jnp.float32) + placed).astype(jnp.bfloat16)
         copies.append(pltpu.make_async_copy(out.at[at], out_h.at[at], sems.at[n]))
         copies[-1].start()
     for copy in copies:
@@ -361,31 +403,43 @@
         [(vmem, f32(ops, rows, HDIM)), (vmem, bf16(ops - 1, rows, HDIM))],
     )
     arrived = lax.ppermute(sent, "tp", swap)
-    chunks = half // WIN
-    partial, lhs, _ = call(
-        functools.partial(project_kernel, ops, stride, chunks),
-        [(smem, table), (vmem, attn), (vmem, found), (vmem, arrived), (vmem, peer_w)],
+    tokens, few = steps * slots, steps * ops
+    partial, lhs, spot_in, spot_out = call(
+        functools.partial(project_kernel, ops, stride),
+        [(smem, table), (vmem, attn), (vmem, found), (vmem, peer_w)],
         [
-            (vmem, bf16(steps * slots, half)),
-            (vmem, bf16(steps * slots, width)),
-            (vmem, f32(rows * stride, HDIM)),
+            (vmem, bf16(tokens, half)),
+            (vmem, bf16(tokens, width)),
+            (vmem, bf16(tokens, few)),
+            (vmem, bf16(tokens, few)),
         ],
-        aliases={1: 2},
+        [vmem((rows * stride, HDIM), jnp.float32)],
+        cost=pl.CostEstimate(
+            flops=2 * tokens * width * half, bytes_accessed=6 * MIB, transcendentals=0
+        ),
     )
     others = lax.ppermute(partial, "tp", swap)
+    partial, late = call(
+        functools.partial(late_kernel, ops, steps),
+        [(vmem, arrived), (vmem, peer_w)],
+        [(vmem, bf16(few, half)), (vmem, bf16(few, width))],
+        [vmem((rows * ops, HDIM), jnp.float32)],
+    )
+    late_others = lax.ppermute(partial, "tp", swap)
     (own,) = call(
-        functools.partial(own_kernel, chunks),
-        [(vmem, lhs), (vmem, own_w)],
-        [(vmem, f32(steps * slots, half))],
+        own_kernel,
+        [(vmem, lhs), (vmem, late), (vmem, spot_in), (vmem, own_w)],
+        [(vmem, f32(tokens, half))],
+        [vmem((tokens, width), jnp.bfloat16)],
         cost=pl.CostEstimate(
-            flops=2 * steps * slots * width * half, bytes_accessed=6 * MIB, transcendentals=0
+            flops=100 * tokens * width * half, bytes_accessed=6 * MIB, transcendentals=0
         ),
     )
     (result,) = call(
         functools.partial(add_kernel, 4),
-        [(vmem, own), (vmem, others)],
-        [(hbm, bf16(steps * slots, half))],
-        [vmem((steps * slots, half), jnp.bfloat16), dma((4,))],
+        [(vmem, spot_out), (vmem, own), (vmem, others), (vmem, late_others)],
+        [(hbm, bf16(tokens, half))],
+        [vmem((tokens, half), jnp.bfloat16), dma((4,))],
     )
     return result.reshape(steps, slots, half)
 

time: 24.5 us -> 24.4 us (level)
  waiting for transfers between devices: 6.47 us -> 4.85 us
  Pallas kernels: 9.99 us -> 11.1 us
  starting transfers between devices: 7.79 us -> 8.16 us
    ppermute x1, waiting for transfers between devices: 1.2 us -> 0.01 us  [body(): arrived = lax.ppermute(sent, 'tp', swap)]
    pallas_call x8 -> x9, Pallas kernels: 9.99 us -> 11.1 us  [call(): pl.pallas_call(kernel, out_shape=[space(shape.shape, shape.dtype) for spa...]
    ppermute x1, waiting for transfers between devices: 0.77 us -> 0.01 us  [body(): others = lax.ppermute(partial, 'tp', swap)]
    ppermute x0 -> x1, waiting for transfers between devices: none -> 0.35 us  [body(): late_others = lax.ppermute(partial, 'tp', swap)]
    ppermute x1, starting transfers between devices: 0.23 us -> 0.56 us  [body(): others = lax.ppermute(partial, 'tp', swap)]
  transfers between devices with their start and end apart: 7 -> 8, of which waited for: 3 -> 2; matrix products, arithmetic and copies ran while one was open for 0% -> 0% of each run, Pallas kernels for 24% -> 32%
where the time goes in v12:
time: 24.4 us; the launch traced here: 24.2 us
  Pallas kernels  11.1 us (45%)
  starting transfers between devices  8.16 us (33%)
  waiting for transfers between devices  4.85 us (20%)
    pallas_call x9, Pallas kernels, call(): pl.pallas_call(kernel, out_shape=[space(shape.shape, shape.dtype) for spa...  11.1 us
    ppermute x4, starting transfers between devices, body(): blocks[i] = lax.ppermute(sends[i], ('inst', 'tp'), pairs)  7.42 us
    ppermute x4, waiting for transfers between devices, body(): blocks[i] = lax.ppermute(sends[i], ('inst', 'tp'), pairs)  4.49 us
    ppermute x1, starting transfers between devices, body(): others = lax.ppermute(partial, 'tp', swap)  0.56 us
  transfers between devices with their start and end apart: 8, of which 2 were waited for; matrix products, arithmetic and copies ran while one was open for 0% of the time, Pallas kernels for 32%

profile of v12, /device:TPU:0, one launch (start us, length us, event | category | flops | bytes accessed | tf_op | source)
XLA Modules:
  0.0 24.2 jit_solution(7363431643013298126)
XLA Ops:
  0.0 1.9 %shard_map.64 = (s32[2,8]{1,0:T(2,128)S(4)}, s32[2,32]{1,0:T(2,128)S(4)}, bf16[6144,256]{1,0:T(8,128)(2,1)S(1)}, bf16[256,256]{1,0:T(8,128)(2,1)S(1)}, bf16[256,...) custom-call(s32[8,32]{1,0:T(8,128)} %anchor_h.1, s32[8,32]{1,0:T(8,128)} %lengths_h.1, ...), custom_call_target="tpu_custom_call" | custom-call | tf_op jit(solution)/shard_map/pallas_call | solution.py:309
  1.9 5.1 %collective-permute-start.1 = (bf16[256,256]{1,0:T(8,128)(2,1)S(1)}, bf16[256,256]{1,0:T(8,128)(2,1)S(1)}, u32[]{:S(2)}, u32[]{:S(2)}) collective-permute-start(bf16[256,256]{1,0:T(8,128)(2,1)S(1)} %get-tuple-element.40), channel_id=1, source_target_pairs={{0,12},{1,15},{2,14},{3,13},{4,8},{5,11},{6,10},{7,9},{8,4},{9,7},... | collective-permute-start | bytes 393224 | tf_op jit(solution)/shard_map/ppermute | solution.py:364
  7.1 0.0 collective-permute-start.2
  7.1 0.6 %collective-permute-start.3 = (bf16[256,256]{1,0:T(8,128)(2,1)S(1)}, bf16[256,256]{1,0:T(8,128)(2,1)S(1)}, u32[]{:S(2)}, u32[]{:S(2)}) collective-permute-start(bf16[256,256]{1,0:T(8,128)(2,1)S(1)} %get-tuple-element.42), channel_id=1, source_target_pairs={{0,4},{1,7},{2,6},{3,5},{4,0},{5,3},{6,2},{7,1},{8,12},{9,15},{10,... | collective-permute-start | bytes 393224 | tf_op jit(solution)/shard_map/ppermute | solution.py:364
  7.7 1.7 %collective-permute-start.4 = (bf16[256,256]{1,0:T(8,128)(2,1)S(1)}, bf16[256,256]{1,0:T(8,128)(2,1)S(1)}, u32[]{:S(2)}, u32[]{:S(2)}) collective-permute-start(bf16[256,256]{1,0:T(8,128)(2,1)S(1)} %get-tuple-element.43), channel_id=1, source_target_pairs={{0,2},{1,3},{2,0},{3,1},{4,6},{5,7},{6,4},{7,5},{8,10},{9,11},{10,... | collective-permute-start | bytes 393224 | tf_op jit(solution)/shard_map/ppermute | solution.py:364
  9.4 1.1 %shard_map.65 = (f32[1920,128]{1,0:T(8,128)S(1)}, bf16[128,256]{1,0:T(8,128)(2,1)S(1)}, bf16[4,48,128]{2,1,0:T(8,128)(2,1)S(1)}, bf16[3,48,128]{2,1,0:T(8,128)(2,1)S(1)}) custom-call(s32[2,8]{1,0:T(2,128)S(4)} %get-tuple-element.29.table, bf16[4,32,1536]{2,1,0:T(8,128)(2,1)} %queries_h.1, bf16[128,256]{1,0:T(8,128)(2,1)} %bitcast.2), custom_call_target="tpu_custom_call" | custom-call | bytes 1048576 | tf_op jit(solution)/shard_map/pallas_call | solution.py:309
  10.5 0.1 collective-permute-start
  10.6 3.8 %shard_map.66 = (f32[1920,128]{1,0:T(8,128)S(1)}, bf16[1536,1536]{1,0:T(8,128)(2,1)S(1)}, bf16[1536,1536]{1,0:T(8,128)(2,1)S(1)}) custom-call(s32[2,32]{1,0:T(2,128)S(4)} %get-tuple-element.30.lists, f32[1920,128]{1,0:T(8,128)S(1)} %get-tuple-element.31.spread, bf16[6144,256]{1,0:T(8,128)(2,1)S(1)} %get-tuple-element.32.pool, ...), custom_call_target="tpu_custom_call" | custom-call | flops 201326592 | bytes 20971520 | tf_op jit(solution)/shard_map/pallas_call | solution.py:309
  14.4 0.0 collective-permute-done.peer_q
  14.4 0.2 shard_map.67
  14.6 0.0 collective-permute-done.1.refs_0_
  14.6 4.5 %collective-permute-done.2.refs_1_ = bf16[256,256]{1,0:T(8,128)(2,1)S(1)} collective-permute-done((bf16[256,256]{1,0:T(8,128)(2,1)S(1)}, bf16[256,256]{1,0:T(8,128)(2,1)S(1)}, u32[]{:S(2)}, u32[]{:S(2)}) %collective-permute-start.2) | collective-permute-done | bytes 131104 | tf_op jit(solution)/shard_map/ppermute | solution.py:364
  19.1 0.0 collective-permute-done.3.refs_2_
  19.1 0.0 collective-permute-done.4.refs_3_
  19.1 0.5 %shard_map.68 = (f32[4,48,128]{2,1,0:T(8,128)S(1)}, bf16[3,48,128]{2,1,0:T(8,128)(2,1)S(1)}) custom-call(s32[2,8]{1,0:T(2,128)S(4)} %get-tuple-element.29.table, bf16[4,96,128]{2,1,0:T(8,128)(2,1)S(1)} %get-tuple-element.38.query, f32[4,96,128]{2,1,0:T(8,128)S(1)} %get-tuple-element.39.recent, bf16[128,256]{1,0:T(8,128)(2,1)S(1)} %get-tuple-element.33.fresh, ...), custom_call_target="tpu_custom_call" | custom-call | tf_op jit(solution)/shard_map/pallas_call | solution.py:309
  19.6 0.1 collective-permute-start.5
  19.7 1.0 %shard_map.69 = (bf16[128,1536]{1,0:T(8,128)(2,1)S(1)}, bf16[128,1536]{1,0:T(8,128)(2,1)S(1)}, bf16[128,16]{1,0:T(8,128)(2,1)S(1)}, bf16[128,16]{1,0:T(8,128)(2,1)S(1)}) custom-call(s32[2,8]{1,0:T(2,128)S(4)} %get-tuple-element.29.table, f32[1920,128]{1,0:T(8,128)S(1)} %get-tuple-element.34.attn, f32[4,48,128]{2,1,0:T(8,128)S(1)} %get-tuple-element.44.found, ...), custom_call_target="tpu_custom_call" | custom-call | flops 603979776 | bytes 6291456 | tf_op jit(solution)/shard_map/pallas_call | solution.py:309
  20.7 0.6 %collective-permute-start.6 = (bf16[128,1536]{1,0:T(8,128)(2,1)S(1)}, bf16[128,1536]{1,0:T(8,128)(2,1)S(1)}, u32[]{:S(2)}, u32[]{:S(2)}) collective-permute-start(bf16[128,1536]{1,0:T(8,128)(2,1)S(1)} %get-tuple-element.51), channel_id=1, source_target_pairs={{0,1},{1,0},{2,3},{3,2},{4,5},{5,4},{6,7},{7,6},{8,9},{9,8},{10,11... | collective-permute-start | bytes 1179656 | tf_op jit(solution)/shard_map/ppermute | solution.py:421
  21.3 0.0 collective-permute-done.5.arrived
  21.3 0.7 %shard_map.70 = (bf16[16,1536]{1,0:T(8,128)(2,1)S(1)}, bf16[16,1536]{1,0:T(8,128)(2,1)S(1)}) custom-call(bf16[3,48,128]{2,1,0:T(8,128)(2,1)S(1)} %collective-permute-done.5.arrived, bf16[1536,1536]{1,0:T(8,128)(2,1)S(1)} %get-tuple-element.45.weight), custom_call_target="tpu_custom_call" | custom-call | tf_op jit(solution)/shard_map/pallas_call | solution.py:309
  22.0 0.0 collective-permute-start.7
  22.0 0.9 %shard_map.71.own = f32[128,1536]{1,0:T(8,128)S(1)} custom-call(bf16[128,1536]{1,0:T(8,128)(2,1)S(1)} %get-tuple-element.47.lhs, bf16[16,1536]{1,0:T(8,128)(2,1)S(1)} %get-tuple-element.49.late, bf16[128,16]{1,0:T(8,128)(2,1)S(1)} %get-tuple-element.50.spot, bf16[1536,1536]{1,0:T(8,128)(2,1)S(1)} %get-tuple-element.35.after.weight), custom_call_target="tpu_custom_call" | custom-call | flops 30198988800 | bytes 6291456 | tf_op jit(solution)/shard_map/pallas_call | solution.py:309
  22.9 0.4 %collective-permute-done.7.late = bf16[16,1536]{1,0:T(8,128)(2,1)S(1)} collective-permute-done((bf16[16,1536]{1,0:T(8,128)(2,1)S(1)}, bf16[16,1536]{1,0:T(8,128)(2,1)S(1)}, u32[]{:S(2)}, u32[]{:S(2)}) %collective-permute-start.7) | collective-permute-done | bytes 49184 | tf_op jit(solution)/shard_map/ppermute | solution.py:428
  23.2 0.0 collective-permute-done.6.others
  23.2 0.9 %shard_map.72 = bf16[128,1536]{1,0:T(8,128)(2,1)} custom-call(bf16[128,16]{1,0:T(8,128)(2,1)S(1)} %get-tuple-element.46.spot, f32[128,1536]{1,0:T(8,128)S(1)} %shard_map.71.own, bf16[128,1536]{1,0:T(8,128)(2,1)S(1)} %collective-permute-done.6.others, bf16[16,1536]{1,0:T(8,128)(2,1)S(1)} %collective-permute-done.7.late), custom_call_target="tpu_custom_call" | custom-call | tf_op jit(solution)/shard_map/pallas_call | solution.py:309
Async XLA Ops:
  1.9 12.7 %collective-permute-start.1 = (bf16[256,256]{1,0:T(8,128)(2,1)S(1)}, bf16[256,256]{1,0:T(8,128)(2,1)S(1)}, u32[]{:S(2)}, u32[]{:S(2)}) collective-permute-start(bf16[256,256]{1,0:T(8,128)(2,1)S(1)} %get-tuple-element.40), channel_id=1, source_target_pairs={{0,12},{1,15},{2,14},{3,13},{4,8},{5,11},{6,10},{7,9},{8,4},{9,7},... | collective-permute-start | bytes 393224 | tf_op jit(solution)/shard_map/ppermute | solution.py:364
  7.1 12.0 %collective-permute-start.2 = (bf16[256,256]{1,0:T(8,128)(2,1)S(1)}, bf16[256,256]{1,0:T(8,128)(2,1)S(1)}, u32[]{:S(2)}, u32[]{:S(2)}) collective-permute-start(bf16[256,256]{1,0:T(8,128)(2,1)S(1)} %get-tuple-element.41), channel_id=1, source_target_pairs={{0,8},{1,11},{2,10},{3,9},{4,12},{5,15},{6,14},{7,13},{8,0},{9,3},... | collective-permute-start | bytes 393224 | tf_op jit(solution)/shard_map/ppermute | solution.py:364
  7.1 12.0 %collective-permute-start.3 = (bf16[256,256]{1,0:T(8,128)(2,1)S(1)}, bf16[256,256]{1,0:T(8,128)(2,1)S(1)}, u32[]{:S(2)}, u32[]{:S(2)}) collective-permute-start(bf16[256,256]{1,0:T(8,128)(2,1)S(1)} %get-tuple-element.42), channel_id=1, source_target_pairs={{0,4},{1,7},{2,6},{3,5},{4,0},{5,3},{6,2},{7,1},{8,12},{9,15},{10,... | collective-permute-start | bytes 393224 | tf_op jit(solution)/shard_map/ppermute | solution.py:364
  7.7 11.4 %collective-permute-start.4 = (bf16[256,256]{1,0:T(8,128)(2,1)S(1)}, bf16[256,256]{1,0:T(8,128)(2,1)S(1)}, u32[]{:S(2)}, u32[]{:S(2)}) collective-permute-start(bf16[256,256]{1,0:T(8,128)(2,1)S(1)} %get-tuple-element.43), channel_id=1, source_target_pairs={{0,2},{1,3},{2,0},{3,1},{4,6},{5,7},{6,4},{7,5},{8,10},{9,11},{10,... | collective-permute-start | bytes 393224 | tf_op jit(solution)/shard_map/ppermute | solution.py:364
  10.5 3.9 %collective-permute-start = (bf16[3,48,128]{2,1,0:T(8,128)(2,1)S(1)}, bf16[3,48,128]{2,1,0:T(8,128)(2,1)S(1)}, u32[]{:S(2)}, u32[]{:S(2)}) collective-permute-start(bf16[3,48,128]{2,1,0:T(8,128)(2,1)S(1)} %get-tuple-element.37), channel_id=1, source_target_pairs={{0,1},{1,0},{2,3},{3,2},{4,5},{5,4},{6,7},{7,6},{8,9},{9,8},{10,11... | collective-permute-start | bytes 110600 | tf_op jit(solution)/shard_map/ppermute | solution.py:379
  19.6 1.7 %collective-permute-start.5 = (bf16[3,48,128]{2,1,0:T(8,128)(2,1)S(1)}, bf16[3,48,128]{2,1,0:T(8,128)(2,1)S(1)}, u32[]{:S(2)}, u32[]{:S(2)}) collective-permute-start(bf16[3,48,128]{2,1,0:T(8,128)(2,1)S(1)} %get-tuple-element.48), channel_id=1, source_target_pairs={{0,1},{1,0},{2,3},{3,2},{4,5},{5,4},{6,7},{7,6},{8,9},{9,8},{10,11... | collective-permute-start | bytes 110600 | tf_op jit(solution)/shard_map/ppermute | solution.py:405
  20.7 2.5 %collective-permute-start.6 = (bf16[128,1536]{1,0:T(8,128)(2,1)S(1)}, bf16[128,1536]{1,0:T(8,128)(2,1)S(1)}, u32[]{:S(2)}, u32[]{:S(2)}) collective-permute-start(bf16[128,1536]{1,0:T(8,128)(2,1)S(1)} %get-tuple-element.51), channel_id=1, source_target_pairs={{0,1},{1,0},{2,3},{3,2},{4,5},{5,4},{6,7},{7,6},{8,9},{9,8},{10,11... | collective-permute-start | bytes 1179656 | tf_op jit(solution)/shard_map/ppermute | solution.py:421
  22.0 1.2 %collective-permute-start.7 = (bf16[16,1536]{1,0:T(8,128)(2,1)S(1)}, bf16[16,1536]{1,0:T(8,128)(2,1)S(1)}, u32[]{:S(2)}, u32[]{:S(2)}) collective-permute-start(bf16[16,1536]{1,0:T(8,128)(2,1)S(1)} %get-tuple-element.52), channel_id=1, source_target_pairs={{0,1},{1,0},{2,3},{3,2},{4,5},{5,4},{6,7},{7,6},{8,9},{9,8},{10,11... | collective-permute-start | bytes 147464 | tf_op jit(solution)/shard_map/ppermute | solution.py:428
